TPU v7x, 256 devices: a whole 4x4x8 slice. The times are simulated.
256 devices in a mesh: seq: 8 (over x, core), exp: 16 (over y, z_lo), dp: 2 (over z_hi).
Axes of the slice: x: 4, y: 4, z: 8 (z_hi: 2, z_lo: 4; z = z_hi * 4 + z_lo), core: 2. Of those that a mesh axis runs over, the one named last changes fastest.
Arguments:
- tokens: bfloat16 [524288, 1280], P(('dp', 'seq', 'exp')), parts along dimension 0, may hold values from -60 to 60
- slot_keys: bfloat16 [1280, 256], replicated, may hold values from -1 to 1
- w_in: bfloat16 [16, 1280, 5120], P('exp', None, 'seq'), may hold values from -0.15625 to 0.15625
- w_out: bfloat16 [16, 5120, 1280], P('exp', 'seq'), may hold values from -0.078125 to 0.078125
Outputs:
- mixed: bfloat16 [524288, 1280], P(('dp', 'seq', 'exp')), parts along dimension 0
There are 2 independent parts, one for each index of `dp`. A program takes and returns all parts, laid end to end along the dimension named above; an argument that names none is the same for every part. Nothing has to cross between parts.
All inputs are finite; a program needn't handle non-finite values.
Results may differ from a plain program's by a relative error of at most 0.007.
Values may be sent and summed in bfloat16 or wider, within the bound.
No kernel may reach another device: no remote copies, remote signals or barrier semaphores. Data moves between devices by JAX's collectives and lax.ppermute only.
A program may use at most 64 MiB of HBM per device.

v0:
```python
import jax
import jax.numpy as jnp
from jax import lax
from jax.sharding import PartitionSpec as P


def body(tokens, slot_keys, w_in, w_out):
    logits = jnp.dot(tokens, slot_keys, preferred_element_type=jnp.float32)
    slot_peak = lax.pmax(jnp.max(logits, axis=0), ("seq", "exp"))
    spread = jnp.exp(logits - slot_peak[None, :])
    local_total = jnp.sum(spread, axis=0)
    dispatch = spread.astype(jnp.bfloat16)
    weighted = lax.dot_general(
        dispatch, tokens, (((0,), (0,)), ((), ())), preferred_element_type=jnp.float32
    )
    per_device = slot_keys.shape[1] // lax.axis_size("exp")
    all_sums, all_totals = lax.psum((weighted, local_total), ("seq", "exp"))
    offset = lax.axis_index("exp") * per_device
    own_sums = lax.dynamic_slice_in_dim(all_sums, offset, per_device, 0)
    own_totals = lax.dynamic_slice_in_dim(all_totals, offset, per_device, 0)
    slot_in = (own_sums / own_totals[:, None]).astype(jnp.bfloat16)
    experts_here = w_in.shape[0]
    slot_blocks = slot_in.reshape(experts_here, per_device // experts_here, slot_in.shape[1])
    hidden = jax.nn.gelu(
        jnp.einsum("epd,edf->epf", slot_blocks, w_in, preferred_element_type=jnp.float32)
    ).astype(jnp.bfloat16)
    partial_out = jnp.einsum("epf,efd->epd", hidden, w_out, preferred_element_type=jnp.float32)
    slot_out = lax.psum(partial_out, "seq").astype(jnp.bfloat16)
    slot_out = slot_out.reshape(per_device, slot_out.shape[2])
    row_peak = jnp.max(logits, axis=1)
    row_exp = jnp.exp(logits - row_peak[:, None])
    combine = (row_exp / jnp.sum(row_exp, axis=1)[:, None]).astype(jnp.bfloat16)
    mixed = jnp.dot(
        combine,
        lax.all_gather(slot_out, "exp", axis=0, tiled=True),
        preferred_element_type=jnp.float32,
    )
    return mixed.astype(jnp.bfloat16)


def solution(mesh):
    return jax.shard_map(
        body,
        mesh=mesh,
        in_specs=(P(("dp", "seq", "exp"), None), P(), P("exp", None, "seq"), P("exp", "seq", None)),
        out_specs=P(("dp", "seq", "exp"), None),
        check_vma=False,
    )
```

profile of v0, /device:TPU:1, one launch (start us, length us, event | category | flops | bytes accessed | tf_op | source)
XLA Modules:
  0.0 1675.9 jit_solution(14645239921303046686)
XLA Ops:
  6.5 0.0 copy-start
  6.5 0.0 all-reduce.2.cloned.1.call-start
  6.5 5.6 fusion.38
  12.2 308.5 %pmax.7 = f32[256]{0:T(256)S(1)} all-reduce(f32[256]{0:T(256)S(1)} %get-tuple-element.7), channel_id=1, replica_groups=mesh['seq'=8,'exp'=16,'dp'=2] {'seq','exp'}, use_global_device_ids=true, to_apply=%region_3.0 | all-reduce | flops 256 | bytes 2048 | tf_op jit(solution)/shard_map/pmax | solution.py:9
  320.7 5.8 fusion.6
  326.4 0.0 copy-start.1
  326.4 0.0 all-reduce.2.cloned.1.call-update
  326.5 2.6 fusion.1
  329.1 335.2 %psum.22 = f32[256]{0:T(256)S(1)} all-reduce(f32[256]{0:T(256)S(1)} %get-tuple-element.5), channel_id=1, replica_groups=mesh['seq'=8,'exp'=16,'dp'=2] {'seq','exp'}, use_global_device_ids=true, to_apply=%region_6.0 | all-reduce | flops 256 | bytes 2048 | tf_op jit(solution)/shard_map/psum | solution.py:17
  664.2 0.1 dynamic_slice.7
  664.3 921.5 %all-reduce.2.cloned.1.call-done = f32[256,1280]{1,0:T(8,128)} async-done(((f32[256,1280]{1,0:T(8,128)}), f32[256,1280]{1,0:T(8,128)}) %all-reduce.2.cloned.1.call-update) | async-done | bytes 1310736 | tf_op jit(solution)/shard_map/psum | solution.py:17
  1585.8 0.0 copy-done
  1585.8 0.0 copy-done.1
  1585.8 1.6 convolution_bitcast_fusion
  1587.4 36.2 %psum.23 = bf16[1,16,1280]{2,1,0:T(8,128)(2,1)S(1)} all-reduce(f32[1,16,1280]{2,1,0:T(8,128)S(1)} %convolution_bitcast_fusion), channel_id=1, replica_groups=mesh['seq'=8,'exp'=16,'dp'=2] {'seq'}, use_global_device_ids=true, to_apply=%region_7.0 | all-reduce | flops 20480 | bytes 122880 | tf_op jit(solution)/shard_map/psum | solution.py:28
  1623.6 39.7 %all-gather = bf16[1,256,1280]{2,1,0:T(8,128)(2,1)S(1)} all-gather(bf16[1,16,1280]{2,1,0:T(8,128)(2,1)S(1)} %psum.23), channel_id=2, replica_groups=mesh['seq'=8,'exp'=16,'dp'=2] {'exp'}, dimensions={1}, use_global_device_ids=true | all-gather | bytes 696320 | tf_op jit(solution)/shard_map/all_gather | solution.py:35
  1663.3 5.8 convolution_convert_fusion
Async XLA Ops:
  6.5 1579.3 %copy-start = (bf16[1,640,1280]{2,1,0:T(8,128)(2,1)S(1)}, bf16[1,640,1280]{2,1,0:T(8,128)(2,1)}, u32[]{:S(2)}) copy-start(bf16[1,640,1280]{2,1,0:T(8,128)(2,1)} %param.7) | copy-start | bytes 4915204
  6.5 1579.3 %all-reduce.2.cloned.1.call-start = ((), (), s32[]{:S(2)}) async-start(), calls=%async_computation | async-start | bytes 2621440 | tf_op jit(solution)/shard_map/psum | solution.py:17
  326.4 1259.4 %copy-start.1 = (bf16[1,1280,640]{2,1,0:T(8,128)(2,1)S(1)}, bf16[1,1280,640]{2,1,0:T(8,128)(2,1)}, u32[]{:S(2)}) copy-start(bf16[1,1280,640]{2,1,0:T(8,128)(2,1)} %param.6) | copy-start | bytes 4915204
Sparse Core Ops, SparseCore 0:
  326.6 1259.2 all-reduce.1
where the time goes:
time: 1680 us
  waiting for transfers between devices  922 us (55%)
  blocking collectives  719 us (43%)
  matrix products  18.8 us (1%)
    psum x1, waiting for transfers between devices, body(): all_sums, all_totals = lax.psum((weighted, local_total), ('seq', 'exp'))  922 us
    psum x1, blocking collectives, body(): all_sums, all_totals = lax.psum((weighted, local_total), ('seq', 'exp'))  335 us
    pmax x1, blocking collectives, body(): slot_peak = lax.pmax(jnp.max(logits, axis=0), ('seq', 'exp'))  308 us
    all_gather x1, blocking collectives, body(): lax.all_gather(slot_out, 'exp', axis=0, tiled=True)  39.7 us
    psum x1, blocking collectives, body(): slot_out = lax.psum(partial_out, 'seq').astype(jnp.bfloat16)  36.2 us
  transfers between devices with their start and end apart: 1, of which 1 were waited for; matrix products, arithmetic and copies ran while one was open for 0% of the time, Pallas kernels for 0%

commit v1 on v0

v1 whole, which is shorter than its diff:
```python
import jax
import jax.numpy as jnp
from jax import lax
from jax.sharding import PartitionSpec as P

F32 = jnp.float32
BF16 = jnp.bfloat16


def _core_perm():
    return [(s, s ^ 1) for s in range(8)]


def _x_perm(k):
    return [(s, ((s // 2 + k) % 4) * 2 + s % 2) for s in range(8)]


def _y_perm(k):
    return [(e, ((e // 4 + k) % 4) * 4 + e % 4) for e in range(16)]


def _z_perm(k):
    return [(e, (e // 4) * 4 + (e % 4 + k) % 4) for e in range(16)]


def _pieces(v, n):
    out = []
    for _ in range(n):
        p = lax.reduce_precision(v, 8, 7)
        out.append(p[:, None])
        v = v - p
    return out


def _pack16(sums, peak, total):
    rows = sums.shape[0]
    stats = _pieces(peak, 3) + _pieces(total, 3) + [jnp.zeros((rows, 122), F32)]
    return jnp.concatenate([sums] + stats, axis=1).astype(BF16)


def _unpack16(packed):
    n = packed.shape[1] - 128
    v = packed.astype(F32)
    return (
        v[:, :n],
        v[:, n] + v[:, n + 1] + v[:, n + 2],
        v[:, n + 3] + v[:, n + 4] + v[:, n + 5],
    )


def _pack32(sums, peak, total):
    rows = sums.shape[0]
    return jnp.concatenate(
        [sums, peak[:, None], total[:, None], jnp.zeros((rows, 126), F32)], axis=1
    )


def _unpack32(v):
    n = v.shape[1] - 128
    return v[:, :n], v[:, n], v[:, n + 1]


def _merge(parts):
    peak = parts[0][1]
    for _, p, _ in parts[1:]:
        peak = jnp.maximum(peak, p)
    sums, total = 0.0, 0.0
    for s, p, t in parts:
        a = jnp.exp(p - peak)
        sums = sums + s * a[:, None]
        total = total + t * a
    return sums, peak, total


def body(tokens, slot_keys, w_in, w_out):
    seq, exp = lax.axis_index("seq"), lax.axis_index("exp")
    core, y, z = seq % 2, exp // 4, exp % 4
    slots, width = slot_keys.shape[1], tokens.shape[1]
    half = width // 2

    logits = jnp.dot(tokens, slot_keys, preferred_element_type=F32)
    peak = jnp.max(logits, axis=0)
    spread = jnp.exp(logits - peak[None, :])
    total = jnp.sum(spread, axis=0)
    sums = lax.dot_general(
        spread.astype(BF16), tokens, (((0,), (0,)), ((), ())), preferred_element_type=F32
    )

    mine = lax.dynamic_slice_in_dim(sums, core * half, half, 1)
    other = lax.dynamic_slice_in_dim(sums, (1 - core) * half, half, 1)
    got = lax.ppermute(_pack16(other, peak, total), "seq", _core_perm())
    state = _merge([(mine, peak, total), _unpack16(got)])

    packed = _pack16(*state)
    rows = slots // 4
    got = [
        lax.ppermute(
            lax.dynamic_slice_in_dim(packed, ((y + k) % 4) * rows, rows, 0), "exp", _y_perm(k)
        )
        for k in range(1, 4)
    ]
    own = [lax.dynamic_slice_in_dim(v, y * rows, rows, 0) for v in state]
    state = _merge([tuple(own)] + [_unpack16(g) for g in got])

    packed = _pack32(*state)
    rows = rows // 4
    got = [
        lax.ppermute(
            lax.dynamic_slice_in_dim(packed, ((z + k) % 4) * rows, rows, 0), "exp", _z_perm(k)
        )
        for k in range(1, 4)
    ]
    own = lax.dynamic_slice_in_dim(packed, z * rows, rows, 0)
    state = _merge([_unpack32(g) for g in [own] + got])

    packed = _pack32(*state)
    got = [lax.ppermute(packed, "seq", _x_perm(k)) for k in range(1, 4)]
    sums, _, total = _merge([state] + [_unpack32(g) for g in got])
    slot_half = (sums / total[:, None]).astype(BF16)
    got = lax.ppermute(slot_half, "seq", _core_perm())
    slot_in = jnp.where(
        core == 0,
        jnp.concatenate([slot_half, got], axis=1),
        jnp.concatenate([got, slot_half], axis=1),
    )

    hidden = jax.nn.gelu(jnp.dot(slot_in, w_in[0], preferred_element_type=F32)).astype(BF16)
    partial = jnp.dot(hidden, w_out[0], preferred_element_type=F32)

    mine = lax.dynamic_slice_in_dim(partial, core * half, half, 1)
    other = lax.dynamic_slice_in_dim(partial, (1 - core) * half, half, 1)
    part = mine + lax.ppermute(other, "seq", _core_perm())
    whole = part + sum(lax.ppermute(part, "seq", _x_perm(k)) for k in range(1, 4))
    out = whole.astype(BF16)

    def spread_out(block, index, perm):
        rows = block.shape[0]
        res = jnp.zeros((4 * rows, block.shape[1]), block.dtype)
        got = [block] + [lax.ppermute(block, "exp", perm(k)) for k in range(1, 4)]
        for k, g in enumerate(got):
            res = lax.dynamic_update_slice_in_dim(res, g, ((index - k) % 4) * rows, 0)
        return res

    out = spread_out(out, z, _z_perm)
    out = spread_out(out, y, _y_perm)
    got = lax.ppermute(out, "seq", _core_perm())
    slot_out = jnp.where(
        core == 0,
        jnp.concatenate([out, got], axis=1),
        jnp.concatenate([got, out], axis=1),
    )

    row_peak = jnp.max(logits, axis=1)
    row_exp = jnp.exp(logits - row_peak[:, None])
    combine = (row_exp / jnp.sum(row_exp, axis=1)[:, None]).astype(BF16)
    return jnp.dot(combine, slot_out, preferred_element_type=F32).astype(BF16)


def solution(mesh):
    return jax.shard_map(
        body,
        mesh=mesh,
        in_specs=(P(("dp", "seq", "exp"), None), P(), P("exp", None, "seq"), P("exp", "seq", None)),
        out_specs=P(("dp", "seq", "exp"), None),
        check_vma=False,
    )
```

time: 1680 us -> 131 us (0.08)
  waiting for transfers between devices: 922 us -> 77.3 us
  blocking collectives: 719 us -> 0 us
  starting transfers between devices: 0.01 us -> 27.4 us
    psum x1 -> x0, waiting for transfers between devices: 922 us -> none  [body(): all_sums, all_totals = lax.psum((weighted, local_total), ('seq', 'exp'))]
    psum x2 -> x0, blocking collectives: 371 us -> none  [the longest x1 335 us: body(): all_sums, all_totals = lax.psum((weighted, local_total), ('seq', 'exp'))]
    pmax x1 -> x0, blocking collectives: 308 us -> none  [body(): slot_peak = lax.pmax(jnp.max(logits, axis=0), ('seq', 'exp'))]
    ppermute x0 -> x22, waiting for transfers between devices: none -> 77.3 us  [the longest x3 34.7 us: body(): lax.ppermute(lax.dynamic_slice_in_dim(packed, (z + k) % 4 * rows, rows, 0...]
    all_gather x1 -> x0, blocking collectives: 39.7 us -> none  [body(): lax.all_gather(slot_out, 'exp', axis=0, tiled=True)]
    ppermute x0 -> x22, starting transfers between devices: none -> 27.4 us  [the longest x6 5.5 us: spread_out(): got = [block] + [lax.ppermute(block, 'exp', perm(k)) for k in range(1, 4)]]
  transfers between devices with their start and end apart: 1 -> 22, of which waited for: 1 -> 18; matrix products, arithmetic and copies ran while one was open for 0% -> 0% of each run, Pallas kernels for 0% -> 0%
where the time goes in v1:
time: 131 us; the launch traced here: 130 us
  waiting for transfers between devices  77.3 us (59%)
  starting transfers between devices  27.4 us (21%)
  matrix products  13.2 us (10%)
  other arithmetic  6.08 us (5%)
  local copies, waits for them, and re-layouts  6.03 us (5%)
    ppermute x3, waiting for transfers between devices, body(): lax.ppermute(lax.dynamic_slice_in_dim(packed, (z + k) % 4 * rows, rows, 0...  34.7 us
    ppermute x3, waiting for transfers between devices, body(): got = [lax.ppermute(packed, 'seq', _x_perm(k)) for k in range(1, 4)]  19.8 us
    ppermute x3, waiting for transfers between devices, body(): lax.ppermute(lax.dynamic_slice_in_dim(packed, (y + k) % 4 * rows, rows, 0...  8.45 us
    ppermute x6, waiting for transfers between devices, spread_out(): got = [block] + [lax.ppermute(block, 'exp', perm(k)) for k in range(1, 4)]  5.87 us
    dot_general x1, matrix products, body(): return jnp.dot(combine, slot_out, preferred_element_type=F32).astype(BF16)  5.81 us
    ppermute x6, starting transfers between devices, spread_out(): got = [block] + [lax.ppermute(block, 'exp', perm(k)) for k in range(1, 4)]  5.5 us
    ppermute x1, starting transfers between devices, body(): got = lax.ppermute(out, 'seq', _core_perm())  5.01 us
    ppermute x3, starting transfers between devices, body(): lax.ppermute(lax.dynamic_slice_in_dim(packed, (z + k) % 4 * rows, rows, 0...  4.54 us
  transfers between devices with their start and end apart: 22, of which 18 were waited for; matrix products, arithmetic and copies ran while one was open for 0% of the time, Pallas kernels for 0%

profile of v1, /device:TPU:1, one launch (start us, length us, event | category | flops | bytes accessed | tf_op | source)
XLA Modules:
  0.0 130.4 jit_solution(655771633245093555)
XLA Ops:
  0.0 4.4 %fusion.103 = (f32[256]{0:T(256)S(1)}, f32[2048]{0:T(1024)S(1)}, f32[2048,256]{1,0:T(8,128)S(1)}) fusion(bf16[2048,1280]{1,0:T(8,128)(2,1)} %param.4, bf16[1280,256]{1,0:T(8,128)(2,1)} %param.5), kind=kOutput, calls=%fused_computation.185 | convolution fusion | flops 1343223552 | bytes 8004608 | tf_op jit(solution)/shard_map/dot_general | solution.py:81
  4.5 2.3 %fusion.7 = f32[256,1280]{0,1:T(8,128)S(1)} fusion(bf16[2048,1280]{1,0:T(8,128)(2,1)S(1)} %copy-done.4, f32[2048,256]{1,0:T(8,128)S(1)} %get-tuple-element.57, f32[256]{0:T(256)S(1)} %get-tuple-element.7), kind=kOutput, calls=%fused_computation.11 | convolution fusion | flops 1343225856 | bytes 8651776 | tf_op jit(solution)/shard_map/dot_general | solution.py:85
  6.8 0.9 fusion.1
  7.8 3.4 %concatenate.26 = bf16[256,768]{0,1:T(8,128)(2,1)} concatenate(bf16[256,640]{0,1:T(8,128)(2,1)S(1)} %dynamic-slice_convert_fusion, bf16[256,1]{0,1:T(2,128)(2,1)S(1)} %get-tuple-element.56, bf16[256,1]{0,1:T(2,128)(2,1)S(1)} %get-tuple-element.55, bf16[256,1]{0,1:T(2,128)(2,1)S(1)} %get-tuple-element.54, bf16[256,1]{0,1:T(2,128)(2,1)S(1)} %get-tuple-element.58, ...), dimensions={1} | concatenate | bytes 786432 | tf_op jit(solution)/shard_map/concatenate | solution.py:38
  11.2 3.2 %collective-permute-start = (bf16[256,768]{0,1:T(8,128)(2,1)}, bf16[256,768]{0,1:T(8,128)(2,1)S(1)}, u32[]{:S(2)}, u32[]{:S(2)}) collective-permute-start(bf16[256,768]{0,1:T(8,128)(2,1)} %concatenate.26), channel_id=1, source_target_pairs={{0,32},{32,0},{64,96},{96,64},{128,160},{160,128},{192,224},{224,1... | collective-permute-start | bytes 1179656 | tf_op jit(solution)/shard_map/ppermute | solution.py:91
  14.5 1.5 %collective-permute-done = bf16[256,768]{0,1:T(8,128)(2,1)S(1)} collective-permute-done((bf16[256,768]{0,1:T(8,128)(2,1)}, bf16[256,768]{0,1:T(8,128)(2,1)S(1)}, u32[]{:S(2)}, u32[]{:S(2)}) %collective-permute-start) | collective-permute-done | bytes 393248 | tf_op jit(solution)/shard_map/ppermute | solution.py:91
  16.1 1.2 fusion.104
  17.3 0.6 concatenate.27
  17.9 0.2 constant_dynamic-slice_fusion.6
  18.3 2.7 %collective-permute-start.3 = (bf16[64,768]{0,1:T(8,128)(2,1)S(1)}, bf16[64,768]{0,1:T(8,128)(2,1)S(1)}, u32[]{:S(2)}, u32[]{:S(2)}) collective-permute-start(bf16[64,768]{0,1:T(8,128)(2,1)S(1)} %get-tuple-element.44), channel_id=1, source_target_pairs={{0,24},{2,26},{4,28},{6,30},{8,0},{10,2},{12,4},{14,6},{16,8},{18,... | collective-permute-start | bytes 294920 | tf_op jit(solution)/shard_map/ppermute | solution.py:97
  20.9 5.0 %collective-permute-done.1 = bf16[64,768]{0,1:T(8,128)(2,1)S(1)} collective-permute-done((bf16[64,768]{0,1:T(8,128)(2,1)S(1)}, bf16[64,768]{0,1:T(8,128)(2,1)S(1)}, u32[]{:S(2)}, u32[]{:S(2)}) %collective-permute-start.1) | collective-permute-done | bytes 98336 | tf_op jit(solution)/shard_map/ppermute | solution.py:97
  26.0 3.4 %collective-permute-done.2 = bf16[64,768]{0,1:T(8,128)(2,1)S(1)} collective-permute-done((bf16[64,768]{0,1:T(8,128)(2,1)S(1)}, bf16[64,768]{0,1:T(8,128)(2,1)S(1)}, u32[]{:S(2)}, u32[]{:S(2)}) %collective-permute-start.2) | collective-permute-done | bytes 98336 | tf_op jit(solution)/shard_map/ppermute | solution.py:97
  29.9 0.4 constant_dynamic-slice_fusion.3
  30.3 1.5 %collective-permute-start.4 = (f32[16,768]{0,1:T(8,128)S(1)}, f32[16,768]{0,1:T(8,128)}, u32[]{:S(2)}, u32[]{:S(2)}) collective-permute-start(f32[16,768]{0,1:T(8,128)S(1)} %get-tuple-element.40), channel_id=1, source_target_pairs={{0,2},{2,4},{4,6},{6,0},{8,10},{10,12},{12,14},{14,8},{16,18},{18,... | collective-permute-start | bytes 147464 | tf_op jit(solution)/shard_map/ppermute | solution.py:108
  31.8 2.8 %collective-permute-start.6 = (f32[16,768]{0,1:T(8,128)S(1)}, f32[16,768]{0,1:T(8,128)}, u32[]{:S(2)}, u32[]{:S(2)}) collective-permute-start(f32[16,768]{0,1:T(8,128)S(1)} %get-tuple-element.41), channel_id=1, source_target_pairs={{0,6},{2,0},{4,2},{6,4},{8,14},{10,8},{12,10},{14,12},{16,22},{18,... | collective-permute-start | bytes 147464 | tf_op jit(solution)/shard_map/ppermute | solution.py:108
  34.8 8.1 %collective-permute-done.4 = f32[16,768]{0,1:T(8,128)} collective-permute-done((f32[16,768]{0,1:T(8,128)S(1)}, f32[16,768]{0,1:T(8,128)}, u32[]{:S(2)}, u32[]{:S(2)}) %collective-permute-start.4) | collective-permute-done | bytes 49184 | tf_op jit(solution)/shard_map/ppermute | solution.py:108
  42.9 7.5 %collective-permute-done.6 = f32[16,768]{0,1:T(8,128)} collective-permute-done((f32[16,768]{0,1:T(8,128)S(1)}, f32[16,768]{0,1:T(8,128)}, u32[]{:S(2)}, u32[]{:S(2)}) %collective-permute-start.6) | collective-permute-done | bytes 49184 | tf_op jit(solution)/shard_map/ppermute | solution.py:108
  50.5 19.1 %collective-permute-done.5 = f32[16,768]{0,1:T(8,128)} collective-permute-done((f32[16,768]{0,1:T(8,128)S(1)}, f32[16,768]{0,1:T(8,128)}, u32[]{:S(2)}, u32[]{:S(2)}) %collective-permute-start.5) | collective-permute-done | bytes 49184 | tf_op jit(solution)/shard_map/ppermute | solution.py:108
  69.5 0.8 fusion.95
  70.3 0.9 fusion.97
  71.2 1.3 %fusion.23 = f32[16,640]{0,1:T(8,128)S(1)} fusion(f32[16,768]{0,1:T(8,128)} %collective-permute-done.6, f32[16,768]{0,1:T(8,128)} %collective-permute-done.5, f32[16,768]{0,1:T(8,128)} %collective-permute-done.4, f32[64,768]{0,1:T(8,128)S(1)} %maximum_maximum_fusion, s32[]{:T(128)S(6)} %select_n.159, f32[16]{0:T(128)S(1)} %get-tuple-element.38, ...), kind=kLoop, calls=%fused_computation.35 | loop fusion | flops 71680 | bytes 205060 | tf_op jit(solution)/shard_map/add | solution.py:70
  72.7 2.7 %collective-permute-start.9 = (f32[16,768]{0,1:T(8,128)S(1)}, f32[16,768]{0,1:T(8,128)S(1)}, u32[]{:S(2)}, u32[]{:S(2)}) collective-permute-start(f32[16,768]{0,1:T(8,128)S(1)} %maximum_maximum_fusion.1), channel_id=1, source_target_pairs={{0,192},{32,224},{64,0},{96,32},{128,64},{160,96},{192,128},{224,1... | collective-permute-start | bytes 147464 | tf_op jit(solution)/shard_map/ppermute | solution.py:117
  75.4 0.5 collective-permute-start.8
  75.9 0.6 collective-permute-start.7
  76.6 7.7 %collective-permute-done.9 = f32[16,768]{0,1:T(8,128)S(1)} collective-permute-done((f32[16,768]{0,1:T(8,128)S(1)}, f32[16,768]{0,1:T(8,128)S(1)}, u32[]{:S(2)}, u32[]{:S(2)}) %collective-permute-start.9) | collective-permute-done | bytes 49184 | tf_op jit(solution)/shard_map/ppermute | solution.py:117
  84.2 2.6 %collective-permute-done.8 = f32[16,768]{0,1:T(8,128)S(1)} collective-permute-done((f32[16,768]{0,1:T(8,128)S(1)}, f32[16,768]{0,1:T(8,128)S(1)}, u32[]{:S(2)}, u32[]{:S(2)}) %collective-permute-start.8) | collective-permute-done | bytes 49184 | tf_op jit(solution)/shard_map/ppermute | solution.py:117
  86.8 9.6 %collective-permute-done.7 = f32[16,768]{0,1:T(8,128)S(1)} collective-permute-done((f32[16,768]{0,1:T(8,128)S(1)}, f32[16,768]{0,1:T(8,128)S(1)}, u32[]{:S(2)}, u32[]{:S(2)}) %collective-permute-start.7) | collective-permute-done | bytes 49184 | tf_op jit(solution)/shard_map/ppermute | solution.py:117
  96.5 0.6 collective-permute-start.10
  97.2 1.1 collective-permute-done.10
  98.3 1.0 copy.33
  99.3 0.7 fusion.3
  100.0 0.4 collective-permute-start.11
  100.4 0.9 collective-permute-done.11
  101.2 0.4 collective-permute-start.14
  101.6 0.5 collective-permute-start.13
  102.1 0.6 collective-permute-start.12
  102.8 1.4 %collective-permute-done.14 = f32[16,640]{1,0:T(8,128)S(1)} collective-permute-done((f32[16,640]{1,0:T(8,128)S(1)}, f32[16,640]{1,0:T(8,128)S(1)}, u32[]{:S(2)}, u32[]{:S(2)}) %collective-permute-start.14) | collective-permute-done | bytes 40992 | tf_op jit(solution)/shard_map/ppermute | solution.py:133
  104.2 1.8 %collective-permute-done.13 = f32[16,640]{1,0:T(8,128)S(1)} collective-permute-done((f32[16,640]{1,0:T(8,128)S(1)}, f32[16,640]{1,0:T(8,128)S(1)}, u32[]{:S(2)}, u32[]{:S(2)}) %collective-permute-start.13) | collective-permute-done | bytes 40992 | tf_op jit(solution)/shard_map/ppermute | solution.py:133
  106.0 0.6 collective-permute-done.12
  106.9 3.0 %collective-permute-start.17 = (bf16[16,640]{1,0:T(8,128)(2,1)S(1)}, bf16[16,640]{1,0:T(8,128)(2,1)S(1)}, u32[]{:S(2)}, u32[]{:S(2)}) collective-permute-start(bf16[16,640]{1,0:T(8,128)(2,1)S(1)} %get-tuple-element.10), channel_id=1, source_target_pairs={{0,6},{2,0},{4,2},{6,4},{8,14},{10,8},{12,10},{14,12},{16,22},{18,... | collective-permute-start | bytes 61448 | tf_op jit(solution)/shard_map/ppermute | solution.py:139
  109.9 1.2 collective-permute-done.15
  111.1 0.3 collective-permute-done.17
  111.4 1.0 collective-permute-start.20
  112.4 1.4 %collective-permute-start.19 = (bf16[64,640]{1,0:T(8,128)(2,1)S(1)}, bf16[64,640]{1,0:T(8,128)(2,1)S(1)}, u32[]{:S(2)}, u32[]{:S(2)}) collective-permute-start(bf16[64,640]{1,0:T(8,128)(2,1)S(1)} %constant_dynamic-update-slice_fusion.4), channel_id=1, source_target_pairs={{0,16},{2,18},{4,20},{6,22},{8,24},{10,26},{12,28},{14,30},{16,0},... | collective-permute-start | bytes 245768 | tf_op jit(solution)/shard_map/ppermute | solution.py:139
  113.8 4.4 %collective-permute-done.18 = bf16[64,640]{1,0:T(8,128)(2,1)S(1)} collective-permute-done((bf16[64,640]{1,0:T(8,128)(2,1)S(1)}, bf16[64,640]{1,0:T(8,128)(2,1)S(1)}, u32[]{:S(2)}, u32[]{:S(2)}) %collective-permute-start.18) | collective-permute-done | bytes 81952 | tf_op jit(solution)/shard_map/ppermute | solution.py:139
  118.3 5.0 %collective-permute-start.21 = (bf16[256,640]{1,0:T(8,128)(2,1)S(1)}, bf16[256,640]{1,0:T(8,128)(2,1)S(1)}, u32[]{:S(2)}, u32[]{:S(2)}) collective-permute-start(bf16[256,640]{1,0:T(8,128)(2,1)S(1)} %constant_dynamic-update-slice_fusion), channel_id=1, source_target_pairs={{0,32},{32,0},{64,96},{96,64},{128,160},{160,128},{192,224},{224,1... | collective-permute-start | bytes 983048 | tf_op jit(solution)/shard_map/ppermute | solution.py:146
  123.3 1.3 collective-permute-done.21
  124.6 5.8 %convolution_convert_fusion = bf16[2048,1280]{1,0:T(8,128)(2,1)} fusion(f32[2048,256]{1,0:T(8,128)} %copy-done.1, f32[2048]{0:T(1024)S(1)} %get-tuple-element.6, f32[2048]{0:T(1024)S(1)} %get-tuple-element.8, bf16[256,640]{1,0:T(8,128)(2,1)S(1)} %collective-permute-done.21, bf16[256,640]{1,0:T(8,128)(2,1)S(1)} %constant_dynamic-update-slice_fusion, pred[]{:T(512)S(6)} %eq.21), kind=kOutput, calls=%fused_computation | convolution fusion | flops 1349320704 | bytes 8011777 | tf_op jit(solution)/shard_map/dot_general | solution.py:156
  (53 shorter events, 1.8 us)
Async XLA Ops:
  0.0 99.3 %copy-start = (bf16[1,640,1280]{2,1,0:T(8,128)(2,1)S(1)}, bf16[1,640,1280]{2,1,0:T(8,128)(2,1)}, u32[]{:S(2)}) copy-start(bf16[1,640,1280]{2,1,0:T(8,128)(2,1)} %param.7) | copy-start | bytes 4915204
  0.0 4.5 %copy-start.4 = (bf16[2048,1280]{1,0:T(8,128)(2,1)S(1)}, bf16[2048,1280]{1,0:T(8,128)(2,1)}, u32[]{:S(2)}) copy-start(bf16[2048,1280]{1,0:T(8,128)(2,1)} %param.4) | copy-start | bytes 15728644
  4.4 2.3 %copy-start.1 = (f32[2048,256]{1,0:T(8,128)}, f32[2048,256]{1,0:T(8,128)S(1)}, u32[]{:S(2)}) copy-start(f32[2048,256]{1,0:T(8,128)S(1)} %get-tuple-element.57) | copy-start | bytes 6291460
  6.7 9.3 %copy-start.3 = (f32[256,1280]{0,1:T(8,128)}, f32[256,1280]{0,1:T(8,128)S(1)}, u32[]{:S(2)}) copy-start(f32[256,1280]{0,1:T(8,128)S(1)} %fusion.7) | copy-start | bytes 3932164
  11.2 4.8 %collective-permute-start = (bf16[256,768]{0,1:T(8,128)(2,1)}, bf16[256,768]{0,1:T(8,128)(2,1)S(1)}, u32[]{:S(2)}, u32[]{:S(2)}) collective-permute-start(bf16[256,768]{0,1:T(8,128)(2,1)} %concatenate.26), channel_id=1, source_target_pairs={{0,32},{32,0},{64,96},{96,64},{128,160},{160,128},{192,224},{224,1... | collective-permute-start | bytes 1179656 | tf_op jit(solution)/shard_map/ppermute | solution.py:91
  18.2 7.8 %collective-permute-start.1 = (bf16[64,768]{0,1:T(8,128)(2,1)S(1)}, bf16[64,768]{0,1:T(8,128)(2,1)S(1)}, u32[]{:S(2)}, u32[]{:S(2)}) collective-permute-start(bf16[64,768]{0,1:T(8,128)(2,1)S(1)} %get-tuple-element.43), channel_id=1, source_target_pairs={{0,8},{2,10},{4,12},{6,14},{8,16},{10,18},{12,20},{14,22},{16,24},... | collective-permute-start | bytes 294920 | tf_op jit(solution)/shard_map/ppermute | solution.py:97
  18.3 7.7 %collective-permute-start.3 = (bf16[64,768]{0,1:T(8,128)(2,1)S(1)}, bf16[64,768]{0,1:T(8,128)(2,1)S(1)}, u32[]{:S(2)}, u32[]{:S(2)}) collective-permute-start(bf16[64,768]{0,1:T(8,128)(2,1)S(1)} %get-tuple-element.44), channel_id=1, source_target_pairs={{0,24},{2,26},{4,28},{6,30},{8,0},{10,2},{12,4},{14,6},{16,8},{18,... | collective-permute-start | bytes 294920 | tf_op jit(solution)/shard_map/ppermute | solution.py:97
  20.9 8.5 %collective-permute-start.2 = (bf16[64,768]{0,1:T(8,128)(2,1)S(1)}, bf16[64,768]{0,1:T(8,128)(2,1)S(1)}, u32[]{:S(2)}, u32[]{:S(2)}) collective-permute-start(bf16[64,768]{0,1:T(8,128)(2,1)S(1)} %get-tuple-element.45), channel_id=1, source_target_pairs={{0,16},{2,18},{4,20},{6,22},{8,24},{10,26},{12,28},{14,30},{16,0},... | collective-permute-start | bytes 294920 | tf_op jit(solution)/shard_map/ppermute | solution.py:97
  30.3 12.6 %collective-permute-start.4 = (f32[16,768]{0,1:T(8,128)S(1)}, f32[16,768]{0,1:T(8,128)}, u32[]{:S(2)}, u32[]{:S(2)}) collective-permute-start(f32[16,768]{0,1:T(8,128)S(1)} %get-tuple-element.40), channel_id=1, source_target_pairs={{0,2},{2,4},{4,6},{6,0},{8,10},{10,12},{12,14},{14,8},{16,18},{18,... | collective-permute-start | bytes 147464 | tf_op jit(solution)/shard_map/ppermute | solution.py:108
  31.8 18.6 %collective-permute-start.6 = (f32[16,768]{0,1:T(8,128)S(1)}, f32[16,768]{0,1:T(8,128)}, u32[]{:S(2)}, u32[]{:S(2)}) collective-permute-start(f32[16,768]{0,1:T(8,128)S(1)} %get-tuple-element.41), channel_id=1, source_target_pairs={{0,6},{2,0},{4,2},{6,4},{8,14},{10,8},{12,10},{14,12},{16,22},{18,... | collective-permute-start | bytes 147464 | tf_op jit(solution)/shard_map/ppermute | solution.py:108
  34.6 34.9 %collective-permute-start.5 = (f32[16,768]{0,1:T(8,128)S(1)}, f32[16,768]{0,1:T(8,128)}, u32[]{:S(2)}, u32[]{:S(2)}) collective-permute-start(f32[16,768]{0,1:T(8,128)S(1)} %get-tuple-element.42), channel_id=1, source_target_pairs={{0,4},{2,6},{4,0},{6,2},{8,12},{10,14},{12,8},{14,10},{16,20},{18,... | collective-permute-start | bytes 147464 | tf_op jit(solution)/shard_map/ppermute | solution.py:108
  72.5 26.8 %copy-start.2 = (bf16[1,1280,640]{2,1,0:T(8,128)(2,1)S(1)}, bf16[1,1280,640]{2,1,0:T(8,128)(2,1)}, u32[]{:S(2)}) copy-start(bf16[1,1280,640]{2,1,0:T(8,128)(2,1)} %param.6) | copy-start | bytes 4915204
  72.7 11.5 %collective-permute-start.9 = (f32[16,768]{0,1:T(8,128)S(1)}, f32[16,768]{0,1:T(8,128)S(1)}, u32[]{:S(2)}, u32[]{:S(2)}) collective-permute-start(f32[16,768]{0,1:T(8,128)S(1)} %maximum_maximum_fusion.1), channel_id=1, source_target_pairs={{0,192},{32,224},{64,0},{96,32},{128,64},{160,96},{192,128},{224,1... | collective-permute-start | bytes 147464 | tf_op jit(solution)/shard_map/ppermute | solution.py:117
  75.4 11.4 %collective-permute-start.8 = (f32[16,768]{0,1:T(8,128)S(1)}, f32[16,768]{0,1:T(8,128)S(1)}, u32[]{:S(2)}, u32[]{:S(2)}) collective-permute-start(f32[16,768]{0,1:T(8,128)S(1)} %maximum_maximum_fusion.1), channel_id=1, source_target_pairs={{0,128},{32,160},{64,192},{96,224},{128,0},{160,32},{192,64},{224,... | collective-permute-start | bytes 147464 | tf_op jit(solution)/shard_map/ppermute | solution.py:117
  75.9 20.4 %collective-permute-start.7 = (f32[16,768]{0,1:T(8,128)S(1)}, f32[16,768]{0,1:T(8,128)S(1)}, u32[]{:S(2)}, u32[]{:S(2)}) collective-permute-start(f32[16,768]{0,1:T(8,128)S(1)} %maximum_maximum_fusion.1), channel_id=1, source_target_pairs={{0,64},{32,96},{64,128},{96,160},{128,192},{160,224},{192,0},{224,... | collective-permute-start | bytes 147464 | tf_op jit(solution)/shard_map/ppermute | solution.py:117
  96.5 1.7 %collective-permute-start.10 = (bf16[16,640]{0,1:T(8,128)(2,1)S(1)}, bf16[16,640]{0,1:T(8,128)(2,1)}, u32[]{:S(2)}, u32[]{:S(2)}) collective-permute-start(bf16[16,640]{0,1:T(8,128)(2,1)S(1)} %fusion.29), channel_id=1, source_target_pairs={{0,32},{32,0},{64,96},{96,64},{128,160},{160,128},{192,224},{224,1... | collective-permute-start | bytes 61448 | tf_op jit(solution)/shard_map/ppermute | solution.py:120
  100.0 1.3 collective-permute-start.11
  101.2 2.9 %collective-permute-start.14 = (f32[16,640]{1,0:T(8,128)S(1)}, f32[16,640]{1,0:T(8,128)S(1)}, u32[]{:S(2)}, u32[]{:S(2)}) collective-permute-start(f32[16,640]{1,0:T(8,128)S(1)} %dynamic-slice_add_fusion), channel_id=1, source_target_pairs={{0,192},{32,224},{64,0},{96,32},{128,64},{160,96},{192,128},{224,1... | collective-permute-start | bytes 122888 | tf_op jit(solution)/shard_map/ppermute | solution.py:133
  101.6 4.4 %collective-permute-start.13 = (f32[16,640]{1,0:T(8,128)S(1)}, f32[16,640]{1,0:T(8,128)S(1)}, u32[]{:S(2)}, u32[]{:S(2)}) collective-permute-start(f32[16,640]{1,0:T(8,128)S(1)} %dynamic-slice_add_fusion), channel_id=1, source_target_pairs={{0,128},{32,160},{64,192},{96,224},{128,0},{160,32},{192,64},{224,... | collective-permute-start | bytes 122888 | tf_op jit(solution)/shard_map/ppermute | solution.py:133
  102.1 4.4 %collective-permute-start.12 = (f32[16,640]{1,0:T(8,128)S(1)}, f32[16,640]{1,0:T(8,128)S(1)}, u32[]{:S(2)}, u32[]{:S(2)}) collective-permute-start(f32[16,640]{1,0:T(8,128)S(1)} %dynamic-slice_add_fusion), channel_id=1, source_target_pairs={{0,64},{32,96},{64,128},{96,160},{128,192},{160,224},{192,0},{224,... | collective-permute-start | bytes 122888 | tf_op jit(solution)/shard_map/ppermute | solution.py:133
  106.6 4.5 %collective-permute-start.15 = (bf16[16,640]{1,0:T(8,128)(2,1)S(1)}, bf16[16,640]{1,0:T(8,128)(2,1)S(1)}, u32[]{:S(2)}, u32[]{:S(2)}) collective-permute-start(bf16[16,640]{1,0:T(8,128)(2,1)S(1)} %get-tuple-element.10), channel_id=1, source_target_pairs={{0,2},{2,4},{4,6},{6,0},{8,10},{10,12},{12,14},{14,8},{16,18},{18,... | collective-permute-start | bytes 61448 | tf_op jit(solution)/shard_map/ppermute | solution.py:139
  106.8 4.3 %collective-permute-start.16 = (bf16[16,640]{1,0:T(8,128)(2,1)S(1)}, bf16[16,640]{1,0:T(8,128)(2,1)S(1)}, u32[]{:S(2)}, u32[]{:S(2)}) collective-permute-start(bf16[16,640]{1,0:T(8,128)(2,1)S(1)} %get-tuple-element.10), channel_id=1, source_target_pairs={{0,4},{2,6},{4,0},{6,2},{8,12},{10,14},{12,8},{14,10},{16,20},{18,... | collective-permute-start | bytes 61448 | tf_op jit(solution)/shard_map/ppermute | solution.py:139
  106.9 4.5 %collective-permute-start.17 = (bf16[16,640]{1,0:T(8,128)(2,1)S(1)}, bf16[16,640]{1,0:T(8,128)(2,1)S(1)}, u32[]{:S(2)}, u32[]{:S(2)}) collective-permute-start(bf16[16,640]{1,0:T(8,128)(2,1)S(1)} %get-tuple-element.10), channel_id=1, source_target_pairs={{0,6},{2,0},{4,2},{6,4},{8,14},{10,8},{12,10},{14,12},{16,22},{18,... | collective-permute-start | bytes 61448 | tf_op jit(solution)/shard_map/ppermute | solution.py:139
  111.4 6.9 %collective-permute-start.20 = (bf16[64,640]{1,0:T(8,128)(2,1)S(1)}, bf16[64,640]{1,0:T(8,128)(2,1)S(1)}, u32[]{:S(2)}, u32[]{:S(2)}) collective-permute-start(bf16[64,640]{1,0:T(8,128)(2,1)S(1)} %constant_dynamic-update-slice_fusion.4), channel_id=1, source_target_pairs={{0,24},{2,26},{4,28},{6,30},{8,0},{10,2},{12,4},{14,6},{16,8},{18,... | collective-permute-start | bytes 245768 | tf_op jit(solution)/shard_map/ppermute | solution.py:139
  112.4 5.9 %collective-permute-start.19 = (bf16[64,640]{1,0:T(8,128)(2,1)S(1)}, bf16[64,640]{1,0:T(8,128)(2,1)S(1)}, u32[]{:S(2)}, u32[]{:S(2)}) collective-permute-start(bf16[64,640]{1,0:T(8,128)(2,1)S(1)} %constant_dynamic-update-slice_fusion.4), channel_id=1, source_target_pairs={{0,16},{2,18},{4,20},{6,22},{8,24},{10,26},{12,28},{14,30},{16,0},... | collective-permute-start | bytes 245768 | tf_op jit(solution)/shard_map/ppermute | solution.py:139
  113.7 4.5 %collective-permute-start.18 = (bf16[64,640]{1,0:T(8,128)(2,1)S(1)}, bf16[64,640]{1,0:T(8,128)(2,1)S(1)}, u32[]{:S(2)}, u32[]{:S(2)}) collective-permute-start(bf16[64,640]{1,0:T(8,128)(2,1)S(1)} %constant_dynamic-update-slice_fusion.4), channel_id=1, source_target_pairs={{0,8},{2,10},{4,12},{6,14},{8,16},{10,18},{12,20},{14,22},{16,24},... | collective-permute-start | bytes 245768 | tf_op jit(solution)/shard_map/ppermute | solution.py:139
  118.3 6.3 %collective-permute-start.21 = (bf16[256,640]{1,0:T(8,128)(2,1)S(1)}, bf16[256,640]{1,0:T(8,128)(2,1)S(1)}, u32[]{:S(2)}, u32[]{:S(2)}) collective-permute-start(bf16[256,640]{1,0:T(8,128)(2,1)S(1)} %constant_dynamic-update-slice_fusion), channel_id=1, source_target_pairs={{0,32},{32,0},{64,96},{96,64},{128,160},{160,128},{192,224},{224,1... | collective-permute-start | bytes 983048 | tf_op jit(solution)/shard_map/ppermute | solution.py:146

commit v2 on v0

v2 whole, which is shorter than its diff:
```python
import functools

import jax
import jax.numpy as jnp
from jax import lax
from jax.experimental import pallas as pl
from jax.experimental.pallas import tpu as pltpu
from jax.sharding import PartitionSpec as P

F32 = jnp.float32
BF16 = jnp.bfloat16
LANES = 128
VMEM = pl.BlockSpec(memory_space=pltpu.VMEM)
SMEM = pl.BlockSpec(memory_space=pltpu.SMEM)
ANY = pl.BlockSpec(memory_space=pl.ANY)


def _core_perm():
    return [(s, s ^ 1) for s in range(8)]


def _x_perm(k):
    return [(s, ((s // 2 + k) % 4) * 2 + s % 2) for s in range(8)]


def _y_perm(k):
    return [(e, ((e // 4 + k) % 4) * 4 + e % 4) for e in range(16)]


def _z_perm(k):
    return [(e, (e // 4) * 4 + (e % 4 + k) % 4) for e in range(16)]


def _call(kernel, name, out_shape, in_specs, scratch=(), out_specs=None, flops=0, bytes_accessed=0, **kw):
    many = isinstance(out_shape, list)
    if out_specs is None:
        out_specs = [VMEM] * len(out_shape) if many else VMEM
    return pl.pallas_call(
        kernel,
        in_specs=in_specs,
        out_specs=out_specs,
        out_shape=out_shape,
        scratch_shapes=list(scratch),
        compiler_params=pltpu.CompilerParams(vmem_limit_bytes=36 << 20),
        cost_estimate=pl.CostEstimate(flops=flops, bytes_accessed=bytes_accessed, transcendentals=0),
        name=name,
        **kw,
    )


def _stats(peak, total, n):
    lane = lax.broadcasted_iota(jnp.int32, (n, LANES), 1)
    st = jnp.zeros((n, LANES), F32)
    j = 0
    for v in (peak, total):
        for _ in range(3):
            p = v.astype(BF16).astype(F32)
            st = jnp.where(lane == j, p, st)
            v = v - p
            j += 1
    return st


def _read16(packed):
    n = packed.shape[1] - LANES
    v = packed.astype(F32)
    st = v[:, n:]
    return (
        v[:, :n],
        st[:, 0:1] + st[:, 1:2] + st[:, 2:3],
        st[:, 3:4] + st[:, 4:5] + st[:, 5:6],
    )


def _read32(v):
    n = v.shape[1] - LANES
    return v[:, :n], v[:, n : n + 1], v[:, n + 1 : n + 2]


def _pair(peak, total, n):
    lane = lax.broadcasted_iota(jnp.int32, (n, LANES), 1)
    return jnp.where(lane == 0, peak, jnp.where(lane == 1, total, 0.0))


def _merge(parts):
    peak = parts[0][1]
    for _, p, _ in parts[1:]:
        peak = jnp.maximum(peak, p)
    sums, total = None, None
    for s, p, t in parts:
        a = jnp.exp(p - peak)
        sums = s * a if sums is None else sums + s * a
        total = t * a if total is None else total + t * a
    return sums, peak, total


def _fold(v, op):
    out = v[:, :LANES]
    for j in range(1, v.shape[1] // LANES):
        out = op(out, v[:, j * LANES : (j + 1) * LANES])
    return out


def first_kernel(chunks, where, tok_hbm, keys_hbm, tok, logits, dispatch, packed, stat, keys, sem):
    tokens, width = tok.shape
    slots = logits.shape[0]
    half = width // 2
    step = tokens // chunks
    keys_copy = pltpu.make_async_copy(keys_hbm, keys, sem.at[chunks])
    keys_copy.start()
    copies = [
        pltpu.make_async_copy(
            tok_hbm.at[pl.ds(i * step, step)], tok.at[pl.ds(i * step, step)], sem.at[i]
        )
        for i in range(chunks)
    ]
    for c in copies:
        c.start()
    keys_copy.wait()
    keys_t = keys[...].T
    peak = None
    for i in range(chunks):
        copies[i].wait()
        part = lax.dot_general(
            keys_t,
            tok[i * step : (i + 1) * step, :],
            (((1,), (1,)), ((), ())),
            preferred_element_type=F32,
        )
        logits[:, i * step : (i + 1) * step] = part
        p = _fold(part, jnp.maximum)
        peak = p if peak is None else jnp.maximum(peak, p)
    peak = jnp.max(peak, axis=1, keepdims=True)
    total = None
    for i in range(chunks):
        e = jnp.exp(logits[:, i * step : (i + 1) * step] - peak)
        dispatch[:, i * step : (i + 1) * step] = e.astype(BF16)
        p = _fold(e, jnp.add)
        total = p if total is None else total + p
    total = jnp.sum(total, axis=1, keepdims=True)
    off = pl.multiple_of((1 - where[0]) * half, LANES)
    sums = jnp.dot(dispatch[...], tok[:, pl.ds(off, half)], preferred_element_type=F32)
    packed[:, :half] = sums.astype(BF16)
    packed[:, half:] = _stats(peak, total, slots).astype(BF16)
    stat[...] = _pair(peak, total, slots)


def own_kernel(where, tok, dispatch, stat, own):
    half = tok.shape[1] // 2
    off = pl.multiple_of(where[0] * half, LANES)
    own[:, :half] = jnp.dot(dispatch[...], tok[:, pl.ds(off, half)], preferred_element_type=F32)
    own[:, half:] = stat[...]


def combine_kernel(logits, combine):
    v = logits[...]
    e = jnp.exp(v - jnp.max(v, axis=0, keepdims=True))
    combine[...] = (e / jnp.sum(e, axis=0, keepdims=True)).astype(BF16).T


def core_merge_kernel(where, own, got, keep, send1, send2, send3):
    rows = keep.shape[0]
    half = own.shape[1] - LANES
    for k, ref in enumerate((keep, send1, send2, send3)):
        start = pl.multiple_of(lax.rem(where[1] + k, 4) * rows, rows)
        sums, peak, total = _merge(
            [_read32(own[pl.ds(start, rows), :]), _read16(got[pl.ds(start, rows), :])]
        )
        ref[:, :half] = sums.astype(ref.dtype)
        st = _pair(peak, total, rows) if k == 0 else _stats(peak, total, rows)
        ref[:, half:] = st.astype(ref.dtype)


def y_merge_kernel(where, own, got1, got2, got3, keep, send1, send2, send3):
    rows = keep.shape[0]
    half = own.shape[1] - LANES
    for k, ref in enumerate((keep, send1, send2, send3)):
        part = pl.ds(pl.multiple_of(lax.rem(where[2] + k, 4) * rows, rows), rows)
        sums, peak, total = _merge(
            [_read32(own[part, :])] + [_read16(g[part, :]) for g in (got1, got2, got3)]
        )
        ref[:, :half] = sums
        ref[:, half:] = _pair(peak, total, rows)


def z_merge_kernel(own, got1, got2, got3, out):
    half = own.shape[1] - LANES
    sums, peak, total = _merge([_read32(g[...]) for g in (own, got1, got2, got3)])
    out[:, :half] = sums
    out[:, half:] = _pair(peak, total, out.shape[0])


def x_merge_kernel(own, got1, got2, got3, out):
    sums, _, total = _merge([_read32(g[...]) for g in (own, got1, got2, got3)])
    out[...] = (sums / total).astype(BF16)


def mix_kernel(chunks, where, combine, own, other, out_hbm, slot_out, buf, sem):
    half = own.shape[1]
    step = combine.shape[0] // chunks
    slot_out[:, pl.ds(pl.multiple_of(where[0] * half, LANES), half)] = own[...]
    slot_out[:, pl.ds(pl.multiple_of((1 - where[0]) * half, LANES), half)] = other[...]
    copies = []
    depth = buf.shape[0]
    for i in range(chunks):
        if i >= depth:
            copies[i - depth].wait()
        buf[i % depth] = jnp.dot(
            combine[i * step : (i + 1) * step, :], slot_out[...], preferred_element_type=F32
        ).astype(BF16)
        c = pltpu.make_async_copy(
            buf.at[i % depth], out_hbm.at[pl.ds(i * step, step)], sem.at[i % depth]
        )
        c.start()
        copies.append(c)
    for c in copies[-depth:]:
        c.wait()


def body(tokens, slot_keys, w_in, w_out):
    seq, exp = lax.axis_index("seq"), lax.axis_index("exp")
    core, y, z = seq % 2, exp // 4, exp % 4
    where = jnp.stack([core, y, z]).astype(jnp.int32)
    count, width = tokens.shape
    slots = slot_keys.shape[1]
    half = width // 2
    packed_width = half + LANES
    chunks = 4

    tok, logits, dispatch, packed, stat = _call(
        functools.partial(first_kernel, chunks),
        "logits_and_sums",
        [
            pltpu.VMEM((count, width), BF16),
            pltpu.VMEM((slots, count), F32),
            pltpu.VMEM((slots, count), BF16),
            pltpu.VMEM((slots, packed_width), BF16),
            pltpu.VMEM((slots, LANES), F32),
        ],
        [SMEM, ANY, ANY],
        [pltpu.VMEM((width, slots), BF16), pltpu.SemaphoreType.DMA((chunks + 1,))],
        flops=3 * count * slots * width,
        bytes_accessed=2 * count * width,
    )(where, tokens, slot_keys)

    got = lax.ppermute(packed, "seq", _core_perm())
    own = _call(
        own_kernel,
        "own_sums",
        pltpu.VMEM((slots, packed_width), F32),
        [SMEM, VMEM, VMEM, VMEM],
        flops=count * slots * width,
    )(where, tok, dispatch, stat)
    combine = _call(
        combine_kernel,
        "combine",
        pltpu.VMEM((count, slots), BF16),
        [VMEM],
        flops=10 * count * slots,
    )(logits)

    rows = slots // 4
    own, *send = _call(
        core_merge_kernel,
        "core_merge",
        [pltpu.VMEM((rows, packed_width), F32)] + [pltpu.VMEM((rows, packed_width), BF16)] * 3,
        [SMEM, VMEM, VMEM],
    )(where, own, got)
    got = [lax.ppermute(v, "exp", _y_perm(k + 1)) for k, v in enumerate(send)]

    rows = rows // 4
    own, *send = _call(
        y_merge_kernel,
        "y_merge",
        [pltpu.VMEM((rows, packed_width), F32)] * 4,
        [SMEM] + [VMEM] * 4,
    )(where, own, *got)
    got = [lax.ppermute(v, "exp", _z_perm(k + 1)) for k, v in enumerate(send)]

    own = _call(
        z_merge_kernel, "z_merge", pltpu.VMEM((rows, packed_width), F32), [VMEM] * 4
    )(own, *got)
    got = [lax.ppermute(own, "seq", _x_perm(k)) for k in range(1, 4)]
    slot_half = _call(x_merge_kernel, "x_merge", pltpu.VMEM((rows, half), BF16), [VMEM] * 4)(
        own, *got
    )
    got = lax.ppermute(slot_half, "seq", _core_perm())
    slot_in = jnp.where(
        core == 0,
        jnp.concatenate([slot_half, got], axis=1),
        jnp.concatenate([got, slot_half], axis=1),
    )

    hidden = jax.nn.gelu(jnp.dot(slot_in, w_in[0], preferred_element_type=F32)).astype(BF16)
    partial = jnp.dot(hidden, w_out[0], preferred_element_type=F32)

    mine = lax.dynamic_slice_in_dim(partial, core * half, half, 1)
    other = lax.dynamic_slice_in_dim(partial, (1 - core) * half, half, 1)
    part = mine + lax.ppermute(other, "seq", _core_perm())
    whole = part + sum(lax.ppermute(part, "seq", _x_perm(k)) for k in range(1, 4))
    out = whole.astype(BF16)

    def gather(block, index, perm):
        n = block.shape[0]
        res = jnp.zeros((4 * n, block.shape[1]), block.dtype)
        blocks = [block] + [lax.ppermute(block, "exp", perm(k)) for k in range(1, 4)]
        for k, g in enumerate(blocks):
            res = lax.dynamic_update_slice_in_dim(res, g, ((index - k) % 4) * n, 0)
        return res

    out = gather(out, z, _z_perm)
    out = gather(out, y, _y_perm)
    other = lax.ppermute(out, "seq", _core_perm())

    steps = 8
    return _call(
        functools.partial(mix_kernel, steps),
        "mix",
        jax.ShapeDtypeStruct((count, width), BF16),
        [SMEM, VMEM, VMEM, VMEM],
        [
            pltpu.VMEM((slots, width), BF16),
            pltpu.VMEM((4, count // steps, width), BF16),
            pltpu.SemaphoreType.DMA((4,)),
        ],
        out_specs=ANY,
    )(where, combine, out, other)


def solution(mesh):
    return jax.shard_map(
        body,
        mesh=mesh,
        in_specs=(P(("dp", "seq", "exp"), None), P(), P("exp", None, "seq"), P("exp", "seq", None)),
        out_specs=P(("dp", "seq", "exp"), None),
        check_vma=False,
    )
```

time: 1680 us -> 75.6 us (0.04)
  waiting for transfers between devices: 922 us -> 18.3 us
  blocking collectives: 719 us -> 0 us
  starting transfers between devices: 0.01 us -> 36.9 us
  matrix products: 18.8 us -> 0.66 us
    psum x1 -> x0, waiting for transfers between devices: 922 us -> none  [body(): all_sums, all_totals = lax.psum((weighted, local_total), ('seq', 'exp'))]
    psum x2 -> x0, blocking collectives: 371 us -> none  [the longest x1 335 us: body(): all_sums, all_totals = lax.psum((weighted, local_total), ('seq', 'exp'))]
    pmax x1 -> x0, blocking collectives: 308 us -> none  [body(): slot_peak = lax.pmax(jnp.max(logits, axis=0), ('seq', 'exp'))]
    all_gather x1 -> x0, blocking collectives: 39.7 us -> none  [body(): lax.all_gather(slot_out, 'exp', axis=0, tiled=True)]
    ppermute x0 -> x22, starting transfers between devices: none -> 36.9 us  [the longest x6 7.71 us: gather(): lax.ppermute(block, 'exp', perm(k))]
    ppermute x0 -> x22, waiting for transfers between devices: none -> 18.3 us  [the longest x3 4.57 us: body(): got = [lax.ppermute(v, 'exp', _y_perm(k + 1)) for k, v in enumerate(send)]]
    dot_general x4 -> x1, matrix products: 18.8 us -> 0.66 us  [body(): partial = jnp.dot(hidden, w_out[0], preferred_element_type=F32)]
  transfers between devices with their start and end apart: 1 -> 22, of which waited for: 1 -> 18; matrix products, arithmetic and copies ran while one was open for 0% -> 0% of each run, Pallas kernels for 0% -> 3%
where the time goes in v2:
time: 75.6 us; the launch traced here: 75.4 us
  starting transfers between devices  36.9 us (49%)
  waiting for transfers between devices  18.3 us (24%)
  Pallas kernels  13.6 us (18%)
  local copies, waits for them, and re-layouts  5.42 us (7%)
    ppermute x6, starting transfers between devices, gather(): lax.ppermute(block, 'exp', perm(k))  7.71 us
    ppermute x1, starting transfers between devices, body(): other = lax.ppermute(out, 'seq', _core_perm())  5.42 us
    unnamed x12, local copies, waits for them, and re-layouts  5.29 us
    ppermute x3, starting transfers between devices, body(): got = [lax.ppermute(own, 'seq', _x_perm(k)) for k in range(1, 4)]  4.81 us
    pallas_call x1, Pallas kernels, body(): _call(functools.partial(first_kernel, chunks), 'logits_and_sums', [pltpu....  4.74 us
    ppermute x3, starting transfers between devices, body(): got = [lax.ppermute(v, 'exp', _z_perm(k + 1)) for k, v in enumerate(send)]  4.68 us
    ppermute x3, waiting for transfers between devices, body(): got = [lax.ppermute(v, 'exp', _y_perm(k + 1)) for k, v in enumerate(send)]  4.57 us
    pallas_call x1, Pallas kernels, body(): _call(functools.partial(mix_kernel, steps), 'mix', jax.ShapeDtypeStruct((...  4.17 us
  transfers between devices with their start and end apart: 22, of which 18 were waited for; matrix products, arithmetic and copies ran while one was open for 0% of the time, Pallas kernels for 3%

profile of v2, /device:TPU:1, one launch (start us, length us, event | category | flops | bytes accessed | tf_op | source)
XLA Modules:
  0.0 75.4 jit_solution(10662959911354456061)
XLA Ops:
  0.1 2.6 %copy-done.3 = bf16[2048,1280]{1,0:T(8,128)(2,1)S(1)} copy-done((bf16[2048,1280]{1,0:T(8,128)(2,1)S(1)}, bf16[2048,1280]{1,0:T(8,128)(2,1)}, u32[]{:S(2)}) %copy-start.3) | copy-done | bytes 5242904
  2.7 1.1 %copy-done.4 = bf16[1280,256]{1,0:T(8,128)(2,1)S(1)} copy-done((bf16[1280,256]{1,0:T(8,128)(2,1)S(1)}, bf16[1280,256]{1,0:T(8,128)(2,1)}, u32[]{:S(2)}) %copy-start.4) | copy-done | bytes 655384
  3.8 4.7 %logits_and_sums.1 = (bf16[2048,1280]{1,0:T(8,128)(2,1)S(1)}, f32[256,2048]{1,0:T(8,128)S(1)}, bf16[256,2048]{1,0:T(8,128)(2,1)S(1)}, bf16[256,768]{1,0:T(8,128)(2,1)S(1)}, f32[256,128]{1,0:T(8,128)S(1)}) custom-call(s32[3]{0:T(128)S(1)} %pad_add_fusion.where, bf16[2048,1280]{1,0:T(8,128)(2,1)S(1)} %copy-done.3, bf16[1280,256]{1,0:T(8,128)(2,1)S(1)} %copy-done.4), custom_call_target="tpu_custom_call" | custom-call | flops 2013265920 | bytes 5242880 | tf_op jit(solution)/shard_map/logits_and_sums/pallas_call | solution.py:230
  8.5 3.4 %collective-permute-start = (bf16[256,768]{1,0:T(8,128)(2,1)S(1)}, bf16[256,768]{1,0:T(8,128)(2,1)S(1)}, u32[]{:S(2)}, u32[]{:S(2)}) collective-permute-start(bf16[256,768]{1,0:T(8,128)(2,1)S(1)} %get-tuple-element.22), channel_id=1, source_target_pairs={{0,32},{32,0},{64,96},{96,64},{128,160},{160,128},{192,224},{224,1... | collective-permute-start | bytes 1179656 | tf_op jit(solution)/shard_map/ppermute | solution.py:246
  11.9 1.5 %own_sums.1.own = f32[256,768]{1,0:T(8,128)S(1)} custom-call(s32[3]{0:T(128)S(1)} %pad_add_fusion.where, bf16[2048,1280]{1,0:T(8,128)(2,1)S(1)} %get-tuple-element.19.tok, bf16[256,2048]{1,0:T(8,128)(2,1)S(1)} %get-tuple-element.20.dispatch, f32[256,128]{1,0:T(8,128)S(1)} %get-tuple-element.21.stat), custom_call_target="tpu_custom_call" | custom-call | flops 671088640 | tf_op jit(solution)/shard_map/own_sums/pallas_call | solution.py:247
  13.5 1.3 %core_merge.1 = (f32[64,768]{1,0:T(8,128)S(1)}, bf16[64,768]{1,0:T(8,128)(2,1)S(1)}, bf16[64,768]{1,0:T(8,128)(2,1)S(1)}, bf16[64,768]{1,0:T(8,128)(2,1)S(1)}) custom-call(s32[3]{0:T(128)S(1)} %pad_add_fusion.where, f32[256,768]{1,0:T(8,128)S(1)} %own_sums.1.own, bf16[256,768]{1,0:T(8,128)(2,1)S(1)} %collective-permute-done.got), custom_call_target="tpu_custom_call" | custom-call | tf_op jit(solution)/shard_map/core_merge/pallas_call | solution.py:263
  14.9 2.2 %collective-permute-start.2 = (bf16[64,768]{1,0:T(8,128)(2,1)S(1)}, bf16[64,768]{1,0:T(8,128)(2,1)S(1)}, u32[]{:S(2)}, u32[]{:S(2)}) collective-permute-start(bf16[64,768]{1,0:T(8,128)(2,1)S(1)} %get-tuple-element.25), channel_id=1, source_target_pairs={{0,16},{2,18},{4,20},{6,22},{8,24},{10,26},{12,28},{14,30},{16,0},... | collective-permute-start | bytes 294920 | tf_op jit(solution)/shard_map/ppermute | solution.py:269
  17.0 1.1 %collective-permute-start.3 = (bf16[64,768]{1,0:T(8,128)(2,1)S(1)}, bf16[64,768]{1,0:T(8,128)(2,1)S(1)}, u32[]{:S(2)}, u32[]{:S(2)}) collective-permute-start(bf16[64,768]{1,0:T(8,128)(2,1)S(1)} %get-tuple-element.26), channel_id=1, source_target_pairs={{0,24},{2,26},{4,28},{6,30},{8,0},{10,2},{12,4},{14,6},{16,8},{18,... | collective-permute-start | bytes 294920 | tf_op jit(solution)/shard_map/ppermute | solution.py:269
  18.1 2.7 %collective-permute-done.1.got1 = bf16[64,768]{1,0:T(8,128)(2,1)S(1)} collective-permute-done((bf16[64,768]{1,0:T(8,128)(2,1)S(1)}, bf16[64,768]{1,0:T(8,128)(2,1)S(1)}, u32[]{:S(2)}, u32[]{:S(2)}) %collective-permute-start.1) | collective-permute-done | bytes 98336 | tf_op jit(solution)/shard_map/ppermute | solution.py:269
  20.8 1.2 %collective-permute-done.2.got2 = bf16[64,768]{1,0:T(8,128)(2,1)S(1)} collective-permute-done((bf16[64,768]{1,0:T(8,128)(2,1)S(1)}, bf16[64,768]{1,0:T(8,128)(2,1)S(1)}, u32[]{:S(2)}, u32[]{:S(2)}) %collective-permute-start.2) | collective-permute-done | bytes 98336 | tf_op jit(solution)/shard_map/ppermute | solution.py:269
  22.0 0.7 collective-permute-done.3.got3
  22.7 0.9 %y_merge.1 = (f32[16,768]{1,0:T(8,128)S(1)}, f32[16,768]{1,0:T(8,128)S(1)}, f32[16,768]{1,0:T(8,128)S(1)}, f32[16,768]{1,0:T(8,128)S(1)}) custom-call(s32[3]{0:T(128)S(1)} %pad_add_fusion.where, f32[64,768]{1,0:T(8,128)S(1)} %get-tuple-element.23.own, bf16[64,768]{1,0:T(8,128)(2,1)S(1)} %collective-permute-done.1.got1, ...), custom_call_target="tpu_custom_call" | custom-call | tf_op jit(solution)/shard_map/y_merge/pallas_call | solution.py:272
  23.6 1.0 %collective-permute-start.4 = (f32[16,768]{1,0:T(8,128)S(1)}, f32[16,768]{1,0:T(8,128)S(1)}, u32[]{:S(2)}, u32[]{:S(2)}) collective-permute-start(f32[16,768]{1,0:T(8,128)S(1)} %get-tuple-element.28), channel_id=1, source_target_pairs={{0,2},{2,4},{4,6},{6,0},{8,10},{10,12},{12,14},{14,8},{16,18},{18,... | collective-permute-start | bytes 147464 | tf_op jit(solution)/shard_map/ppermute | solution.py:278
  24.5 3.0 %collective-permute-start.5 = (f32[16,768]{1,0:T(8,128)S(1)}, f32[16,768]{1,0:T(8,128)S(1)}, u32[]{:S(2)}, u32[]{:S(2)}) collective-permute-start(f32[16,768]{1,0:T(8,128)S(1)} %get-tuple-element.29), channel_id=1, source_target_pairs={{0,4},{2,6},{4,0},{6,2},{8,12},{10,14},{12,8},{14,10},{16,20},{18,... | collective-permute-start | bytes 147464 | tf_op jit(solution)/shard_map/ppermute | solution.py:278
  27.5 0.7 collective-permute-start.6
  28.3 0.5 collective-permute-done.4.got1
  28.8 0.5 collective-permute-done.5.got2
  29.3 2.1 %collective-permute-done.6.got3 = f32[16,768]{1,0:T(8,128)S(1)} collective-permute-done((f32[16,768]{1,0:T(8,128)S(1)}, f32[16,768]{1,0:T(8,128)S(1)}, u32[]{:S(2)}, u32[]{:S(2)}) %collective-permute-start.6) | collective-permute-done | bytes 49184 | tf_op jit(solution)/shard_map/ppermute | solution.py:278
  31.6 1.2 %collective-permute-start.7 = (f32[16,768]{1,0:T(8,128)S(1)}, f32[16,768]{1,0:T(8,128)S(1)}, u32[]{:S(2)}, u32[]{:S(2)}) collective-permute-start(f32[16,768]{1,0:T(8,128)S(1)} %z_merge.1.own), channel_id=1, source_target_pairs={{0,64},{32,96},{64,128},{96,160},{128,192},{160,224},{192,0},{224,... | collective-permute-start | bytes 147464 | tf_op jit(solution)/shard_map/ppermute | solution.py:283
  32.8 2.4 %collective-permute-start.8 = (f32[16,768]{1,0:T(8,128)S(1)}, f32[16,768]{1,0:T(8,128)S(1)}, u32[]{:S(2)}, u32[]{:S(2)}) collective-permute-start(f32[16,768]{1,0:T(8,128)S(1)} %z_merge.1.own), channel_id=1, source_target_pairs={{0,128},{32,160},{64,192},{96,224},{128,0},{160,32},{192,64},{224,... | collective-permute-start | bytes 147464 | tf_op jit(solution)/shard_map/ppermute | solution.py:283
  35.2 1.2 %collective-permute-start.9 = (f32[16,768]{1,0:T(8,128)S(1)}, f32[16,768]{1,0:T(8,128)S(1)}, u32[]{:S(2)}, u32[]{:S(2)}) collective-permute-start(f32[16,768]{1,0:T(8,128)S(1)} %z_merge.1.own), channel_id=1, source_target_pairs={{0,192},{32,224},{64,0},{96,32},{128,64},{160,96},{192,128},{224,1... | collective-permute-start | bytes 147464 | tf_op jit(solution)/shard_map/ppermute | solution.py:283
  36.4 0.8 %collective-permute-done.8.got2 = f32[16,768]{1,0:T(8,128)S(1)} collective-permute-done((f32[16,768]{1,0:T(8,128)S(1)}, f32[16,768]{1,0:T(8,128)S(1)}, u32[]{:S(2)}, u32[]{:S(2)}) %collective-permute-start.8) | collective-permute-done | bytes 49184 | tf_op jit(solution)/shard_map/ppermute | solution.py:283
  37.2 1.0 %collective-permute-done.9.got3 = f32[16,768]{1,0:T(8,128)S(1)} collective-permute-done((f32[16,768]{1,0:T(8,128)S(1)}, f32[16,768]{1,0:T(8,128)S(1)}, u32[]{:S(2)}, u32[]{:S(2)}) %collective-permute-start.9) | collective-permute-done | bytes 49184 | tf_op jit(solution)/shard_map/ppermute | solution.py:283
  38.2 0.2 x_merge.1
  38.4 3.7 %collective-permute-start.10 = (bf16[16,640]{1,0:T(8,128)(2,1)S(1)}, bf16[16,640]{1,0:T(8,128)(2,1)S(1)}, u32[]{:S(2)}, u32[]{:S(2)}) collective-permute-start(bf16[16,640]{1,0:T(8,128)(2,1)S(1)} %x_merge.1), channel_id=1, source_target_pairs={{0,32},{32,0},{64,96},{96,64},{128,160},{160,128},{192,224},{224,1... | collective-permute-start | bytes 61448 | tf_op jit(solution)/shard_map/ppermute | solution.py:287
  42.1 0.8 %collective-permute-done.10 = bf16[16,640]{1,0:T(8,128)(2,1)S(1)} collective-permute-done((bf16[16,640]{1,0:T(8,128)(2,1)S(1)}, bf16[16,640]{1,0:T(8,128)(2,1)S(1)}, u32[]{:S(2)}, u32[]{:S(2)}) %collective-permute-start.10) | collective-permute-done | bytes 20512 | tf_op jit(solution)/shard_map/ppermute | solution.py:287
  42.9 0.7 fusion
  43.6 0.4 collective-permute-start.11
  44.0 0.9 %collective-permute-done.11 = f32[16,640]{1,0:T(8,128)S(1)} collective-permute-done((f32[16,640]{1,0:T(8,128)S(1)}, f32[16,640]{1,0:T(8,128)S(1)}, u32[]{:S(2)}, u32[]{:S(2)}) %collective-permute-start.11) | collective-permute-done | bytes 40992 | tf_op jit(solution)/shard_map/ppermute | solution.py:299
  44.8 0.2 collective-permute-start.12
  45.0 3.4 %collective-permute-start.13 = (f32[16,640]{1,0:T(8,128)S(1)}, f32[16,640]{1,0:T(8,128)S(1)}, u32[]{:S(2)}, u32[]{:S(2)}) collective-permute-start(f32[16,640]{1,0:T(8,128)S(1)} %dynamic-slice_add_fusion), channel_id=1, source_target_pairs={{0,128},{32,160},{64,192},{96,224},{128,0},{160,32},{192,64},{224,... | collective-permute-start | bytes 122888 | tf_op jit(solution)/shard_map/ppermute | solution.py:300
  48.5 0.5 collective-permute-done.12
  49.0 1.4 %collective-permute-done.13 = f32[16,640]{1,0:T(8,128)S(1)} collective-permute-done((f32[16,640]{1,0:T(8,128)S(1)}, f32[16,640]{1,0:T(8,128)S(1)}, u32[]{:S(2)}, u32[]{:S(2)}) %collective-permute-start.13) | collective-permute-done | bytes 40992 | tf_op jit(solution)/shard_map/ppermute | solution.py:300
  50.4 1.1 %collective-permute-done.14 = f32[16,640]{1,0:T(8,128)S(1)} collective-permute-done((f32[16,640]{1,0:T(8,128)S(1)}, f32[16,640]{1,0:T(8,128)S(1)}, u32[]{:S(2)}, u32[]{:S(2)}) %collective-permute-start.14) | collective-permute-done | bytes 40992 | tf_op jit(solution)/shard_map/ppermute | solution.py:300
  51.5 0.3 collective-permute-start.15
  51.8 2.6 %collective-permute-start.16 = (bf16[16,640]{1,0:T(8,128)(2,1)S(1)}, bf16[16,640]{1,0:T(8,128)(2,1)S(1)}, u32[]{:S(2)}, u32[]{:S(2)}) collective-permute-start(bf16[16,640]{1,0:T(8,128)(2,1)S(1)} %get-tuple-element.32), channel_id=1, source_target_pairs={{0,4},{2,6},{4,0},{6,2},{8,12},{10,14},{12,8},{14,10},{16,20},{18,... | collective-permute-start | bytes 61448 | tf_op jit(solution)/shard_map/ppermute | solution.py:306
  54.4 0.5 collective-permute-start.17
  54.8 1.2 %collective-permute-done.15 = bf16[16,640]{1,0:T(8,128)(2,1)S(1)} collective-permute-done((bf16[16,640]{1,0:T(8,128)(2,1)S(1)}, bf16[16,640]{1,0:T(8,128)(2,1)S(1)}, u32[]{:S(2)}, u32[]{:S(2)}) %collective-permute-start.15) | collective-permute-done | bytes 20512 | tf_op jit(solution)/shard_map/ppermute | solution.py:306
  56.0 1.0 %collective-permute-done.17 = bf16[16,640]{1,0:T(8,128)(2,1)S(1)} collective-permute-done((bf16[16,640]{1,0:T(8,128)(2,1)S(1)}, bf16[16,640]{1,0:T(8,128)(2,1)S(1)}, u32[]{:S(2)}, u32[]{:S(2)}) %collective-permute-start.17) | collective-permute-done | bytes 20512 | tf_op jit(solution)/shard_map/ppermute | solution.py:306
  57.0 1.0 %collective-permute-start.18 = (bf16[64,640]{1,0:T(8,128)(2,1)S(1)}, bf16[64,640]{1,0:T(8,128)(2,1)S(1)}, u32[]{:S(2)}, u32[]{:S(2)}) collective-permute-start(bf16[64,640]{1,0:T(8,128)(2,1)S(1)} %constant_dynamic-update-slice_fusion.4), channel_id=1, source_target_pairs={{0,8},{2,10},{4,12},{6,14},{8,16},{10,18},{12,20},{14,22},{16,24},... | collective-permute-start | bytes 245768 | tf_op jit(solution)/shard_map/ppermute | solution.py:306
  58.0 2.1 %collective-permute-start.19 = (bf16[64,640]{1,0:T(8,128)(2,1)S(1)}, bf16[64,640]{1,0:T(8,128)(2,1)S(1)}, u32[]{:S(2)}, u32[]{:S(2)}) collective-permute-start(bf16[64,640]{1,0:T(8,128)(2,1)S(1)} %constant_dynamic-update-slice_fusion.4), channel_id=1, source_target_pairs={{0,16},{2,18},{4,20},{6,22},{8,24},{10,26},{12,28},{14,30},{16,0},... | collective-permute-start | bytes 245768 | tf_op jit(solution)/shard_map/ppermute | solution.py:306
  60.1 1.3 %collective-permute-start.20 = (bf16[64,640]{1,0:T(8,128)(2,1)S(1)}, bf16[64,640]{1,0:T(8,128)(2,1)S(1)}, u32[]{:S(2)}, u32[]{:S(2)}) collective-permute-start(bf16[64,640]{1,0:T(8,128)(2,1)S(1)} %constant_dynamic-update-slice_fusion.4), channel_id=1, source_target_pairs={{0,24},{2,26},{4,28},{6,30},{8,0},{10,2},{12,4},{14,6},{16,8},{18,... | collective-permute-start | bytes 245768 | tf_op jit(solution)/shard_map/ppermute | solution.py:306
  61.5 1.3 %collective-permute-done.19 = bf16[64,640]{1,0:T(8,128)(2,1)S(1)} collective-permute-done((bf16[64,640]{1,0:T(8,128)(2,1)S(1)}, bf16[64,640]{1,0:T(8,128)(2,1)S(1)}, u32[]{:S(2)}, u32[]{:S(2)}) %collective-permute-start.19) | collective-permute-done | bytes 81952 | tf_op jit(solution)/shard_map/ppermute | solution.py:306
  62.8 0.6 collective-permute-done.20
  63.4 5.4 %collective-permute-start.21 = (bf16[256,640]{1,0:T(8,128)(2,1)S(1)}, bf16[256,640]{1,0:T(8,128)(2,1)S(1)}, u32[]{:S(2)}, u32[]{:S(2)}) collective-permute-start(bf16[256,640]{1,0:T(8,128)(2,1)S(1)} %constant_dynamic-update-slice_fusion.own), channel_id=1, source_target_pairs={{0,32},{32,0},{64,96},{96,64},{128,160},{160,128},{192,224},{224,1... | collective-permute-start | bytes 983048 | tf_op jit(solution)/shard_map/ppermute | solution.py:313
  68.8 1.6 %copy-done.2 = f32[256,2048]{1,0:T(8,128)S(1)} copy-done((f32[256,2048]{1,0:T(8,128)S(1)}, f32[256,2048]{1,0:T(8,128)}, u32[]{:S(2)}) %copy-start.2) | copy-done | bytes 2097176
  70.4 0.7 combine.1
  71.1 4.2 %mix.1 = bf16[2048,1280]{1,0:T(8,128)(2,1)} custom-call(s32[3]{0:T(128)S(1)} %pad_add_fusion.where, bf16[2048,256]{1,0:T(8,128)(2,1)S(1)} %combine.1, bf16[256,640]{1,0:T(8,128)(2,1)S(1)} %constant_dynamic-update-slice_fusion.own, bf16[256,640]{1,0:T(8,128)(2,1)S(1)} %collective-permute-done.21.other), custom_call_target="tpu_custom_call" | custom-call | tf_op jit(solution)/shard_map/mix/pallas_call | solution.py:316
  (30 shorter events, 0.6 us)
Async XLA Ops:
  0.0 42.9 %copy-start = (bf16[1,640,1280]{2,1,0:T(8,128)(2,1)S(1)}, bf16[1,640,1280]{2,1,0:T(8,128)(2,1)}, u32[]{:S(2)}) copy-start(bf16[1,640,1280]{2,1,0:T(8,128)(2,1)} %param.7) | copy-start | bytes 4915204
  0.1 2.6 %copy-start.3 = (bf16[2048,1280]{1,0:T(8,128)(2,1)S(1)}, bf16[2048,1280]{1,0:T(8,128)(2,1)}, u32[]{:S(2)}) copy-start(bf16[2048,1280]{1,0:T(8,128)(2,1)} %tok_hbm.1) | copy-start | bytes 15728644
  2.7 1.1 %copy-start.4 = (bf16[1280,256]{1,0:T(8,128)(2,1)S(1)}, bf16[1280,256]{1,0:T(8,128)(2,1)}, u32[]{:S(2)}) copy-start(bf16[1280,256]{1,0:T(8,128)(2,1)} %keys_hbm.1) | copy-start | bytes 1966084
  8.5 4.9 %copy-start.1 = (f32[256,2048]{1,0:T(8,128)}, f32[256,2048]{1,0:T(8,128)S(1)}, u32[]{:S(2)}) copy-start(f32[256,2048]{1,0:T(8,128)S(1)} %get-tuple-element.18.logits) | copy-start | bytes 6291460
  8.5 4.9 %collective-permute-start = (bf16[256,768]{1,0:T(8,128)(2,1)S(1)}, bf16[256,768]{1,0:T(8,128)(2,1)S(1)}, u32[]{:S(2)}, u32[]{:S(2)}) collective-permute-start(bf16[256,768]{1,0:T(8,128)(2,1)S(1)} %get-tuple-element.22), channel_id=1, source_target_pairs={{0,32},{32,0},{64,96},{96,64},{128,160},{160,128},{192,224},{224,1... | collective-permute-start | bytes 1179656 | tf_op jit(solution)/shard_map/ppermute | solution.py:246
  13.4 29.5 %copy-start.5 = (bf16[1,1280,640]{2,1,0:T(8,128)(2,1)S(1)}, bf16[1,1280,640]{2,1,0:T(8,128)(2,1)}, u32[]{:S(2)}) copy-start(bf16[1,1280,640]{2,1,0:T(8,128)(2,1)} %param.6) | copy-start | bytes 4915204
  14.8 6.0 %collective-permute-start.1 = (bf16[64,768]{1,0:T(8,128)(2,1)S(1)}, bf16[64,768]{1,0:T(8,128)(2,1)S(1)}, u32[]{:S(2)}, u32[]{:S(2)}) collective-permute-start(bf16[64,768]{1,0:T(8,128)(2,1)S(1)} %get-tuple-element.24), channel_id=1, source_target_pairs={{0,8},{2,10},{4,12},{6,14},{8,16},{10,18},{12,20},{14,22},{16,24},... | collective-permute-start | bytes 294920 | tf_op jit(solution)/shard_map/ppermute | solution.py:269
  14.9 7.1 %collective-permute-start.2 = (bf16[64,768]{1,0:T(8,128)(2,1)S(1)}, bf16[64,768]{1,0:T(8,128)(2,1)S(1)}, u32[]{:S(2)}, u32[]{:S(2)}) collective-permute-start(bf16[64,768]{1,0:T(8,128)(2,1)S(1)} %get-tuple-element.25), channel_id=1, source_target_pairs={{0,16},{2,18},{4,20},{6,22},{8,24},{10,26},{12,28},{14,30},{16,0},... | collective-permute-start | bytes 294920 | tf_op jit(solution)/shard_map/ppermute | solution.py:269
  17.0 5.6 %collective-permute-start.3 = (bf16[64,768]{1,0:T(8,128)(2,1)S(1)}, bf16[64,768]{1,0:T(8,128)(2,1)S(1)}, u32[]{:S(2)}, u32[]{:S(2)}) collective-permute-start(bf16[64,768]{1,0:T(8,128)(2,1)S(1)} %get-tuple-element.26), channel_id=1, source_target_pairs={{0,24},{2,26},{4,28},{6,30},{8,0},{10,2},{12,4},{14,6},{16,8},{18,... | collective-permute-start | bytes 294920 | tf_op jit(solution)/shard_map/ppermute | solution.py:269
  23.6 5.2 %collective-permute-start.4 = (f32[16,768]{1,0:T(8,128)S(1)}, f32[16,768]{1,0:T(8,128)S(1)}, u32[]{:S(2)}, u32[]{:S(2)}) collective-permute-start(f32[16,768]{1,0:T(8,128)S(1)} %get-tuple-element.28), channel_id=1, source_target_pairs={{0,2},{2,4},{4,6},{6,0},{8,10},{10,12},{12,14},{14,8},{16,18},{18,... | collective-permute-start | bytes 147464 | tf_op jit(solution)/shard_map/ppermute | solution.py:278
  24.5 4.7 %collective-permute-start.5 = (f32[16,768]{1,0:T(8,128)S(1)}, f32[16,768]{1,0:T(8,128)S(1)}, u32[]{:S(2)}, u32[]{:S(2)}) collective-permute-start(f32[16,768]{1,0:T(8,128)S(1)} %get-tuple-element.29), channel_id=1, source_target_pairs={{0,4},{2,6},{4,0},{6,2},{8,12},{10,14},{12,8},{14,10},{16,20},{18,... | collective-permute-start | bytes 147464 | tf_op jit(solution)/shard_map/ppermute | solution.py:278
  27.5 3.9 %collective-permute-start.6 = (f32[16,768]{1,0:T(8,128)S(1)}, f32[16,768]{1,0:T(8,128)S(1)}, u32[]{:S(2)}, u32[]{:S(2)}) collective-permute-start(f32[16,768]{1,0:T(8,128)S(1)} %get-tuple-element.30), channel_id=1, source_target_pairs={{0,6},{2,0},{4,2},{6,4},{8,14},{10,8},{12,10},{14,12},{16,22},{18,... | collective-permute-start | bytes 147464 | tf_op jit(solution)/shard_map/ppermute | solution.py:278
  31.6 4.8 %collective-permute-start.7 = (f32[16,768]{1,0:T(8,128)S(1)}, f32[16,768]{1,0:T(8,128)S(1)}, u32[]{:S(2)}, u32[]{:S(2)}) collective-permute-start(f32[16,768]{1,0:T(8,128)S(1)} %z_merge.1.own), channel_id=1, source_target_pairs={{0,64},{32,96},{64,128},{96,160},{128,192},{160,224},{192,0},{224,... | collective-permute-start | bytes 147464 | tf_op jit(solution)/shard_map/ppermute | solution.py:283
  32.8 4.4 %collective-permute-start.8 = (f32[16,768]{1,0:T(8,128)S(1)}, f32[16,768]{1,0:T(8,128)S(1)}, u32[]{:S(2)}, u32[]{:S(2)}) collective-permute-start(f32[16,768]{1,0:T(8,128)S(1)} %z_merge.1.own), channel_id=1, source_target_pairs={{0,128},{32,160},{64,192},{96,224},{128,0},{160,32},{192,64},{224,... | collective-permute-start | bytes 147464 | tf_op jit(solution)/shard_map/ppermute | solution.py:283
  35.2 3.0 %collective-permute-start.9 = (f32[16,768]{1,0:T(8,128)S(1)}, f32[16,768]{1,0:T(8,128)S(1)}, u32[]{:S(2)}, u32[]{:S(2)}) collective-permute-start(f32[16,768]{1,0:T(8,128)S(1)} %z_merge.1.own), channel_id=1, source_target_pairs={{0,192},{32,224},{64,0},{96,32},{128,64},{160,96},{192,128},{224,1... | collective-permute-start | bytes 147464 | tf_op jit(solution)/shard_map/ppermute | solution.py:283
  38.4 4.5 %collective-permute-start.10 = (bf16[16,640]{1,0:T(8,128)(2,1)S(1)}, bf16[16,640]{1,0:T(8,128)(2,1)S(1)}, u32[]{:S(2)}, u32[]{:S(2)}) collective-permute-start(bf16[16,640]{1,0:T(8,128)(2,1)S(1)} %x_merge.1), channel_id=1, source_target_pairs={{0,32},{32,0},{64,96},{96,64},{128,160},{160,128},{192,224},{224,1... | collective-permute-start | bytes 61448 | tf_op jit(solution)/shard_map/ppermute | solution.py:287
  43.6 1.2 %collective-permute-start.11 = (f32[16,640]{1,0:T(8,128)S(1)}, f32[16,640]{1,0:T(8,128)S(1)}, u32[]{:S(2)}, u32[]{:S(2)}) collective-permute-start(f32[16,640]{1,0:T(8,128)S(1)} %constant_dynamic-slice_fusion), channel_id=1, source_target_pairs={{0,32},{32,0},{64,96},{96,64},{128,160},{160,128},{192,224},{224,1... | collective-permute-start | bytes 122888 | tf_op jit(solution)/shard_map/ppermute | solution.py:299
  44.8 4.1 %collective-permute-start.12 = (f32[16,640]{1,0:T(8,128)S(1)}, f32[16,640]{1,0:T(8,128)S(1)}, u32[]{:S(2)}, u32[]{:S(2)}) collective-permute-start(f32[16,640]{1,0:T(8,128)S(1)} %dynamic-slice_add_fusion), channel_id=1, source_target_pairs={{0,64},{32,96},{64,128},{96,160},{128,192},{160,224},{192,0},{224,... | collective-permute-start | bytes 122888 | tf_op jit(solution)/shard_map/ppermute | solution.py:300
  45.0 5.3 %collective-permute-start.13 = (f32[16,640]{1,0:T(8,128)S(1)}, f32[16,640]{1,0:T(8,128)S(1)}, u32[]{:S(2)}, u32[]{:S(2)}) collective-permute-start(f32[16,640]{1,0:T(8,128)S(1)} %dynamic-slice_add_fusion), channel_id=1, source_target_pairs={{0,128},{32,160},{64,192},{96,224},{128,0},{160,32},{192,64},{224,... | collective-permute-start | bytes 122888 | tf_op jit(solution)/shard_map/ppermute | solution.py:300
  48.5 3.0 %collective-permute-start.14 = (f32[16,640]{1,0:T(8,128)S(1)}, f32[16,640]{1,0:T(8,128)S(1)}, u32[]{:S(2)}, u32[]{:S(2)}) collective-permute-start(f32[16,640]{1,0:T(8,128)S(1)} %dynamic-slice_add_fusion), channel_id=1, source_target_pairs={{0,192},{32,224},{64,0},{96,32},{128,64},{160,96},{192,128},{224,1... | collective-permute-start | bytes 122888 | tf_op jit(solution)/shard_map/ppermute | solution.py:300
  51.5 4.5 %collective-permute-start.15 = (bf16[16,640]{1,0:T(8,128)(2,1)S(1)}, bf16[16,640]{1,0:T(8,128)(2,1)S(1)}, u32[]{:S(2)}, u32[]{:S(2)}) collective-permute-start(bf16[16,640]{1,0:T(8,128)(2,1)S(1)} %get-tuple-element.32), channel_id=1, source_target_pairs={{0,2},{2,4},{4,6},{6,0},{8,10},{10,12},{12,14},{14,8},{16,18},{18,... | collective-permute-start | bytes 61448 | tf_op jit(solution)/shard_map/ppermute | solution.py:306
  51.8 4.2 %collective-permute-start.16 = (bf16[16,640]{1,0:T(8,128)(2,1)S(1)}, bf16[16,640]{1,0:T(8,128)(2,1)S(1)}, u32[]{:S(2)}, u32[]{:S(2)}) collective-permute-start(bf16[16,640]{1,0:T(8,128)(2,1)S(1)} %get-tuple-element.32), channel_id=1, source_target_pairs={{0,4},{2,6},{4,0},{6,2},{8,12},{10,14},{12,8},{14,10},{16,20},{18,... | collective-permute-start | bytes 61448 | tf_op jit(solution)/shard_map/ppermute | solution.py:306
  54.4 2.6 %collective-permute-start.17 = (bf16[16,640]{1,0:T(8,128)(2,1)S(1)}, bf16[16,640]{1,0:T(8,128)(2,1)S(1)}, u32[]{:S(2)}, u32[]{:S(2)}) collective-permute-start(bf16[16,640]{1,0:T(8,128)(2,1)S(1)} %get-tuple-element.32), channel_id=1, source_target_pairs={{0,6},{2,0},{4,2},{6,4},{8,14},{10,8},{12,10},{14,12},{16,22},{18,... | collective-permute-start | bytes 61448 | tf_op jit(solution)/shard_map/ppermute | solution.py:306
  57.0 4.5 %collective-permute-start.18 = (bf16[64,640]{1,0:T(8,128)(2,1)S(1)}, bf16[64,640]{1,0:T(8,128)(2,1)S(1)}, u32[]{:S(2)}, u32[]{:S(2)}) collective-permute-start(bf16[64,640]{1,0:T(8,128)(2,1)S(1)} %constant_dynamic-update-slice_fusion.4), channel_id=1, source_target_pairs={{0,8},{2,10},{4,12},{6,14},{8,16},{10,18},{12,20},{14,22},{16,24},... | collective-permute-start | bytes 245768 | tf_op jit(solution)/shard_map/ppermute | solution.py:306
  58.0 4.8 %collective-permute-start.19 = (bf16[64,640]{1,0:T(8,128)(2,1)S(1)}, bf16[64,640]{1,0:T(8,128)(2,1)S(1)}, u32[]{:S(2)}, u32[]{:S(2)}) collective-permute-start(bf16[64,640]{1,0:T(8,128)(2,1)S(1)} %constant_dynamic-update-slice_fusion.4), channel_id=1, source_target_pairs={{0,16},{2,18},{4,20},{6,22},{8,24},{10,26},{12,28},{14,30},{16,0},... | collective-permute-start | bytes 245768 | tf_op jit(solution)/shard_map/ppermute | solution.py:306
  60.1 3.3 %collective-permute-start.20 = (bf16[64,640]{1,0:T(8,128)(2,1)S(1)}, bf16[64,640]{1,0:T(8,128)(2,1)S(1)}, u32[]{:S(2)}, u32[]{:S(2)}) collective-permute-start(bf16[64,640]{1,0:T(8,128)(2,1)S(1)} %constant_dynamic-update-slice_fusion.4), channel_id=1, source_target_pairs={{0,24},{2,26},{4,28},{6,30},{8,0},{10,2},{12,4},{14,6},{16,8},{18,... | collective-permute-start | bytes 245768 | tf_op jit(solution)/shard_map/ppermute | solution.py:306
  63.4 7.7 %collective-permute-start.21 = (bf16[256,640]{1,0:T(8,128)(2,1)S(1)}, bf16[256,640]{1,0:T(8,128)(2,1)S(1)}, u32[]{:S(2)}, u32[]{:S(2)}) collective-permute-start(bf16[256,640]{1,0:T(8,128)(2,1)S(1)} %constant_dynamic-update-slice_fusion.own), channel_id=1, source_target_pairs={{0,32},{32,0},{64,96},{96,64},{128,160},{160,128},{192,224},{224,1... | collective-permute-start | bytes 983048 | tf_op jit(solution)/shard_map/ppermute | solution.py:313
  68.8 1.6 %copy-start.2 = (f32[256,2048]{1,0:T(8,128)S(1)}, f32[256,2048]{1,0:T(8,128)}, u32[]{:S(2)}) copy-start(f32[256,2048]{1,0:T(8,128)} %copy-done.1) | copy-start | bytes 6291460

commit v3 on v2

v3 whole, which is shorter than its diff:
```python
import functools

import jax
import jax.numpy as jnp
from jax import lax
from jax.experimental import pallas as pl
from jax.experimental.pallas import tpu as pltpu
from jax.sharding import PartitionSpec as P

F32 = jnp.float32
BF16 = jnp.bfloat16
LANES = 128
VMEM = pl.BlockSpec(memory_space=pltpu.VMEM)
SMEM = pl.BlockSpec(memory_space=pltpu.SMEM)
ANY = pl.BlockSpec(memory_space=pl.ANY)


def _core_perm():
    return [(s, s ^ 1) for s in range(8)]


def _x_perm(k):
    return [(s, ((s // 2 + k) % 4) * 2 + s % 2) for s in range(8)]


def _y_perm(k):
    return [(e, ((e // 4 + k) % 4) * 4 + e % 4) for e in range(16)]


def _z_perm(k):
    return [(e, (e // 4) * 4 + (e % 4 + k) % 4) for e in range(16)]


def _call(kernel, name, out_shape, in_specs, scratch=(), out_specs=None, vmem=6, flops=0, bytes_accessed=0, **kw):
    many = isinstance(out_shape, list)
    if out_specs is None:
        out_specs = [VMEM] * len(out_shape) if many else VMEM
    return pl.pallas_call(
        kernel,
        in_specs=in_specs,
        out_specs=out_specs,
        out_shape=out_shape,
        scratch_shapes=list(scratch),
        compiler_params=pltpu.CompilerParams(vmem_limit_bytes=vmem << 20),
        cost_estimate=pl.CostEstimate(flops=flops, bytes_accessed=bytes_accessed, transcendentals=0),
        name=name,
        **kw,
    )


def _lane(n):
    return lax.broadcasted_iota(jnp.int32, (n, LANES), 1)


def _wide(v):
    return jnp.broadcast_to(v, (v.shape[0], LANES))


def _pieces(peak, total):
    lane = _lane(peak.shape[0])
    st = jnp.zeros(peak.shape, F32)
    j = 0
    for v in (peak, total):
        for _ in range(3):
            p = v.astype(BF16).astype(F32)
            st = jnp.where(lane == j, p, st)
            v = v - p
            j += 1
    return st.astype(BF16)


def _unpieces(st):
    row = lax.broadcasted_iota(jnp.int32, (LANES, 2 * LANES), 0)
    column = lax.broadcasted_iota(jnp.int32, (LANES, 2 * LANES), 1)
    first = jnp.where(column < LANES, 0, 3)
    pick = jnp.where((row >= first) & (row < first + 3), 1.0, 0.0).astype(BF16)
    both = jnp.dot(st, pick, preferred_element_type=F32)
    return both[:, :LANES], both[:, LANES:]


def _pair(peak, total):
    lane = _lane(peak.shape[0])
    return jnp.where(lane == 0, peak, jnp.where(lane == 1, total, 0.0))


def _unpair(st):
    return _wide(st[:, 0:1]), _wide(st[:, 1:2])


def _times(v, scale):
    return jnp.concatenate(
        [v[:, j : j + LANES] * scale for j in range(0, v.shape[1], LANES)], axis=1
    )


def _merge(parts):
    peak = parts[0][1]
    for _, p, _ in parts[1:]:
        peak = jnp.maximum(peak, p)
    sums, total = None, None
    for s, p, t in parts:
        a = jnp.exp(p - peak)
        sums = _times(s, a) if sums is None else sums + _times(s, a)
        total = t * a if total is None else total + t * a
    return sums, peak, total


def _fold(v, op):
    out = v[:, :LANES]
    for j in range(1, v.shape[1] // LANES):
        out = op(out, v[:, j * LANES : (j + 1) * LANES])
    return out


def first_kernel(chunks, where, tok_hbm, keys_hbm, tok, logits, dispatch, packed, stat, keys, acc, sem):
    tokens, width = tok.shape
    half = width // 2
    step = tokens // chunks
    keys_copy = pltpu.make_async_copy(keys_hbm, keys, sem.at[chunks])
    keys_copy.start()
    copies = [
        pltpu.make_async_copy(
            tok_hbm.at[pl.ds(i * step, step)], tok.at[pl.ds(i * step, step)], sem.at[i]
        )
        for i in range(chunks)
    ]
    for c in copies:
        c.start()
    other = pl.multiple_of((1 - where[0]) * half, LANES)
    keys_copy.wait()
    keys_t = keys[...].T

    def weigh(i):
        return jnp.dot(
            dispatch[:, i * step : (i + 1) * step],
            tok[i * step : (i + 1) * step, pl.ds(other, half)],
            preferred_element_type=F32,
        )

    peaks, total = [], None
    for i in range(chunks):
        copies[i].wait()
        part = lax.dot_general(
            keys_t,
            tok[i * step : (i + 1) * step, :],
            (((1,), (1,)), ((), ())),
            preferred_element_type=F32,
        )
        logits[:, i * step : (i + 1) * step] = part
        peak = _wide(jnp.max(_fold(part, jnp.maximum), axis=1, keepdims=True))
        if i:
            peak = jnp.maximum(peak, peaks[-1])
        e = jnp.concatenate(
            [jnp.exp(part[:, j : j + LANES] - peak) for j in range(0, step, LANES)], axis=1
        )
        if i == 1:
            acc[...] = _times(weigh(0), jnp.exp(peaks[0] - peak))
        elif i > 1:
            acc[...] = _times(acc[...] + weigh(i - 1), jnp.exp(peaks[-1] - peak))
        dispatch[:, i * step : (i + 1) * step] = e.astype(BF16)
        add = _fold(e, jnp.add)
        total = add if i == 0 else total * jnp.exp(peaks[-1] - peak) + add
        peaks.append(peak)
    total = _wide(jnp.sum(total, axis=1, keepdims=True))
    sums = acc[...] + weigh(chunks - 1)
    packed[:, :half] = sums.astype(BF16)
    packed[:, half:] = _pieces(peak, total)
    stat[:, :LANES] = peak
    stat[:, LANES : 2 * LANES] = total
    for i in range(chunks):
        stat[:, (2 + i) * LANES : (3 + i) * LANES] = jnp.exp(peaks[i] - peak)


def own_kernel(chunks, where, tok, dispatch, stat, own):
    half = tok.shape[1] // 2
    step = tok.shape[0] // chunks
    off = pl.multiple_of(where[0] * half, LANES)
    sums = None
    for i in range(chunks):
        part = _times(
            jnp.dot(
                dispatch[:, i * step : (i + 1) * step],
                tok[i * step : (i + 1) * step, pl.ds(off, half)],
                preferred_element_type=F32,
            ),
            stat[:, (2 + i) * LANES : (3 + i) * LANES],
        )
        sums = part if sums is None else sums + part
    own[...] = sums


def combine_kernel(after, logits, w_in_hbm, w_out_hbm, combine, w_in, w_out, sem):
    copies = [
        pltpu.make_async_copy(w_in_hbm, w_in, sem.at[0]),
        pltpu.make_async_copy(w_out_hbm, w_out, sem.at[1]),
    ]
    for c in copies:
        c.start()
    v = logits[...]
    e = jnp.exp(v - jnp.max(v, axis=0, keepdims=True))
    combine[...] = (e / jnp.sum(e, axis=0, keepdims=True)).astype(BF16).T
    for c in copies:
        c.wait()


def expert_kernel(where, slot_own, slot_other, w_in, w_out, own, send):
    half = slot_own.shape[1]
    mine = pl.multiple_of(where[0] * half, LANES)
    other = pl.multiple_of((1 - where[0]) * half, LANES)
    hidden = jnp.dot(slot_own[...], w_in[pl.ds(mine, half), :], preferred_element_type=F32)
    hidden += jnp.dot(slot_other[...], w_in[pl.ds(other, half), :], preferred_element_type=F32)
    hidden = jax.nn.gelu(hidden).astype(BF16)
    send[...] = jnp.dot(hidden, w_out[:, pl.ds(other, half)], preferred_element_type=F32)
    own[...] = jnp.dot(hidden, w_out[:, pl.ds(mine, half)], preferred_element_type=F32)


def core_merge_kernel(where, own, stat, got, keep, keep_stat, send1, send2, send3):
    rows, half = keep.shape
    for k, ref in enumerate((keep, send1, send2, send3)):
        part = pl.ds(pl.multiple_of(lax.rem(where[1] + k, 4) * rows, rows), rows)
        sums, peak, total = _merge(
            [
                (own[part, :], stat[part, :LANES], stat[part, LANES : 2 * LANES]),
                (got[part, :half].astype(F32), *_unpieces(got[part, half:])),
            ]
        )
        ref[:, :half] = sums.astype(ref.dtype)
        if k == 0:
            keep_stat[:, :LANES] = peak
            keep_stat[:, LANES:] = total
        else:
            ref[:, half:] = _pieces(peak, total)


def y_merge_kernel(where, after, own, stat, got1, got2, got3, keep, send1, send2, send3):
    rows, half = keep.shape[0], own.shape[1]
    for k, ref in enumerate((keep, send1, send2, send3)):
        part = pl.ds(pl.multiple_of(lax.rem(where[2] + k, 4) * rows, rows), rows)
        sums, peak, total = _merge(
            [(own[part, :], stat[part, :LANES], stat[part, LANES:])]
            + [
                (g[part, :half].astype(F32), *_unpieces(g[part, half:]))
                for g in (got1, got2, got3)
            ]
        )
        ref[:, :half] = sums
        ref[:, half:] = _pair(peak, total)


def z_merge_kernel(own, got1, got2, got3, out):
    half = own.shape[1] - LANES
    sums, peak, total = _merge(
        [(g[:, :half], *_unpair(g[:, half:])) for g in (own, got1, got2, got3)]
    )
    out[:, :half] = sums
    out[:, half:] = _pair(peak, total)


def x_merge_kernel(own, got1, got2, got3, out):
    half = own.shape[1] - LANES
    sums, _, total = _merge(
        [(g[:, :half], *_unpair(g[:, half:])) for g in (own, got1, got2, got3)]
    )
    out[...] = (sums / _wide_as(total, half)).astype(BF16)


def _wide_as(v, width):
    return jnp.concatenate([v] * (width // LANES), axis=1)


def mix_kernel(chunks, own, where, combine, slot_out, *refs):
    out_hbm, buf, sem = refs[-3:]
    half = slot_out.shape[1]
    step = combine.shape[0] // chunks
    column = pl.multiple_of((where[0] if own else 1 - where[0]) * half, LANES)
    copies = []
    for i in range(chunks):
        buf[i] = jnp.dot(
            combine[i * step : (i + 1) * step, :], slot_out[...], preferred_element_type=F32
        ).astype(BF16)
        c = pltpu.make_async_copy(
            buf.at[i], out_hbm.at[pl.ds(i * step, step), pl.ds(column, half)], sem.at[i]
        )
        c.start()
        copies.append(c)
    for c in copies:
        c.wait()


def body(tokens, slot_keys, w_in, w_out):
    seq, exp = lax.axis_index("seq"), lax.axis_index("exp")
    y, z = exp // 4, exp % 4
    where = jnp.stack([seq % 2, y, z]).astype(jnp.int32)

    tok, logits, dispatch, packed, stat = first(where, tokens, slot_keys)
    got = lax.ppermute(packed, "seq", _core_perm())
    own = own_sums(where, tok, dispatch, stat)

    own, stat, *send = core_merge(where, own, stat, got)
    got = [lax.ppermute(v, "exp", _y_perm(k + 1)) for k, v in enumerate(send)]
    combine, w_in, w_out = combine_weights(own, logits, w_in[0], w_out[0])
    own, *send = y_merge(where, combine, own, stat, *got)
    got = [lax.ppermute(v, "exp", _z_perm(k + 1)) for k, v in enumerate(send)]
    own = z_merge(own, *got)
    got = [lax.ppermute(own, "seq", _x_perm(k)) for k in range(1, 4)]
    slot_half = x_merge(own, *got)
    got = lax.ppermute(slot_half, "seq", _core_perm())
    mine, other = expert(where, slot_half, got, w_in, w_out)
    part = mine + lax.ppermute(other, "seq", _core_perm())
    whole = part + sum(lax.ppermute(part, "seq", _x_perm(k)) for k in range(1, 4))
    out = whole.astype(BF16)

    def gather(block, index, perm):
        n = block.shape[0]
        res = jnp.zeros((4 * n, block.shape[1]), block.dtype)
        blocks = [block] + [lax.ppermute(block, "exp", perm(k)) for k in range(1, 4)]
        for k, g in enumerate(blocks):
            res = lax.dynamic_update_slice_in_dim(res, g, ((index - k) % 4) * n, 0)
        return res

    out = gather(out, z, _z_perm)
    out = gather(out, y, _y_perm)
    other = lax.ppermute(out, "seq", _core_perm())
    mixed = mix(where, combine, out)
    return mix(where, combine, other, mixed)


CHUNKS = 4


def first(where, tokens, slot_keys):
    count, width = tokens.shape
    slots = slot_keys.shape[1]
    half = width // 2
    return _call(
        functools.partial(first_kernel, CHUNKS),
        "logits_and_sums",
        [
            pltpu.VMEM((count, width), BF16),
            pltpu.VMEM((slots, count), F32),
            pltpu.VMEM((slots, count), BF16),
            pltpu.VMEM((slots, half + LANES), BF16),
            pltpu.VMEM((slots, (2 + CHUNKS) * LANES), F32),
        ],
        [SMEM, ANY, ANY],
        [
            pltpu.VMEM((width, slots), BF16),
            pltpu.VMEM((slots, half), F32),
            pltpu.SemaphoreType.DMA((CHUNKS + 1,)),
        ],
        vmem=16,
        flops=3 * count * slots * width,
        bytes_accessed=2 * count * width,
    )(where, *(pltpu.with_memory_space_constraint(v, pltpu.HBM) for v in (tokens, slot_keys)))


def own_sums(where, tok, dispatch, stat):
    return _call(
        functools.partial(own_kernel, CHUNKS),
        "own_sums",
        pltpu.VMEM((stat.shape[0], tok.shape[1] // 2), F32),
        [SMEM, VMEM, VMEM, VMEM],
        vmem=12,
        flops=dispatch.size * tok.shape[1],
    )(where, tok, dispatch, stat)


def combine_weights(after, logits, w_in, w_out):
    slots, count = logits.shape
    return _call(
        combine_kernel,
        "combine",
        [
            pltpu.VMEM((count, slots), BF16),
            pltpu.VMEM(w_in.shape, BF16),
            pltpu.VMEM(w_out.shape, BF16),
        ],
        [ANY, VMEM, ANY, ANY],
        [pltpu.SemaphoreType.DMA((2,))],
        vmem=12,
        flops=10 * count * slots,
        bytes_accessed=4 * w_in.size,
    )(after, logits, *(pltpu.with_memory_space_constraint(v, pltpu.HBM) for v in (w_in, w_out)))


def expert(where, slot_own, slot_other, w_in, w_out):
    return _call(
        expert_kernel,
        "expert",
        [pltpu.VMEM(slot_own.shape, F32)] * 2,
        [SMEM] + [VMEM] * 4,
        flops=4 * slot_own.shape[0] * w_in.size,
    )(where, slot_own, slot_other, w_in, w_out)


def core_merge(where, own, stat, got):
    rows, half = own.shape[0] // 4, own.shape[1]
    return _call(
        core_merge_kernel,
        "core_merge",
        [pltpu.VMEM((rows, half), F32), pltpu.VMEM((rows, 2 * LANES), F32)]
        + [pltpu.VMEM((rows, half + LANES), BF16)] * 3,
        [SMEM] + [VMEM] * 3,
    )(where, own, stat, got)


def y_merge(where, after, own, stat, *got):
    rows, half = own.shape[0] // 4, own.shape[1]
    return _call(
        y_merge_kernel,
        "y_merge",
        [pltpu.VMEM((rows, half + LANES), F32)] * 4,
        [SMEM, ANY] + [VMEM] * 5,
    )(where, after, own, stat, *got)


def z_merge(own, *got):
    return _call(z_merge_kernel, "z_merge", pltpu.VMEM(own.shape, F32), [VMEM] * 4)(own, *got)


def x_merge(own, *got):
    out = pltpu.VMEM((own.shape[0], own.shape[1] - LANES), BF16)
    return _call(x_merge_kernel, "x_merge", out, [VMEM] * 4)(own, *got)


def mix(where, combine, slot_out, *mixed):
    count, slots = combine.shape
    half = slot_out.shape[1]
    steps = 8
    return _call(
        functools.partial(mix_kernel, steps, not mixed),
        "mix",
        jax.ShapeDtypeStruct((count, 2 * half), BF16),
        [SMEM, VMEM, VMEM] + [ANY] * len(mixed),
        [pltpu.VMEM((steps, count // steps, half), BF16), pltpu.SemaphoreType.DMA((steps,))],
        out_specs=ANY,
        vmem=12,
        flops=2 * count * slots * half,
        bytes_accessed=2 * count * half,
        input_output_aliases={3: 0} if mixed else {},
    )(where, combine, slot_out, *mixed)


def solution(mesh):
    return jax.shard_map(
        body,
        mesh=mesh,
        in_specs=(P(("dp", "seq", "exp"), None), P(), P("exp", None, "seq"), P("exp", "seq", None)),
        out_specs=P(("dp", "seq", "exp"), None),
        check_vma=False,
    )
```

time: 75.6 us -> 71 us (0.939)
  local copies, waits for them, and re-layouts: 5.42 us -> 0.14 us
  starting transfers between devices: 36.9 us -> 32.3 us
  Pallas kernels: 13.6 us -> 16.7 us
  waiting for transfers between devices: 18.3 us -> 21.4 us
    unnamed x12 -> x0, local copies, waits for them, and re-layouts: 5.29 us -> none
    pallas_call x8 -> x10, Pallas kernels: 13.6 us -> 16.7 us  [the longest x1 5.34 us: first(): _call(functools.partial(first_kernel, CHUNKS), 'logits_and_sums', [pltpu....]
    ppermute x6, waiting for transfers between devices: 4.06 us -> 6.45 us  [gather(): lax.ppermute(block, 'exp', perm(k))]
    ppermute x3, waiting for transfers between devices: 1.87 us -> 3.85 us  [body(): got = [lax.ppermute(own, 'seq', _x_perm(k)) for k in range(1, 4)]]
    ppermute x3, waiting for transfers between devices: 4.57 us -> 2.71 us  [body(): got = [lax.ppermute(v, 'exp', _y_perm(k + 1)) for k, v in enumerate(send)]]
    ppermute x3, starting transfers between devices: 3.62 us -> 2.08 us  [body(): lax.ppermute(part, 'seq', _x_perm(k))]
    ppermute x3, starting transfers between devices: 4.81 us -> 3.59 us  [body(): got = [lax.ppermute(own, 'seq', _x_perm(k)) for k in range(1, 4)]]
    ppermute x6, starting transfers between devices: 7.71 us -> 6.5 us  [gather(): lax.ppermute(block, 'exp', perm(k))]
  transfers between devices with their start and end apart: 22 -> 22, of which waited for: 18 -> 17; matrix products, arithmetic and copies ran while one was open for 0% -> 0% of each run, Pallas kernels for 3% -> 8%
where the time goes in v3:
time: 71 us
  starting transfers between devices  32.3 us (45%)
  waiting for transfers between devices  21.4 us (30%)
  Pallas kernels  16.7 us (24%)
    ppermute x6, starting transfers between devices, gather(): lax.ppermute(block, 'exp', perm(k))  6.5 us
    ppermute x6, waiting for transfers between devices, gather(): lax.ppermute(block, 'exp', perm(k))  6.45 us
    pallas_call x1, Pallas kernels, first(): _call(functools.partial(first_kernel, CHUNKS), 'logits_and_sums', [pltpu....  5.34 us
    ppermute x1, starting transfers between devices, body(): other = lax.ppermute(out, 'seq', _core_perm())  4.83 us
    pallas_call x2, Pallas kernels, mix(): _call(functools.partial(mix_kernel, steps, not mixed), 'mix', jax.ShapeDt...  4.79 us
    ppermute x3, starting transfers between devices, body(): got = [lax.ppermute(v, 'exp', _z_perm(k + 1)) for k, v in enumerate(send)]  4.68 us
    ppermute x3, waiting for transfers between devices, body(): got = [lax.ppermute(own, 'seq', _x_perm(k)) for k in range(1, 4)]  3.85 us
    ppermute x3, waiting for transfers between devices, body(): lax.ppermute(part, 'seq', _x_perm(k))  3.6 us
  transfers between devices with their start and end apart: 22, of which 17 were waited for; matrix products, arithmetic and copies ran while one was open for 0% of the time, Pallas kernels for 8%

profile of v3, /device:TPU:1, one launch (start us, length us, event | category | flops | bytes accessed | tf_op | source)
XLA Modules:
  0.0 71.0 jit_solution(10165163422552182237)
XLA Ops:
  0.1 5.3 %logits_and_sums.1 = (bf16[2048,1280]{1,0:T(8,128)(2,1)S(1)}, f32[256,2048]{1,0:T(8,128)S(1)}, bf16[256,2048]{1,0:T(8,128)(2,1)S(1)}, bf16[256,768]{1,0:T(8,128)(2,1)S(1)}, f32[256,768]{1,0:T(8,128)S(1)}) custom-call(s32[3]{0:T(128)S(1)} %pad_add_fusion.where, bf16[2048,1280]{1,0:T(8,128)(2,1)} %tok_hbm.1, bf16[1280,256]{1,0:T(8,128)(2,1)} %keys_hbm.1), custom_call_target="tpu_custom_call" | custom-call | flops 2013265920 | bytes 5242880 | tf_op jit(solution)/shard_map/logits_and_sums/pallas_call | solution.py:335
  5.4 3.3 %collective-permute-start = (bf16[256,768]{1,0:T(8,128)(2,1)S(1)}, bf16[256,768]{1,0:T(8,128)(2,1)S(1)}, u32[]{:S(2)}, u32[]{:S(2)}) collective-permute-start(bf16[256,768]{1,0:T(8,128)(2,1)S(1)} %get-tuple-element.27), channel_id=1, source_target_pairs={{0,32},{32,0},{64,96},{96,64},{128,160},{160,128},{192,224},{224,1... | collective-permute-start | bytes 1179656 | tf_op jit(solution)/shard_map/ppermute | solution.py:296
  8.8 1.6 %own_sums.1.own = f32[256,640]{1,0:T(8,128)S(1)} custom-call(s32[3]{0:T(128)S(1)} %pad_add_fusion.where, bf16[2048,1280]{1,0:T(8,128)(2,1)S(1)} %get-tuple-element.24.tok, bf16[256,2048]{1,0:T(8,128)(2,1)S(1)} %get-tuple-element.25.dispatch, f32[256,768]{1,0:T(8,128)S(1)} %get-tuple-element.26.stat), custom_call_target="tpu_custom_call" | custom-call | flops 671088640 | tf_op jit(solution)/shard_map/own_sums/pallas_call | solution.py:358
  10.4 0.9 %core_merge.1 = (f32[64,640]{1,0:T(8,128)S(1)}, f32[64,256]{1,0:T(8,128)S(1)}, bf16[64,768]{1,0:T(8,128)(2,1)S(1)}, bf16[64,768]{1,0:T(8,128)(2,1)S(1)}, bf16[64,768]{1,0:T(8,128)(2,1)S(1)}) custom-call(s32[3]{0:T(128)S(1)} %pad_add_fusion.where, f32[256,640]{1,0:T(8,128)S(1)} %own_sums.1.own, f32[256,768]{1,0:T(8,128)S(1)} %get-tuple-element.26.stat, ...), custom_call_target="tpu_custom_call" | custom-call | tf_op jit(solution)/shard_map/core_merge/pallas_call | solution.py:398
  11.3 0.1 collective-permute-start.1
  11.4 2.2 %collective-permute-start.2 = (bf16[64,768]{1,0:T(8,128)(2,1)S(1)}, bf16[64,768]{1,0:T(8,128)(2,1)S(1)}, u32[]{:S(2)}, u32[]{:S(2)}) collective-permute-start(bf16[64,768]{1,0:T(8,128)(2,1)S(1)} %get-tuple-element.33), channel_id=1, source_target_pairs={{0,16},{2,18},{4,20},{6,22},{8,24},{10,26},{12,28},{14,30},{16,0},... | collective-permute-start | bytes 294920 | tf_op jit(solution)/shard_map/ppermute | solution.py:300
  13.6 1.1 %collective-permute-start.3 = (bf16[64,768]{1,0:T(8,128)(2,1)S(1)}, bf16[64,768]{1,0:T(8,128)(2,1)S(1)}, u32[]{:S(2)}, u32[]{:S(2)}) collective-permute-start(bf16[64,768]{1,0:T(8,128)(2,1)S(1)} %get-tuple-element.34), channel_id=1, source_target_pairs={{0,24},{2,26},{4,28},{6,30},{8,0},{10,2},{12,4},{14,6},{16,8},{18,... | collective-permute-start | bytes 294920 | tf_op jit(solution)/shard_map/ppermute | solution.py:300
  14.6 1.9 %combine.1 = (bf16[2048,256]{1,0:T(8,128)(2,1)S(1)}, bf16[1280,640]{1,0:T(8,128)(2,1)S(1)}, bf16[640,1280]{1,0:T(8,128)(2,1)S(1)}) custom-call(f32[64,640]{1,0:T(8,128)S(1)} %get-tuple-element.28.after.own, f32[256,2048]{1,0:T(8,128)S(1)} %get-tuple-element.29.logits, bf16[1280,640]{1,0:T(8,128)(2,1)} %bitcast.5, bf16[640,1280]{1,0:T(8,128)(2,1)} %bitcast.6), custom_call_target="tpu_custom_call" | custom-call | flops 5242880 | bytes 3276800 | tf_op jit(solution)/shard_map/combine/pallas_call | solution.py:370
  16.6 0.8 %collective-permute-done.1.got1 = bf16[64,768]{1,0:T(8,128)(2,1)S(1)} collective-permute-done((bf16[64,768]{1,0:T(8,128)(2,1)S(1)}, bf16[64,768]{1,0:T(8,128)(2,1)S(1)}, u32[]{:S(2)}, u32[]{:S(2)}) %collective-permute-start.1) | collective-permute-done | bytes 98336 | tf_op jit(solution)/shard_map/ppermute | solution.py:300
  17.4 1.2 %collective-permute-done.2.got2 = bf16[64,768]{1,0:T(8,128)(2,1)S(1)} collective-permute-done((bf16[64,768]{1,0:T(8,128)(2,1)S(1)}, bf16[64,768]{1,0:T(8,128)(2,1)S(1)}, u32[]{:S(2)}, u32[]{:S(2)}) %collective-permute-start.2) | collective-permute-done | bytes 98336 | tf_op jit(solution)/shard_map/ppermute | solution.py:300
  18.6 0.7 collective-permute-done.3.got3
  19.3 0.8 %y_merge.1 = (f32[16,768]{1,0:T(8,128)S(1)}, f32[16,768]{1,0:T(8,128)S(1)}, f32[16,768]{1,0:T(8,128)S(1)}, f32[16,768]{1,0:T(8,128)S(1)}) custom-call(s32[3]{0:T(128)S(1)} %pad_add_fusion.where, bf16[2048,256]{1,0:T(8,128)(2,1)S(1)} %get-tuple-element.30.after.combine, f32[64,640]{1,0:T(8,128)S(1)} %get-tuple-element.28.after.own, ...), custom_call_target="tpu_custom_call" | custom-call | tf_op jit(solution)/shard_map/y_merge/pallas_call | solution.py:409
  20.0 1.0 %collective-permute-start.4 = (f32[16,768]{1,0:T(8,128)S(1)}, f32[16,768]{1,0:T(8,128)S(1)}, u32[]{:S(2)}, u32[]{:S(2)}) collective-permute-start(f32[16,768]{1,0:T(8,128)S(1)} %get-tuple-element.36), channel_id=1, source_target_pairs={{0,2},{2,4},{4,6},{6,0},{8,10},{10,12},{12,14},{14,8},{16,18},{18,... | collective-permute-start | bytes 147464 | tf_op jit(solution)/shard_map/ppermute | solution.py:303
  21.0 3.0 %collective-permute-start.5 = (f32[16,768]{1,0:T(8,128)S(1)}, f32[16,768]{1,0:T(8,128)S(1)}, u32[]{:S(2)}, u32[]{:S(2)}) collective-permute-start(f32[16,768]{1,0:T(8,128)S(1)} %get-tuple-element.37), channel_id=1, source_target_pairs={{0,4},{2,6},{4,0},{6,2},{8,12},{10,14},{12,8},{14,10},{16,20},{18,... | collective-permute-start | bytes 147464 | tf_op jit(solution)/shard_map/ppermute | solution.py:303
  24.0 0.7 %collective-permute-start.6 = (f32[16,768]{1,0:T(8,128)S(1)}, f32[16,768]{1,0:T(8,128)S(1)}, u32[]{:S(2)}, u32[]{:S(2)}) collective-permute-start(f32[16,768]{1,0:T(8,128)S(1)} %get-tuple-element.38), channel_id=1, source_target_pairs={{0,6},{2,0},{4,2},{6,4},{8,14},{10,8},{12,10},{14,12},{16,22},{18,... | collective-permute-start | bytes 147464 | tf_op jit(solution)/shard_map/ppermute | solution.py:303
  24.7 0.5 collective-permute-done.4.got1
  25.2 0.5 collective-permute-done.5.got2
  25.7 2.1 %collective-permute-done.6.got3 = f32[16,768]{1,0:T(8,128)S(1)} collective-permute-done((f32[16,768]{1,0:T(8,128)S(1)}, f32[16,768]{1,0:T(8,128)S(1)}, u32[]{:S(2)}, u32[]{:S(2)}) %collective-permute-start.6) | collective-permute-done | bytes 49184 | tf_op jit(solution)/shard_map/ppermute | solution.py:303
  27.8 0.1 z_merge.1.own
  27.9 2.5 %collective-permute-start.9 = (f32[16,768]{1,0:T(8,128)S(1)}, f32[16,768]{1,0:T(8,128)S(1)}, u32[]{:S(2)}, u32[]{:S(2)}) collective-permute-start(f32[16,768]{1,0:T(8,128)S(1)} %z_merge.1.own), channel_id=1, source_target_pairs={{0,192},{32,224},{64,0},{96,32},{128,64},{160,96},{192,128},{224,1... | collective-permute-start | bytes 147464 | tf_op jit(solution)/shard_map/ppermute | solution.py:305
  30.4 0.5 collective-permute-start.8
  30.9 0.6 collective-permute-start.7
  31.6 3.3 %collective-permute-done.8.got2 = f32[16,768]{1,0:T(8,128)S(1)} collective-permute-done((f32[16,768]{1,0:T(8,128)S(1)}, f32[16,768]{1,0:T(8,128)S(1)}, u32[]{:S(2)}, u32[]{:S(2)}) %collective-permute-start.8) | collective-permute-done | bytes 49184 | tf_op jit(solution)/shard_map/ppermute | solution.py:305
  34.9 0.5 collective-permute-done.7.got1
  35.4 0.1 x_merge.1.slot_own
  35.5 3.5 %collective-permute-start.10 = (bf16[16,640]{1,0:T(8,128)(2,1)S(1)}, bf16[16,640]{1,0:T(8,128)(2,1)S(1)}, u32[]{:S(2)}, u32[]{:S(2)}) collective-permute-start(bf16[16,640]{1,0:T(8,128)(2,1)S(1)} %x_merge.1.slot_own), channel_id=1, source_target_pairs={{0,32},{32,0},{64,96},{96,64},{128,160},{160,128},{192,224},{224,1... | collective-permute-start | bytes 61448 | tf_op jit(solution)/shard_map/ppermute | solution.py:307
  39.0 0.8 %collective-permute-done.10.slot_other = bf16[16,640]{1,0:T(8,128)(2,1)S(1)} collective-permute-done((bf16[16,640]{1,0:T(8,128)(2,1)S(1)}, bf16[16,640]{1,0:T(8,128)(2,1)S(1)}, u32[]{:S(2)}, u32[]{:S(2)}) %collective-permute-start.10) | collective-permute-done | bytes 20512 | tf_op jit(solution)/shard_map/ppermute | solution.py:307
  39.8 1.2 %expert.1 = (f32[16,640]{1,0:T(8,128)S(1)}, f32[16,640]{1,0:T(8,128)S(1)}) custom-call(s32[3]{0:T(128)S(1)} %pad_add_fusion.where, bf16[16,640]{1,0:T(8,128)(2,1)S(1)} %x_merge.1.slot_own, bf16[16,640]{1,0:T(8,128)(2,1)S(1)} %collective-permute-done.10.slot_other, bf16[1280,640]{1,0:T(8,128)(2,1)S(1)} %get-tuple-element.39.w_in, ...), custom_call_target="tpu_custom_call" | custom-call | flops 52428800 | tf_op jit(solution)/shard_map/expert/pallas_call | solution.py:387
  41.0 0.4 collective-permute-start.11
  41.4 0.9 %collective-permute-done.11 = f32[16,640]{1,0:T(8,128)S(1)} collective-permute-done((f32[16,640]{1,0:T(8,128)S(1)}, f32[16,640]{1,0:T(8,128)S(1)}, u32[]{:S(2)}, u32[]{:S(2)}) %collective-permute-start.11) | collective-permute-done | bytes 40992 | tf_op jit(solution)/shard_map/ppermute | solution.py:309
  42.3 0.3 collective-permute-start.14
  42.6 1.0 %collective-permute-start.13 = (f32[16,640]{1,0:T(8,128)S(1)}, f32[16,640]{1,0:T(8,128)S(1)}, u32[]{:S(2)}, u32[]{:S(2)}) collective-permute-start(f32[16,640]{1,0:T(8,128)S(1)} %add.76), channel_id=1, source_target_pairs={{0,128},{32,160},{64,192},{96,224},{128,0},{160,32},{192,64},{224,... | collective-permute-start | bytes 122888 | tf_op jit(solution)/shard_map/ppermute | solution.py:310
  43.6 0.8 %collective-permute-start.12 = (f32[16,640]{1,0:T(8,128)S(1)}, f32[16,640]{1,0:T(8,128)S(1)}, u32[]{:S(2)}, u32[]{:S(2)}) collective-permute-start(f32[16,640]{1,0:T(8,128)S(1)} %add.76), channel_id=1, source_target_pairs={{0,64},{32,96},{64,128},{96,160},{128,192},{160,224},{192,0},{224,... | collective-permute-start | bytes 122888 | tf_op jit(solution)/shard_map/ppermute | solution.py:310
  44.4 0.8 %collective-permute-done.14 = f32[16,640]{1,0:T(8,128)S(1)} collective-permute-done((f32[16,640]{1,0:T(8,128)S(1)}, f32[16,640]{1,0:T(8,128)S(1)}, u32[]{:S(2)}, u32[]{:S(2)}) %collective-permute-start.14) | collective-permute-done | bytes 40992 | tf_op jit(solution)/shard_map/ppermute | solution.py:310
  45.2 1.8 %collective-permute-done.13 = f32[16,640]{1,0:T(8,128)S(1)} collective-permute-done((f32[16,640]{1,0:T(8,128)S(1)}, f32[16,640]{1,0:T(8,128)S(1)}, u32[]{:S(2)}, u32[]{:S(2)}) %collective-permute-start.13) | collective-permute-done | bytes 40992 | tf_op jit(solution)/shard_map/ppermute | solution.py:310
  47.0 1.0 %collective-permute-done.12 = f32[16,640]{1,0:T(8,128)S(1)} collective-permute-done((f32[16,640]{1,0:T(8,128)S(1)}, f32[16,640]{1,0:T(8,128)S(1)}, u32[]{:S(2)}, u32[]{:S(2)}) %collective-permute-start.12) | collective-permute-done | bytes 40992 | tf_op jit(solution)/shard_map/ppermute | solution.py:310
  48.0 0.4 collective-permute-start.15
  48.4 2.5 %collective-permute-start.16 = (bf16[16,640]{1,0:T(8,128)(2,1)S(1)}, bf16[16,640]{1,0:T(8,128)(2,1)S(1)}, u32[]{:S(2)}, u32[]{:S(2)}) collective-permute-start(bf16[16,640]{1,0:T(8,128)(2,1)S(1)} %get-tuple-element.44), channel_id=1, source_target_pairs={{0,4},{2,6},{4,0},{6,2},{8,12},{10,14},{12,8},{14,10},{16,20},{18,... | collective-permute-start | bytes 61448 | tf_op jit(solution)/shard_map/ppermute | solution.py:316
  50.9 0.5 collective-permute-start.17
  51.4 1.2 %collective-permute-done.15 = bf16[16,640]{1,0:T(8,128)(2,1)S(1)} collective-permute-done((bf16[16,640]{1,0:T(8,128)(2,1)S(1)}, bf16[16,640]{1,0:T(8,128)(2,1)S(1)}, u32[]{:S(2)}, u32[]{:S(2)}) %collective-permute-start.15) | collective-permute-done | bytes 20512 | tf_op jit(solution)/shard_map/ppermute | solution.py:316
  52.6 1.0 %collective-permute-done.17 = bf16[16,640]{1,0:T(8,128)(2,1)S(1)} collective-permute-done((bf16[16,640]{1,0:T(8,128)(2,1)S(1)}, bf16[16,640]{1,0:T(8,128)(2,1)S(1)}, u32[]{:S(2)}, u32[]{:S(2)}) %collective-permute-start.17) | collective-permute-done | bytes 20512 | tf_op jit(solution)/shard_map/ppermute | solution.py:316
  53.5 1.9 %collective-permute-start.20 = (bf16[64,640]{1,0:T(8,128)(2,1)S(1)}, bf16[64,640]{1,0:T(8,128)(2,1)S(1)}, u32[]{:S(2)}, u32[]{:S(2)}) collective-permute-start(bf16[64,640]{1,0:T(8,128)(2,1)S(1)} %constant_dynamic-update-slice_fusion.4), channel_id=1, source_target_pairs={{0,24},{2,26},{4,28},{6,30},{8,0},{10,2},{12,4},{14,6},{16,8},{18,... | collective-permute-start | bytes 245768 | tf_op jit(solution)/shard_map/ppermute | solution.py:316
  55.4 0.9 %collective-permute-start.19 = (bf16[64,640]{1,0:T(8,128)(2,1)S(1)}, bf16[64,640]{1,0:T(8,128)(2,1)S(1)}, u32[]{:S(2)}, u32[]{:S(2)}) collective-permute-start(bf16[64,640]{1,0:T(8,128)(2,1)S(1)} %constant_dynamic-update-slice_fusion.4), channel_id=1, source_target_pairs={{0,16},{2,18},{4,20},{6,22},{8,24},{10,26},{12,28},{14,30},{16,0},... | collective-permute-start | bytes 245768 | tf_op jit(solution)/shard_map/ppermute | solution.py:316
  56.3 0.4 collective-permute-start.18
  56.8 4.3 %collective-permute-done.18 = bf16[64,640]{1,0:T(8,128)(2,1)S(1)} collective-permute-done((bf16[64,640]{1,0:T(8,128)(2,1)S(1)}, bf16[64,640]{1,0:T(8,128)(2,1)S(1)}, u32[]{:S(2)}, u32[]{:S(2)}) %collective-permute-start.18) | collective-permute-done | bytes 81952 | tf_op jit(solution)/shard_map/ppermute | solution.py:316
  61.2 4.8 %collective-permute-start.21 = (bf16[256,640]{1,0:T(8,128)(2,1)S(1)}, bf16[256,640]{1,0:T(8,128)(2,1)S(1)}, u32[]{:S(2)}, u32[]{:S(2)}) collective-permute-start(bf16[256,640]{1,0:T(8,128)(2,1)S(1)} %constant_dynamic-update-slice_fusion.slot_out), channel_id=1, source_target_pairs={{0,32},{32,0},{64,96},{96,64},{128,160},{160,128},{192,224},{224,1... | collective-permute-start | bytes 983048 | tf_op jit(solution)/shard_map/ppermute | solution.py:323
  66.0 2.4 %mix.2.refs_0_ = bf16[2048,1280]{1,0:T(8,128)(2,1)} custom-call(s32[3]{0:T(128)S(1)} %pad_add_fusion.where, bf16[2048,256]{1,0:T(8,128)(2,1)S(1)} %get-tuple-element.30.after.combine, bf16[256,640]{1,0:T(8,128)(2,1)S(1)} %constant_dynamic-update-slice_fusion.slot_out), custom_call_target="tpu_custom_call" | custom-call | flops 671088640 | bytes 2621440 | tf_op jit(solution)/shard_map/mix/pallas_call | solution.py:430
  68.4 2.4 %mix.3 = bf16[2048,1280]{1,0:T(8,128)(2,1)} custom-call(s32[3]{0:T(128)S(1)} %pad_add_fusion.where, bf16[2048,256]{1,0:T(8,128)(2,1)S(1)} %get-tuple-element.30.after.combine, bf16[256,640]{1,0:T(8,128)(2,1)S(1)} %collective-permute-done.21.slot_out, bf16[2048,1280]{1,0:T(8,128)(2,1)} %mix.2.refs_0_), custom_call_target="tpu_custom_call", output_to_operand_aliasing={{}: (3, {})} | custom-call | flops 671088640 | bytes 2621440 | tf_op jit(solution)/shard_map/mix/pallas_call | solution.py:430
  (18 shorter events, 0.3 us)
Async XLA Ops:
  5.4 5.0 %collective-permute-start = (bf16[256,768]{1,0:T(8,128)(2,1)S(1)}, bf16[256,768]{1,0:T(8,128)(2,1)S(1)}, u32[]{:S(2)}, u32[]{:S(2)}) collective-permute-start(bf16[256,768]{1,0:T(8,128)(2,1)S(1)} %get-tuple-element.27), channel_id=1, source_target_pairs={{0,32},{32,0},{64,96},{96,64},{128,160},{160,128},{192,224},{224,1... | collective-permute-start | bytes 1179656 | tf_op jit(solution)/shard_map/ppermute | solution.py:296
  11.3 6.1 %collective-permute-start.1 = (bf16[64,768]{1,0:T(8,128)(2,1)S(1)}, bf16[64,768]{1,0:T(8,128)(2,1)S(1)}, u32[]{:S(2)}, u32[]{:S(2)}) collective-permute-start(bf16[64,768]{1,0:T(8,128)(2,1)S(1)} %get-tuple-element.32), channel_id=1, source_target_pairs={{0,8},{2,10},{4,12},{6,14},{8,16},{10,18},{12,20},{14,22},{16,24},... | collective-permute-start | bytes 294920 | tf_op jit(solution)/shard_map/ppermute | solution.py:300
  11.4 7.2 %collective-permute-start.2 = (bf16[64,768]{1,0:T(8,128)(2,1)S(1)}, bf16[64,768]{1,0:T(8,128)(2,1)S(1)}, u32[]{:S(2)}, u32[]{:S(2)}) collective-permute-start(bf16[64,768]{1,0:T(8,128)(2,1)S(1)} %get-tuple-element.33), channel_id=1, source_target_pairs={{0,16},{2,18},{4,20},{6,22},{8,24},{10,26},{12,28},{14,30},{16,0},... | collective-permute-start | bytes 294920 | tf_op jit(solution)/shard_map/ppermute | solution.py:300
  13.6 5.7 %collective-permute-start.3 = (bf16[64,768]{1,0:T(8,128)(2,1)S(1)}, bf16[64,768]{1,0:T(8,128)(2,1)S(1)}, u32[]{:S(2)}, u32[]{:S(2)}) collective-permute-start(bf16[64,768]{1,0:T(8,128)(2,1)S(1)} %get-tuple-element.34), channel_id=1, source_target_pairs={{0,24},{2,26},{4,28},{6,30},{8,0},{10,2},{12,4},{14,6},{16,8},{18,... | collective-permute-start | bytes 294920 | tf_op jit(solution)/shard_map/ppermute | solution.py:300
  20.0 5.2 %collective-permute-start.4 = (f32[16,768]{1,0:T(8,128)S(1)}, f32[16,768]{1,0:T(8,128)S(1)}, u32[]{:S(2)}, u32[]{:S(2)}) collective-permute-start(f32[16,768]{1,0:T(8,128)S(1)} %get-tuple-element.36), channel_id=1, source_target_pairs={{0,2},{2,4},{4,6},{6,0},{8,10},{10,12},{12,14},{14,8},{16,18},{18,... | collective-permute-start | bytes 147464 | tf_op jit(solution)/shard_map/ppermute | solution.py:303
  21.0 4.7 %collective-permute-start.5 = (f32[16,768]{1,0:T(8,128)S(1)}, f32[16,768]{1,0:T(8,128)S(1)}, u32[]{:S(2)}, u32[]{:S(2)}) collective-permute-start(f32[16,768]{1,0:T(8,128)S(1)} %get-tuple-element.37), channel_id=1, source_target_pairs={{0,4},{2,6},{4,0},{6,2},{8,12},{10,14},{12,8},{14,10},{16,20},{18,... | collective-permute-start | bytes 147464 | tf_op jit(solution)/shard_map/ppermute | solution.py:303
  24.0 3.8 %collective-permute-start.6 = (f32[16,768]{1,0:T(8,128)S(1)}, f32[16,768]{1,0:T(8,128)S(1)}, u32[]{:S(2)}, u32[]{:S(2)}) collective-permute-start(f32[16,768]{1,0:T(8,128)S(1)} %get-tuple-element.38), channel_id=1, source_target_pairs={{0,6},{2,0},{4,2},{6,4},{8,14},{10,8},{12,10},{14,12},{16,22},{18,... | collective-permute-start | bytes 147464 | tf_op jit(solution)/shard_map/ppermute | solution.py:303
  27.9 3.7 %collective-permute-start.9 = (f32[16,768]{1,0:T(8,128)S(1)}, f32[16,768]{1,0:T(8,128)S(1)}, u32[]{:S(2)}, u32[]{:S(2)}) collective-permute-start(f32[16,768]{1,0:T(8,128)S(1)} %z_merge.1.own), channel_id=1, source_target_pairs={{0,192},{32,224},{64,0},{96,32},{128,64},{160,96},{192,128},{224,1... | collective-permute-start | bytes 147464 | tf_op jit(solution)/shard_map/ppermute | solution.py:305
  30.4 4.5 %collective-permute-start.8 = (f32[16,768]{1,0:T(8,128)S(1)}, f32[16,768]{1,0:T(8,128)S(1)}, u32[]{:S(2)}, u32[]{:S(2)}) collective-permute-start(f32[16,768]{1,0:T(8,128)S(1)} %z_merge.1.own), channel_id=1, source_target_pairs={{0,128},{32,160},{64,192},{96,224},{128,0},{160,32},{192,64},{224,... | collective-permute-start | bytes 147464 | tf_op jit(solution)/shard_map/ppermute | solution.py:305
  30.9 4.5 %collective-permute-start.7 = (f32[16,768]{1,0:T(8,128)S(1)}, f32[16,768]{1,0:T(8,128)S(1)}, u32[]{:S(2)}, u32[]{:S(2)}) collective-permute-start(f32[16,768]{1,0:T(8,128)S(1)} %z_merge.1.own), channel_id=1, source_target_pairs={{0,64},{32,96},{64,128},{96,160},{128,192},{160,224},{192,0},{224,... | collective-permute-start | bytes 147464 | tf_op jit(solution)/shard_map/ppermute | solution.py:305
  35.5 4.3 %collective-permute-start.10 = (bf16[16,640]{1,0:T(8,128)(2,1)S(1)}, bf16[16,640]{1,0:T(8,128)(2,1)S(1)}, u32[]{:S(2)}, u32[]{:S(2)}) collective-permute-start(bf16[16,640]{1,0:T(8,128)(2,1)S(1)} %x_merge.1.slot_own), channel_id=1, source_target_pairs={{0,32},{32,0},{64,96},{96,64},{128,160},{160,128},{192,224},{224,1... | collective-permute-start | bytes 61448 | tf_op jit(solution)/shard_map/ppermute | solution.py:307
  41.0 1.3 %collective-permute-start.11 = (f32[16,640]{1,0:T(8,128)S(1)}, f32[16,640]{1,0:T(8,128)S(1)}, u32[]{:S(2)}, u32[]{:S(2)}) collective-permute-start(f32[16,640]{1,0:T(8,128)S(1)} %get-tuple-element.42), channel_id=1, source_target_pairs={{0,32},{32,0},{64,96},{96,64},{128,160},{160,128},{192,224},{224,1... | collective-permute-start | bytes 122888 | tf_op jit(solution)/shard_map/ppermute | solution.py:309
  42.3 2.9 %collective-permute-start.14 = (f32[16,640]{1,0:T(8,128)S(1)}, f32[16,640]{1,0:T(8,128)S(1)}, u32[]{:S(2)}, u32[]{:S(2)}) collective-permute-start(f32[16,640]{1,0:T(8,128)S(1)} %add.76), channel_id=1, source_target_pairs={{0,192},{32,224},{64,0},{96,32},{128,64},{160,96},{192,128},{224,1... | collective-permute-start | bytes 122888 | tf_op jit(solution)/shard_map/ppermute | solution.py:310
  42.6 4.4 %collective-permute-start.13 = (f32[16,640]{1,0:T(8,128)S(1)}, f32[16,640]{1,0:T(8,128)S(1)}, u32[]{:S(2)}, u32[]{:S(2)}) collective-permute-start(f32[16,640]{1,0:T(8,128)S(1)} %add.76), channel_id=1, source_target_pairs={{0,128},{32,160},{64,192},{96,224},{128,0},{160,32},{192,64},{224,... | collective-permute-start | bytes 122888 | tf_op jit(solution)/shard_map/ppermute | solution.py:310
  43.6 4.4 %collective-permute-start.12 = (f32[16,640]{1,0:T(8,128)S(1)}, f32[16,640]{1,0:T(8,128)S(1)}, u32[]{:S(2)}, u32[]{:S(2)}) collective-permute-start(f32[16,640]{1,0:T(8,128)S(1)} %add.76), channel_id=1, source_target_pairs={{0,64},{32,96},{64,128},{96,160},{128,192},{160,224},{192,0},{224,... | collective-permute-start | bytes 122888 | tf_op jit(solution)/shard_map/ppermute | solution.py:310
  48.0 4.5 %collective-permute-start.15 = (bf16[16,640]{1,0:T(8,128)(2,1)S(1)}, bf16[16,640]{1,0:T(8,128)(2,1)S(1)}, u32[]{:S(2)}, u32[]{:S(2)}) collective-permute-start(bf16[16,640]{1,0:T(8,128)(2,1)S(1)} %get-tuple-element.44), channel_id=1, source_target_pairs={{0,2},{2,4},{4,6},{6,0},{8,10},{10,12},{12,14},{14,8},{16,18},{18,... | collective-permute-start | bytes 61448 | tf_op jit(solution)/shard_map/ppermute | solution.py:316
  48.4 4.1 %collective-permute-start.16 = (bf16[16,640]{1,0:T(8,128)(2,1)S(1)}, bf16[16,640]{1,0:T(8,128)(2,1)S(1)}, u32[]{:S(2)}, u32[]{:S(2)}) collective-permute-start(bf16[16,640]{1,0:T(8,128)(2,1)S(1)} %get-tuple-element.44), channel_id=1, source_target_pairs={{0,4},{2,6},{4,0},{6,2},{8,12},{10,14},{12,8},{14,10},{16,20},{18,... | collective-permute-start | bytes 61448 | tf_op jit(solution)/shard_map/ppermute | solution.py:316
  50.9 2.6 %collective-permute-start.17 = (bf16[16,640]{1,0:T(8,128)(2,1)S(1)}, bf16[16,640]{1,0:T(8,128)(2,1)S(1)}, u32[]{:S(2)}, u32[]{:S(2)}) collective-permute-start(bf16[16,640]{1,0:T(8,128)(2,1)S(1)} %get-tuple-element.44), channel_id=1, source_target_pairs={{0,6},{2,0},{4,2},{6,4},{8,14},{10,8},{12,10},{14,12},{16,22},{18,... | collective-permute-start | bytes 61448 | tf_op jit(solution)/shard_map/ppermute | solution.py:316
  53.5 7.6 %collective-permute-start.20 = (bf16[64,640]{1,0:T(8,128)(2,1)S(1)}, bf16[64,640]{1,0:T(8,128)(2,1)S(1)}, u32[]{:S(2)}, u32[]{:S(2)}) collective-permute-start(bf16[64,640]{1,0:T(8,128)(2,1)S(1)} %constant_dynamic-update-slice_fusion.4), channel_id=1, source_target_pairs={{0,24},{2,26},{4,28},{6,30},{8,0},{10,2},{12,4},{14,6},{16,8},{18,... | collective-permute-start | bytes 245768 | tf_op jit(solution)/shard_map/ppermute | solution.py:316
  55.4 5.7 %collective-permute-start.19 = (bf16[64,640]{1,0:T(8,128)(2,1)S(1)}, bf16[64,640]{1,0:T(8,128)(2,1)S(1)}, u32[]{:S(2)}, u32[]{:S(2)}) collective-permute-start(bf16[64,640]{1,0:T(8,128)(2,1)S(1)} %constant_dynamic-update-slice_fusion.4), channel_id=1, source_target_pairs={{0,16},{2,18},{4,20},{6,22},{8,24},{10,26},{12,28},{14,30},{16,0},... | collective-permute-start | bytes 245768 | tf_op jit(solution)/shard_map/ppermute | solution.py:316
  56.3 4.8 %collective-permute-start.18 = (bf16[64,640]{1,0:T(8,128)(2,1)S(1)}, bf16[64,640]{1,0:T(8,128)(2,1)S(1)}, u32[]{:S(2)}, u32[]{:S(2)}) collective-permute-start(bf16[64,640]{1,0:T(8,128)(2,1)S(1)} %constant_dynamic-update-slice_fusion.4), channel_id=1, source_target_pairs={{0,8},{2,10},{4,12},{6,14},{8,16},{10,18},{12,20},{14,22},{16,24},... | collective-permute-start | bytes 245768 | tf_op jit(solution)/shard_map/ppermute | solution.py:316
  61.2 7.2 %collective-permute-start.21 = (bf16[256,640]{1,0:T(8,128)(2,1)S(1)}, bf16[256,640]{1,0:T(8,128)(2,1)S(1)}, u32[]{:S(2)}, u32[]{:S(2)}) collective-permute-start(bf16[256,640]{1,0:T(8,128)(2,1)S(1)} %constant_dynamic-update-slice_fusion.slot_out), channel_id=1, source_target_pairs={{0,32},{32,0},{64,96},{96,64},{128,160},{160,128},{192,224},{224,1... | collective-permute-start | bytes 983048 | tf_op jit(solution)/shard_map/ppermute | solution.py:323

commit v4 on v3

--- a/solution.py
+++ b/solution.py
@@ -11,8 +11,19 @@
 BF16 = jnp.bfloat16
 LANES = 128
 VMEM = pl.BlockSpec(memory_space=pltpu.VMEM)
-SMEM = pl.BlockSpec(memory_space=pltpu.SMEM)
 ANY = pl.BlockSpec(memory_space=pl.ANY)
+
+
+def _core():
+    return lax.rem(lax.axis_index("seq"), 2)
+
+
+def _y():
+    return lax.div(lax.axis_index("exp"), 4)
+
+
+def _z():
+    return lax.rem(lax.axis_index("exp"), 4)
 
 
 def _core_perm():
@@ -112,7 +123,7 @@
     return out
 
 
-def first_kernel(chunks, where, tok_hbm, keys_hbm, tok, logits, dispatch, packed, stat, keys, acc, sem):
+def first_kernel(chunks, tok_hbm, keys_hbm, tok, logits, dispatch, packed, stat, keys, acc, sem):
     tokens, width = tok.shape
     half = width // 2
     step = tokens // chunks
@@ -126,7 +137,7 @@
     ]
     for c in copies:
         c.start()
-    other = pl.multiple_of((1 - where[0]) * half, LANES)
+    other = pl.multiple_of((1 - _core()) * half, LANES)
     keys_copy.wait()
     keys_t = keys[...].T
 
@@ -171,10 +182,10 @@
         stat[:, (2 + i) * LANES : (3 + i) * LANES] = jnp.exp(peaks[i] - peak)
 
 
-def own_kernel(chunks, where, tok, dispatch, stat, own):
+def own_kernel(chunks, tok, dispatch, stat, own):
     half = tok.shape[1] // 2
     step = tok.shape[0] // chunks
-    off = pl.multiple_of(where[0] * half, LANES)
+    off = pl.multiple_of(_core() * half, LANES)
     sums = None
     for i in range(chunks):
         part = _times(
@@ -203,10 +214,10 @@
         c.wait()
 
 
-def expert_kernel(where, slot_own, slot_other, w_in, w_out, own, send):
+def expert_kernel(slot_own, slot_other, w_in, w_out, own, send):
     half = slot_own.shape[1]
-    mine = pl.multiple_of(where[0] * half, LANES)
-    other = pl.multiple_of((1 - where[0]) * half, LANES)
+    mine = pl.multiple_of(_core() * half, LANES)
+    other = pl.multiple_of((1 - _core()) * half, LANES)
     hidden = jnp.dot(slot_own[...], w_in[pl.ds(mine, half), :], preferred_element_type=F32)
     hidden += jnp.dot(slot_other[...], w_in[pl.ds(other, half), :], preferred_element_type=F32)
     hidden = jax.nn.gelu(hidden).astype(BF16)
@@ -214,10 +225,10 @@
     own[...] = jnp.dot(hidden, w_out[:, pl.ds(mine, half)], preferred_element_type=F32)
 
 
-def core_merge_kernel(where, own, stat, got, keep, keep_stat, send1, send2, send3):
+def core_merge_kernel(own, stat, got, keep, keep_stat, send1, send2, send3):
     rows, half = keep.shape
     for k, ref in enumerate((keep, send1, send2, send3)):
-        part = pl.ds(pl.multiple_of(lax.rem(where[1] + k, 4) * rows, rows), rows)
+        part = pl.ds(pl.multiple_of(lax.rem(_y() + k, 4) * rows, rows), rows)
         sums, peak, total = _merge(
             [
                 (own[part, :], stat[part, :LANES], stat[part, LANES : 2 * LANES]),
@@ -232,10 +243,10 @@
             ref[:, half:] = _pieces(peak, total)
 
 
-def y_merge_kernel(where, after, own, stat, got1, got2, got3, keep, send1, send2, send3):
+def y_merge_kernel(after, own, stat, got1, got2, got3, keep, send1, send2, send3):
     rows, half = keep.shape[0], own.shape[1]
     for k, ref in enumerate((keep, send1, send2, send3)):
-        part = pl.ds(pl.multiple_of(lax.rem(where[2] + k, 4) * rows, rows), rows)
+        part = pl.ds(pl.multiple_of(lax.rem(_z() + k, 4) * rows, rows), rows)
         sums, peak, total = _merge(
             [(own[part, :], stat[part, :LANES], stat[part, LANES:])]
             + [
@@ -268,11 +279,11 @@
     return jnp.concatenate([v] * (width // LANES), axis=1)
 
 
-def mix_kernel(chunks, own, where, combine, slot_out, *refs):
+def mix_kernel(chunks, own, combine, slot_out, *refs):
     out_hbm, buf, sem = refs[-3:]
     half = slot_out.shape[1]
     step = combine.shape[0] // chunks
-    column = pl.multiple_of((where[0] if own else 1 - where[0]) * half, LANES)
+    column = pl.multiple_of((_core() if own else 1 - _core()) * half, LANES)
     copies = []
     for i in range(chunks):
         buf[i] = jnp.dot(
@@ -288,24 +299,22 @@
 
 
 def body(tokens, slot_keys, w_in, w_out):
-    seq, exp = lax.axis_index("seq"), lax.axis_index("exp")
-    y, z = exp // 4, exp % 4
-    where = jnp.stack([seq % 2, y, z]).astype(jnp.int32)
-
-    tok, logits, dispatch, packed, stat = first(where, tokens, slot_keys)
+    y, z = _y(), _z()
+
+    tok, logits, dispatch, packed, stat = first(tokens, slot_keys)
     got = lax.ppermute(packed, "seq", _core_perm())
-    own = own_sums(where, tok, dispatch, stat)
-
-    own, stat, *send = core_merge(where, own, stat, got)
+    own = own_sums(tok, dispatch, stat)
+
+    own, stat, *send = core_merge(own, stat, got)
     got = [lax.ppermute(v, "exp", _y_perm(k + 1)) for k, v in enumerate(send)]
     combine, w_in, w_out = combine_weights(own, logits, w_in[0], w_out[0])
-    own, *send = y_merge(where, combine, own, stat, *got)
+    own, *send = y_merge(combine, own, stat, *got)
     got = [lax.ppermute(v, "exp", _z_perm(k + 1)) for k, v in enumerate(send)]
     own = z_merge(own, *got)
     got = [lax.ppermute(own, "seq", _x_perm(k)) for k in range(1, 4)]
     slot_half = x_merge(own, *got)
     got = lax.ppermute(slot_half, "seq", _core_perm())
-    mine, other = expert(where, slot_half, got, w_in, w_out)
+    mine, other = expert(slot_half, got, w_in, w_out)
     part = mine + lax.ppermute(other, "seq", _core_perm())
     whole = part + sum(lax.ppermute(part, "seq", _x_perm(k)) for k in range(1, 4))
     out = whole.astype(BF16)
@@ -321,14 +330,14 @@
     out = gather(out, z, _z_perm)
     out = gather(out, y, _y_perm)
     other = lax.ppermute(out, "seq", _core_perm())
-    mixed = mix(where, combine, out)
-    return mix(where, combine, other, mixed)
+    mixed = mix(combine, out)
+    return mix(combine, other, mixed)
 
 
 CHUNKS = 4
 
 
-def first(where, tokens, slot_keys):
+def first(tokens, slot_keys):
     count, width = tokens.shape
     slots = slot_keys.shape[1]
     half = width // 2
@@ -342,7 +351,7 @@
             pltpu.VMEM((slots, half + LANES), BF16),
             pltpu.VMEM((slots, (2 + CHUNKS) * LANES), F32),
         ],
-        [SMEM, ANY, ANY],
+        [ANY, ANY],
         [
             pltpu.VMEM((width, slots), BF16),
             pltpu.VMEM((slots, half), F32),
@@ -351,18 +360,18 @@
         vmem=16,
         flops=3 * count * slots * width,
         bytes_accessed=2 * count * width,
-    )(where, *(pltpu.with_memory_space_constraint(v, pltpu.HBM) for v in (tokens, slot_keys)))
-
-
-def own_sums(where, tok, dispatch, stat):
+    )(*(pltpu.with_memory_space_constraint(v, pltpu.HBM) for v in (tokens, slot_keys)))
+
+
+def own_sums(tok, dispatch, stat):
     return _call(
         functools.partial(own_kernel, CHUNKS),
         "own_sums",
         pltpu.VMEM((stat.shape[0], tok.shape[1] // 2), F32),
-        [SMEM, VMEM, VMEM, VMEM],
+        [VMEM, VMEM, VMEM],
         vmem=12,
         flops=dispatch.size * tok.shape[1],
-    )(where, tok, dispatch, stat)
+    )(tok, dispatch, stat)
 
 
 def combine_weights(after, logits, w_in, w_out):
@@ -383,35 +392,35 @@
     )(after, logits, *(pltpu.with_memory_space_constraint(v, pltpu.HBM) for v in (w_in, w_out)))
 
 
-def expert(where, slot_own, slot_other, w_in, w_out):
+def expert(slot_own, slot_other, w_in, w_out):
     return _call(
         expert_kernel,
         "expert",
         [pltpu.VMEM(slot_own.shape, F32)] * 2,
-        [SMEM] + [VMEM] * 4,
+        [VMEM] * 4,
         flops=4 * slot_own.shape[0] * w_in.size,
-    )(where, slot_own, slot_other, w_in, w_out)
-
-
-def core_merge(where, own, stat, got):
+    )(slot_own, slot_other, w_in, w_out)
+
+
+def core_merge(own, stat, got):
     rows, half = own.shape[0] // 4, own.shape[1]
     return _call(
         core_merge_kernel,
         "core_merge",
         [pltpu.VMEM((rows, half), F32), pltpu.VMEM((rows, 2 * LANES), F32)]
         + [pltpu.VMEM((rows, half + LANES), BF16)] * 3,
-        [SMEM] + [VMEM] * 3,
-    )(where, own, stat, got)
-
-
-def y_merge(where, after, own, stat, *got):
+        [VMEM] * 3,
+    )(own, stat, got)
+
+
+def y_merge(after, own, stat, *got):
     rows, half = own.shape[0] // 4, own.shape[1]
     return _call(
         y_merge_kernel,
         "y_merge",
         [pltpu.VMEM((rows, half + LANES), F32)] * 4,
-        [SMEM, ANY] + [VMEM] * 5,
-    )(where, after, own, stat, *got)
+        [ANY] + [VMEM] * 5,
+    )(after, own, stat, *got)
 
 
 def z_merge(own, *got):
@@ -423,7 +432,7 @@
     return _call(x_merge_kernel, "x_merge", out, [VMEM] * 4)(own, *got)
 
 
-def mix(where, combine, slot_out, *mixed):
+def mix(combine, slot_out, *mixed):
     count, slots = combine.shape
     half = slot_out.shape[1]
     steps = 8
@@ -431,14 +440,14 @@
         functools.partial(mix_kernel, steps, not mixed),
         "mix",
         jax.ShapeDtypeStruct((count, 2 * half), BF16),
-        [SMEM, VMEM, VMEM] + [ANY] * len(mixed),
+        [VMEM, VMEM] + [ANY] * len(mixed),
         [pltpu.VMEM((steps, count // steps, half), BF16), pltpu.SemaphoreType.DMA((steps,))],
         out_specs=ANY,
         vmem=12,
         flops=2 * count * slots * half,
         bytes_accessed=2 * count * half,
-        input_output_aliases={3: 0} if mixed else {},
-    )(where, combine, slot_out, *mixed)
+        input_output_aliases={2: 0} if mixed else {},
+    )(combine, slot_out, *mixed)
 
 
 def solution(mesh):

time: 71 us -> 67.5 us (0.951)
  Pallas kernels: 16.7 us -> 12.8 us
    pallas_call x2, Pallas kernels: 4.79 us -> 3.7 us  [mix(): _call(functools.partial(mix_kernel, steps, not mixed), 'mix', jax.ShapeDt...]
  transfers between devices with their start and end apart: 22 -> 22, of which waited for: 17 -> 18; matrix products, arithmetic and copies ran while one was open for 0% -> 0% of each run, Pallas kernels for 8% -> 7%
where the time goes in v4:
time: 67.5 us; the launch traced here: 67.4 us
  starting transfers between devices  32.2 us (48%)
  waiting for transfers between devices  21.7 us (32%)
  Pallas kernels  12.8 us (19%)
    ppermute x6, waiting for transfers between devices, gather(): lax.ppermute(block, 'exp', perm(k))  6.59 us
    ppermute x6, starting transfers between devices, gather(): lax.ppermute(block, 'exp', perm(k))  6.33 us
    ppermute x1, starting transfers between devices, body(): other = lax.ppermute(out, 'seq', _core_perm())  4.83 us
    pallas_call x1, Pallas kernels, first(): _call(functools.partial(first_kernel, CHUNKS), 'logits_and_sums', [pltpu....  4.76 us
    ppermute x3, starting transfers between devices, body(): got = [lax.ppermute(v, 'exp', _z_perm(k + 1)) for k, v in enumerate(send)]  4.7 us
    ppermute x3, waiting for transfers between devices, body(): got = [lax.ppermute(own, 'seq', _x_perm(k)) for k in range(1, 4)]  3.85 us
    pallas_call x2, Pallas kernels, mix(): _call(functools.partial(mix_kernel, steps, not mixed), 'mix', jax.ShapeDt...  3.7 us
    ppermute x3, starting transfers between devices, body(): got = [lax.ppermute(own, 'seq', _x_perm(k)) for k in range(1, 4)]  3.67 us
  transfers between devices with their start and end apart: 22, of which 18 were waited for; matrix products, arithmetic and copies ran while one was open for 0% of the time, Pallas kernels for 7%

profile of v4, /device:TPU:1, one launch (start us, length us, event | category | flops | bytes accessed | tf_op | source)
XLA Modules:
  0.0 67.4 jit_solution(6139911273272202672)
XLA Ops:
  0.0 4.8 %logits_and_sums.1 = (bf16[2048,1280]{1,0:T(8,128)(2,1)S(1)}, f32[256,2048]{1,0:T(8,128)S(1)}, bf16[256,2048]{1,0:T(8,128)(2,1)S(1)}, bf16[256,768]{1,0:T(8,128)(2,1)S(1)}, f32[256,768]{1,0:T(8,128)S(1)}) custom-call(bf16[2048,1280]{1,0:T(8,128)(2,1)} %tok_hbm.1, bf16[1280,256]{1,0:T(8,128)(2,1)} %keys_hbm.1), custom_call_target="tpu_custom_call" | custom-call | flops 2013265920 | bytes 5242880 | tf_op jit(solution)/shard_map/logits_and_sums/pallas_call | solution.py:344
  4.8 3.4 %collective-permute-start = (bf16[256,768]{1,0:T(8,128)(2,1)S(1)}, bf16[256,768]{1,0:T(8,128)(2,1)S(1)}, u32[]{:S(2)}, u32[]{:S(2)}) collective-permute-start(bf16[256,768]{1,0:T(8,128)(2,1)S(1)} %get-tuple-element.27), channel_id=1, source_target_pairs={{0,32},{32,0},{64,96},{96,64},{128,160},{160,128},{192,224},{224,1... | collective-permute-start | bytes 1179656 | tf_op jit(solution)/shard_map/ppermute | solution.py:305
  8.1 1.0 %own_sums.1.own = f32[256,640]{1,0:T(8,128)S(1)} custom-call(bf16[2048,1280]{1,0:T(8,128)(2,1)S(1)} %get-tuple-element.24.tok, bf16[256,2048]{1,0:T(8,128)(2,1)S(1)} %get-tuple-element.25.dispatch, f32[256,768]{1,0:T(8,128)S(1)} %get-tuple-element.26.stat), custom_call_target="tpu_custom_call" | custom-call | flops 671088640 | tf_op jit(solution)/shard_map/own_sums/pallas_call | solution.py:367
  9.2 0.3 collective-permute-done.got
  9.5 0.3 core_merge.1
  9.9 2.2 %collective-permute-start.2 = (bf16[64,768]{1,0:T(8,128)(2,1)S(1)}, bf16[64,768]{1,0:T(8,128)(2,1)S(1)}, u32[]{:S(2)}, u32[]{:S(2)}) collective-permute-start(bf16[64,768]{1,0:T(8,128)(2,1)S(1)} %get-tuple-element.33), channel_id=1, source_target_pairs={{0,16},{2,18},{4,20},{6,22},{8,24},{10,26},{12,28},{14,30},{16,0},... | collective-permute-start | bytes 294920 | tf_op jit(solution)/shard_map/ppermute | solution.py:309
  12.1 1.1 %collective-permute-start.3 = (bf16[64,768]{1,0:T(8,128)(2,1)S(1)}, bf16[64,768]{1,0:T(8,128)(2,1)S(1)}, u32[]{:S(2)}, u32[]{:S(2)}) collective-permute-start(bf16[64,768]{1,0:T(8,128)(2,1)S(1)} %get-tuple-element.34), channel_id=1, source_target_pairs={{0,24},{2,26},{4,28},{6,30},{8,0},{10,2},{12,4},{14,6},{16,8},{18,... | collective-permute-start | bytes 294920 | tf_op jit(solution)/shard_map/ppermute | solution.py:309
  13.2 1.9 %combine.1 = (bf16[2048,256]{1,0:T(8,128)(2,1)S(1)}, bf16[1280,640]{1,0:T(8,128)(2,1)S(1)}, bf16[640,1280]{1,0:T(8,128)(2,1)S(1)}) custom-call(f32[64,640]{1,0:T(8,128)S(1)} %get-tuple-element.28.after.own, f32[256,2048]{1,0:T(8,128)S(1)} %get-tuple-element.29.logits, bf16[1280,640]{1,0:T(8,128)(2,1)} %bitcast.2, bf16[640,1280]{1,0:T(8,128)(2,1)} %bitcast.3), custom_call_target="tpu_custom_call" | custom-call | flops 5242880 | bytes 3276800 | tf_op jit(solution)/shard_map/combine/pallas_call | solution.py:379
  15.1 0.5 collective-permute-done.1.got1
  15.6 1.1 %collective-permute-done.2.got2 = bf16[64,768]{1,0:T(8,128)(2,1)S(1)} collective-permute-done((bf16[64,768]{1,0:T(8,128)(2,1)S(1)}, bf16[64,768]{1,0:T(8,128)(2,1)S(1)}, u32[]{:S(2)}, u32[]{:S(2)}) %collective-permute-start.2) | collective-permute-done | bytes 98336 | tf_op jit(solution)/shard_map/ppermute | solution.py:309
  16.7 0.7 %collective-permute-done.3.got3 = bf16[64,768]{1,0:T(8,128)(2,1)S(1)} collective-permute-done((bf16[64,768]{1,0:T(8,128)(2,1)S(1)}, bf16[64,768]{1,0:T(8,128)(2,1)S(1)}, u32[]{:S(2)}, u32[]{:S(2)}) %collective-permute-start.3) | collective-permute-done | bytes 98336 | tf_op jit(solution)/shard_map/ppermute | solution.py:309
  17.5 0.2 y_merge.1
  17.7 1.0 %collective-permute-start.4 = (f32[16,768]{1,0:T(8,128)S(1)}, f32[16,768]{1,0:T(8,128)S(1)}, u32[]{:S(2)}, u32[]{:S(2)}) collective-permute-start(f32[16,768]{1,0:T(8,128)S(1)} %get-tuple-element.36), channel_id=1, source_target_pairs={{0,2},{2,4},{4,6},{6,0},{8,10},{10,12},{12,14},{14,8},{16,18},{18,... | collective-permute-start | bytes 147464 | tf_op jit(solution)/shard_map/ppermute | solution.py:312
  18.7 3.0 %collective-permute-start.5 = (f32[16,768]{1,0:T(8,128)S(1)}, f32[16,768]{1,0:T(8,128)S(1)}, u32[]{:S(2)}, u32[]{:S(2)}) collective-permute-start(f32[16,768]{1,0:T(8,128)S(1)} %get-tuple-element.37), channel_id=1, source_target_pairs={{0,4},{2,6},{4,0},{6,2},{8,12},{10,14},{12,8},{14,10},{16,20},{18,... | collective-permute-start | bytes 147464 | tf_op jit(solution)/shard_map/ppermute | solution.py:312
  21.7 0.7 %collective-permute-start.6 = (f32[16,768]{1,0:T(8,128)S(1)}, f32[16,768]{1,0:T(8,128)S(1)}, u32[]{:S(2)}, u32[]{:S(2)}) collective-permute-start(f32[16,768]{1,0:T(8,128)S(1)} %get-tuple-element.38), channel_id=1, source_target_pairs={{0,6},{2,0},{4,2},{6,4},{8,14},{10,8},{12,10},{14,12},{16,22},{18,... | collective-permute-start | bytes 147464 | tf_op jit(solution)/shard_map/ppermute | solution.py:312
  22.4 0.5 collective-permute-done.4.got1
  22.9 0.5 collective-permute-done.5.got2
  23.4 2.3 %collective-permute-done.6.got3 = f32[16,768]{1,0:T(8,128)S(1)} collective-permute-done((f32[16,768]{1,0:T(8,128)S(1)}, f32[16,768]{1,0:T(8,128)S(1)}, u32[]{:S(2)}, u32[]{:S(2)}) %collective-permute-start.6) | collective-permute-done | bytes 49184 | tf_op jit(solution)/shard_map/ppermute | solution.py:312
  25.7 0.1 z_merge.1.own
  25.8 2.5 %collective-permute-start.9 = (f32[16,768]{1,0:T(8,128)S(1)}, f32[16,768]{1,0:T(8,128)S(1)}, u32[]{:S(2)}, u32[]{:S(2)}) collective-permute-start(f32[16,768]{1,0:T(8,128)S(1)} %z_merge.1.own), channel_id=1, source_target_pairs={{0,192},{32,224},{64,0},{96,32},{128,64},{160,96},{192,128},{224,1... | collective-permute-start | bytes 147464 | tf_op jit(solution)/shard_map/ppermute | solution.py:314
  28.3 0.5 collective-permute-start.8
  28.8 0.6 collective-permute-start.7
  29.5 3.3 %collective-permute-done.8.got2 = f32[16,768]{1,0:T(8,128)S(1)} collective-permute-done((f32[16,768]{1,0:T(8,128)S(1)}, f32[16,768]{1,0:T(8,128)S(1)}, u32[]{:S(2)}, u32[]{:S(2)}) %collective-permute-start.8) | collective-permute-done | bytes 49184 | tf_op jit(solution)/shard_map/ppermute | solution.py:314
  32.8 0.5 collective-permute-done.7.got1
  33.3 0.1 x_merge.1.slot_own
  33.4 3.5 %collective-permute-start.10 = (bf16[16,640]{1,0:T(8,128)(2,1)S(1)}, bf16[16,640]{1,0:T(8,128)(2,1)S(1)}, u32[]{:S(2)}, u32[]{:S(2)}) collective-permute-start(bf16[16,640]{1,0:T(8,128)(2,1)S(1)} %x_merge.1.slot_own), channel_id=1, source_target_pairs={{0,32},{32,0},{64,96},{96,64},{128,160},{160,128},{192,224},{224,1... | collective-permute-start | bytes 61448 | tf_op jit(solution)/shard_map/ppermute | solution.py:316
  37.0 0.8 %collective-permute-done.10.slot_other = bf16[16,640]{1,0:T(8,128)(2,1)S(1)} collective-permute-done((bf16[16,640]{1,0:T(8,128)(2,1)S(1)}, bf16[16,640]{1,0:T(8,128)(2,1)S(1)}, u32[]{:S(2)}, u32[]{:S(2)}) %collective-permute-start.10) | collective-permute-done | bytes 20512 | tf_op jit(solution)/shard_map/ppermute | solution.py:316
  37.8 0.6 expert.1
  38.4 0.4 collective-permute-start.11
  38.9 0.9 %collective-permute-done.11 = f32[16,640]{1,0:T(8,128)S(1)} collective-permute-done((f32[16,640]{1,0:T(8,128)S(1)}, f32[16,640]{1,0:T(8,128)S(1)}, u32[]{:S(2)}, u32[]{:S(2)}) %collective-permute-start.11) | collective-permute-done | bytes 40992 | tf_op jit(solution)/shard_map/ppermute | solution.py:318
  39.7 0.3 collective-permute-start.14
  40.0 1.0 %collective-permute-start.13 = (f32[16,640]{1,0:T(8,128)S(1)}, f32[16,640]{1,0:T(8,128)S(1)}, u32[]{:S(2)}, u32[]{:S(2)}) collective-permute-start(f32[16,640]{1,0:T(8,128)S(1)} %add.67), channel_id=1, source_target_pairs={{0,128},{32,160},{64,192},{96,224},{128,0},{160,32},{192,64},{224,... | collective-permute-start | bytes 122888 | tf_op jit(solution)/shard_map/ppermute | solution.py:319
  41.1 0.8 %collective-permute-start.12 = (f32[16,640]{1,0:T(8,128)S(1)}, f32[16,640]{1,0:T(8,128)S(1)}, u32[]{:S(2)}, u32[]{:S(2)}) collective-permute-start(f32[16,640]{1,0:T(8,128)S(1)} %add.67), channel_id=1, source_target_pairs={{0,64},{32,96},{64,128},{96,160},{128,192},{160,224},{192,0},{224,... | collective-permute-start | bytes 122888 | tf_op jit(solution)/shard_map/ppermute | solution.py:319
  41.8 0.8 %collective-permute-done.14 = f32[16,640]{1,0:T(8,128)S(1)} collective-permute-done((f32[16,640]{1,0:T(8,128)S(1)}, f32[16,640]{1,0:T(8,128)S(1)}, u32[]{:S(2)}, u32[]{:S(2)}) %collective-permute-start.14) | collective-permute-done | bytes 40992 | tf_op jit(solution)/shard_map/ppermute | solution.py:319
  42.6 1.8 %collective-permute-done.13 = f32[16,640]{1,0:T(8,128)S(1)} collective-permute-done((f32[16,640]{1,0:T(8,128)S(1)}, f32[16,640]{1,0:T(8,128)S(1)}, u32[]{:S(2)}, u32[]{:S(2)}) %collective-permute-start.13) | collective-permute-done | bytes 40992 | tf_op jit(solution)/shard_map/ppermute | solution.py:319
  44.4 1.0 %collective-permute-done.12 = f32[16,640]{1,0:T(8,128)S(1)} collective-permute-done((f32[16,640]{1,0:T(8,128)S(1)}, f32[16,640]{1,0:T(8,128)S(1)}, u32[]{:S(2)}, u32[]{:S(2)}) %collective-permute-start.12) | collective-permute-done | bytes 40992 | tf_op jit(solution)/shard_map/ppermute | solution.py:319
  45.5 0.1 collective-permute-start.15
  45.7 2.6 %collective-permute-start.16 = (bf16[16,640]{1,0:T(8,128)(2,1)S(1)}, bf16[16,640]{1,0:T(8,128)(2,1)S(1)}, u32[]{:S(2)}, u32[]{:S(2)}) collective-permute-start(bf16[16,640]{1,0:T(8,128)(2,1)S(1)} %get-tuple-element.44), channel_id=1, source_target_pairs={{0,4},{2,6},{4,0},{6,2},{8,12},{10,14},{12,8},{14,10},{16,20},{18,... | collective-permute-start | bytes 61448 | tf_op jit(solution)/shard_map/ppermute | solution.py:325
  48.3 0.5 collective-permute-start.17
  48.8 1.2 %collective-permute-done.15 = bf16[16,640]{1,0:T(8,128)(2,1)S(1)} collective-permute-done((bf16[16,640]{1,0:T(8,128)(2,1)S(1)}, bf16[16,640]{1,0:T(8,128)(2,1)S(1)}, u32[]{:S(2)}, u32[]{:S(2)}) %collective-permute-start.15) | collective-permute-done | bytes 20512 | tf_op jit(solution)/shard_map/ppermute | solution.py:325
  50.0 1.0 %collective-permute-done.17 = bf16[16,640]{1,0:T(8,128)(2,1)S(1)} collective-permute-done((bf16[16,640]{1,0:T(8,128)(2,1)S(1)}, bf16[16,640]{1,0:T(8,128)(2,1)S(1)}, u32[]{:S(2)}, u32[]{:S(2)}) %collective-permute-start.17) | collective-permute-done | bytes 20512 | tf_op jit(solution)/shard_map/ppermute | solution.py:325
  51.0 2.0 %collective-permute-start.20 = (bf16[64,640]{1,0:T(8,128)(2,1)S(1)}, bf16[64,640]{1,0:T(8,128)(2,1)S(1)}, u32[]{:S(2)}, u32[]{:S(2)}) collective-permute-start(bf16[64,640]{1,0:T(8,128)(2,1)S(1)} %constant_dynamic-update-slice_fusion.4), channel_id=1, source_target_pairs={{0,24},{2,26},{4,28},{6,30},{8,0},{10,2},{12,4},{14,6},{16,8},{18,... | collective-permute-start | bytes 245768 | tf_op jit(solution)/shard_map/ppermute | solution.py:325
  53.0 0.8 %collective-permute-start.19 = (bf16[64,640]{1,0:T(8,128)(2,1)S(1)}, bf16[64,640]{1,0:T(8,128)(2,1)S(1)}, u32[]{:S(2)}, u32[]{:S(2)}) collective-permute-start(bf16[64,640]{1,0:T(8,128)(2,1)S(1)} %constant_dynamic-update-slice_fusion.4), channel_id=1, source_target_pairs={{0,16},{2,18},{4,20},{6,22},{8,24},{10,26},{12,28},{14,30},{16,0},... | collective-permute-start | bytes 245768 | tf_op jit(solution)/shard_map/ppermute | solution.py:325
  53.7 0.4 collective-permute-start.18
  54.2 4.4 %collective-permute-done.18 = bf16[64,640]{1,0:T(8,128)(2,1)S(1)} collective-permute-done((bf16[64,640]{1,0:T(8,128)(2,1)S(1)}, bf16[64,640]{1,0:T(8,128)(2,1)S(1)}, u32[]{:S(2)}, u32[]{:S(2)}) %collective-permute-start.18) | collective-permute-done | bytes 81952 | tf_op jit(solution)/shard_map/ppermute | solution.py:325
  58.7 4.8 %collective-permute-start.21 = (bf16[256,640]{1,0:T(8,128)(2,1)S(1)}, bf16[256,640]{1,0:T(8,128)(2,1)S(1)}, u32[]{:S(2)}, u32[]{:S(2)}) collective-permute-start(bf16[256,640]{1,0:T(8,128)(2,1)S(1)} %constant_dynamic-update-slice_fusion.slot_out), channel_id=1, source_target_pairs={{0,32},{32,0},{64,96},{96,64},{128,160},{160,128},{192,224},{224,1... | collective-permute-start | bytes 983048 | tf_op jit(solution)/shard_map/ppermute | solution.py:332
  63.5 1.8 %mix.2.refs_0_ = bf16[2048,1280]{1,0:T(8,128)(2,1)} custom-call(bf16[2048,256]{1,0:T(8,128)(2,1)S(1)} %get-tuple-element.30.after.combine, bf16[256,640]{1,0:T(8,128)(2,1)S(1)} %constant_dynamic-update-slice_fusion.slot_out), custom_call_target="tpu_custom_call" | custom-call | flops 671088640 | bytes 2621440 | tf_op jit(solution)/shard_map/mix/pallas_call | solution.py:439
  65.4 1.9 %mix.3 = bf16[2048,1280]{1,0:T(8,128)(2,1)} custom-call(bf16[2048,256]{1,0:T(8,128)(2,1)S(1)} %get-tuple-element.30.after.combine, bf16[256,640]{1,0:T(8,128)(2,1)S(1)} %collective-permute-done.21.slot_out, bf16[2048,1280]{1,0:T(8,128)(2,1)} %mix.2.refs_0_), custom_call_target="tpu_custom_call", output_to_operand_aliasing={{}: (2, {})} | custom-call | flops 671088640 | bytes 2621440 | tf_op jit(solution)/shard_map/mix/pallas_call | solution.py:439
  (17 shorter events, 0.3 us)
Async XLA Ops:
  4.8 4.7 %collective-permute-start = (bf16[256,768]{1,0:T(8,128)(2,1)S(1)}, bf16[256,768]{1,0:T(8,128)(2,1)S(1)}, u32[]{:S(2)}, u32[]{:S(2)}) collective-permute-start(bf16[256,768]{1,0:T(8,128)(2,1)S(1)} %get-tuple-element.27), channel_id=1, source_target_pairs={{0,32},{32,0},{64,96},{96,64},{128,160},{160,128},{192,224},{224,1... | collective-permute-start | bytes 1179656 | tf_op jit(solution)/shard_map/ppermute | solution.py:305
  9.8 5.8 %collective-permute-start.1 = (bf16[64,768]{1,0:T(8,128)(2,1)S(1)}, bf16[64,768]{1,0:T(8,128)(2,1)S(1)}, u32[]{:S(2)}, u32[]{:S(2)}) collective-permute-start(bf16[64,768]{1,0:T(8,128)(2,1)S(1)} %get-tuple-element.32), channel_id=1, source_target_pairs={{0,8},{2,10},{4,12},{6,14},{8,16},{10,18},{12,20},{14,22},{16,24},... | collective-permute-start | bytes 294920 | tf_op jit(solution)/shard_map/ppermute | solution.py:309
  9.9 6.8 %collective-permute-start.2 = (bf16[64,768]{1,0:T(8,128)(2,1)S(1)}, bf16[64,768]{1,0:T(8,128)(2,1)S(1)}, u32[]{:S(2)}, u32[]{:S(2)}) collective-permute-start(bf16[64,768]{1,0:T(8,128)(2,1)S(1)} %get-tuple-element.33), channel_id=1, source_target_pairs={{0,16},{2,18},{4,20},{6,22},{8,24},{10,26},{12,28},{14,30},{16,0},... | collective-permute-start | bytes 294920 | tf_op jit(solution)/shard_map/ppermute | solution.py:309
  12.1 5.4 %collective-permute-start.3 = (bf16[64,768]{1,0:T(8,128)(2,1)S(1)}, bf16[64,768]{1,0:T(8,128)(2,1)S(1)}, u32[]{:S(2)}, u32[]{:S(2)}) collective-permute-start(bf16[64,768]{1,0:T(8,128)(2,1)S(1)} %get-tuple-element.34), channel_id=1, source_target_pairs={{0,24},{2,26},{4,28},{6,30},{8,0},{10,2},{12,4},{14,6},{16,8},{18,... | collective-permute-start | bytes 294920 | tf_op jit(solution)/shard_map/ppermute | solution.py:309
  17.7 5.2 %collective-permute-start.4 = (f32[16,768]{1,0:T(8,128)S(1)}, f32[16,768]{1,0:T(8,128)S(1)}, u32[]{:S(2)}, u32[]{:S(2)}) collective-permute-start(f32[16,768]{1,0:T(8,128)S(1)} %get-tuple-element.36), channel_id=1, source_target_pairs={{0,2},{2,4},{4,6},{6,0},{8,10},{10,12},{12,14},{14,8},{16,18},{18,... | collective-permute-start | bytes 147464 | tf_op jit(solution)/shard_map/ppermute | solution.py:312
  18.7 4.7 %collective-permute-start.5 = (f32[16,768]{1,0:T(8,128)S(1)}, f32[16,768]{1,0:T(8,128)S(1)}, u32[]{:S(2)}, u32[]{:S(2)}) collective-permute-start(f32[16,768]{1,0:T(8,128)S(1)} %get-tuple-element.37), channel_id=1, source_target_pairs={{0,4},{2,6},{4,0},{6,2},{8,12},{10,14},{12,8},{14,10},{16,20},{18,... | collective-permute-start | bytes 147464 | tf_op jit(solution)/shard_map/ppermute | solution.py:312
  21.7 4.0 %collective-permute-start.6 = (f32[16,768]{1,0:T(8,128)S(1)}, f32[16,768]{1,0:T(8,128)S(1)}, u32[]{:S(2)}, u32[]{:S(2)}) collective-permute-start(f32[16,768]{1,0:T(8,128)S(1)} %get-tuple-element.38), channel_id=1, source_target_pairs={{0,6},{2,0},{4,2},{6,4},{8,14},{10,8},{12,10},{14,12},{16,22},{18,... | collective-permute-start | bytes 147464 | tf_op jit(solution)/shard_map/ppermute | solution.py:312
  25.8 3.7 %collective-permute-start.9 = (f32[16,768]{1,0:T(8,128)S(1)}, f32[16,768]{1,0:T(8,128)S(1)}, u32[]{:S(2)}, u32[]{:S(2)}) collective-permute-start(f32[16,768]{1,0:T(8,128)S(1)} %z_merge.1.own), channel_id=1, source_target_pairs={{0,192},{32,224},{64,0},{96,32},{128,64},{160,96},{192,128},{224,1... | collective-permute-start | bytes 147464 | tf_op jit(solution)/shard_map/ppermute | solution.py:314
  28.3 4.5 %collective-permute-start.8 = (f32[16,768]{1,0:T(8,128)S(1)}, f32[16,768]{1,0:T(8,128)S(1)}, u32[]{:S(2)}, u32[]{:S(2)}) collective-permute-start(f32[16,768]{1,0:T(8,128)S(1)} %z_merge.1.own), channel_id=1, source_target_pairs={{0,128},{32,160},{64,192},{96,224},{128,0},{160,32},{192,64},{224,... | collective-permute-start | bytes 147464 | tf_op jit(solution)/shard_map/ppermute | solution.py:314
  28.8 4.5 %collective-permute-start.7 = (f32[16,768]{1,0:T(8,128)S(1)}, f32[16,768]{1,0:T(8,128)S(1)}, u32[]{:S(2)}, u32[]{:S(2)}) collective-permute-start(f32[16,768]{1,0:T(8,128)S(1)} %z_merge.1.own), channel_id=1, source_target_pairs={{0,64},{32,96},{64,128},{96,160},{128,192},{160,224},{192,0},{224,... | collective-permute-start | bytes 147464 | tf_op jit(solution)/shard_map/ppermute | solution.py:314
  33.4 4.4 %collective-permute-start.10 = (bf16[16,640]{1,0:T(8,128)(2,1)S(1)}, bf16[16,640]{1,0:T(8,128)(2,1)S(1)}, u32[]{:S(2)}, u32[]{:S(2)}) collective-permute-start(bf16[16,640]{1,0:T(8,128)(2,1)S(1)} %x_merge.1.slot_own), channel_id=1, source_target_pairs={{0,32},{32,0},{64,96},{96,64},{128,160},{160,128},{192,224},{224,1... | collective-permute-start | bytes 61448 | tf_op jit(solution)/shard_map/ppermute | solution.py:316
  38.4 1.3 %collective-permute-start.11 = (f32[16,640]{1,0:T(8,128)S(1)}, f32[16,640]{1,0:T(8,128)S(1)}, u32[]{:S(2)}, u32[]{:S(2)}) collective-permute-start(f32[16,640]{1,0:T(8,128)S(1)} %get-tuple-element.42), channel_id=1, source_target_pairs={{0,32},{32,0},{64,96},{96,64},{128,160},{160,128},{192,224},{224,1... | collective-permute-start | bytes 122888 | tf_op jit(solution)/shard_map/ppermute | solution.py:318
  39.7 2.9 %collective-permute-start.14 = (f32[16,640]{1,0:T(8,128)S(1)}, f32[16,640]{1,0:T(8,128)S(1)}, u32[]{:S(2)}, u32[]{:S(2)}) collective-permute-start(f32[16,640]{1,0:T(8,128)S(1)} %add.67), channel_id=1, source_target_pairs={{0,192},{32,224},{64,0},{96,32},{128,64},{160,96},{192,128},{224,1... | collective-permute-start | bytes 122888 | tf_op jit(solution)/shard_map/ppermute | solution.py:319
  40.0 4.4 %collective-permute-start.13 = (f32[16,640]{1,0:T(8,128)S(1)}, f32[16,640]{1,0:T(8,128)S(1)}, u32[]{:S(2)}, u32[]{:S(2)}) collective-permute-start(f32[16,640]{1,0:T(8,128)S(1)} %add.67), channel_id=1, source_target_pairs={{0,128},{32,160},{64,192},{96,224},{128,0},{160,32},{192,64},{224,... | collective-permute-start | bytes 122888 | tf_op jit(solution)/shard_map/ppermute | solution.py:319
  41.1 4.4 %collective-permute-start.12 = (f32[16,640]{1,0:T(8,128)S(1)}, f32[16,640]{1,0:T(8,128)S(1)}, u32[]{:S(2)}, u32[]{:S(2)}) collective-permute-start(f32[16,640]{1,0:T(8,128)S(1)} %add.67), channel_id=1, source_target_pairs={{0,64},{32,96},{64,128},{96,160},{128,192},{160,224},{192,0},{224,... | collective-permute-start | bytes 122888 | tf_op jit(solution)/shard_map/ppermute | solution.py:319
  45.5 4.5 %collective-permute-start.15 = (bf16[16,640]{1,0:T(8,128)(2,1)S(1)}, bf16[16,640]{1,0:T(8,128)(2,1)S(1)}, u32[]{:S(2)}, u32[]{:S(2)}) collective-permute-start(bf16[16,640]{1,0:T(8,128)(2,1)S(1)} %get-tuple-element.44), channel_id=1, source_target_pairs={{0,2},{2,4},{4,6},{6,0},{8,10},{10,12},{12,14},{14,8},{16,18},{18,... | collective-permute-start | bytes 61448 | tf_op jit(solution)/shard_map/ppermute | solution.py:325
  45.7 4.3 %collective-permute-start.16 = (bf16[16,640]{1,0:T(8,128)(2,1)S(1)}, bf16[16,640]{1,0:T(8,128)(2,1)S(1)}, u32[]{:S(2)}, u32[]{:S(2)}) collective-permute-start(bf16[16,640]{1,0:T(8,128)(2,1)S(1)} %get-tuple-element.44), channel_id=1, source_target_pairs={{0,4},{2,6},{4,0},{6,2},{8,12},{10,14},{12,8},{14,10},{16,20},{18,... | collective-permute-start | bytes 61448 | tf_op jit(solution)/shard_map/ppermute | solution.py:325
  48.3 2.6 %collective-permute-start.17 = (bf16[16,640]{1,0:T(8,128)(2,1)S(1)}, bf16[16,640]{1,0:T(8,128)(2,1)S(1)}, u32[]{:S(2)}, u32[]{:S(2)}) collective-permute-start(bf16[16,640]{1,0:T(8,128)(2,1)S(1)} %get-tuple-element.44), channel_id=1, source_target_pairs={{0,6},{2,0},{4,2},{6,4},{8,14},{10,8},{12,10},{14,12},{16,22},{18,... | collective-permute-start | bytes 61448 | tf_op jit(solution)/shard_map/ppermute | solution.py:325
  51.0 7.7 %collective-permute-start.20 = (bf16[64,640]{1,0:T(8,128)(2,1)S(1)}, bf16[64,640]{1,0:T(8,128)(2,1)S(1)}, u32[]{:S(2)}, u32[]{:S(2)}) collective-permute-start(bf16[64,640]{1,0:T(8,128)(2,1)S(1)} %constant_dynamic-update-slice_fusion.4), channel_id=1, source_target_pairs={{0,24},{2,26},{4,28},{6,30},{8,0},{10,2},{12,4},{14,6},{16,8},{18,... | collective-permute-start | bytes 245768 | tf_op jit(solution)/shard_map/ppermute | solution.py:325
  53.0 5.7 %collective-permute-start.19 = (bf16[64,640]{1,0:T(8,128)(2,1)S(1)}, bf16[64,640]{1,0:T(8,128)(2,1)S(1)}, u32[]{:S(2)}, u32[]{:S(2)}) collective-permute-start(bf16[64,640]{1,0:T(8,128)(2,1)S(1)} %constant_dynamic-update-slice_fusion.4), channel_id=1, source_target_pairs={{0,16},{2,18},{4,20},{6,22},{8,24},{10,26},{12,28},{14,30},{16,0},... | collective-permute-start | bytes 245768 | tf_op jit(solution)/shard_map/ppermute | solution.py:325
  53.7 4.9 %collective-permute-start.18 = (bf16[64,640]{1,0:T(8,128)(2,1)S(1)}, bf16[64,640]{1,0:T(8,128)(2,1)S(1)}, u32[]{:S(2)}, u32[]{:S(2)}) collective-permute-start(bf16[64,640]{1,0:T(8,128)(2,1)S(1)} %constant_dynamic-update-slice_fusion.4), channel_id=1, source_target_pairs={{0,8},{2,10},{4,12},{6,14},{8,16},{10,18},{12,20},{14,22},{16,24},... | collective-permute-start | bytes 245768 | tf_op jit(solution)/shard_map/ppermute | solution.py:325
  58.7 6.7 %collective-permute-start.21 = (bf16[256,640]{1,0:T(8,128)(2,1)S(1)}, bf16[256,640]{1,0:T(8,128)(2,1)S(1)}, u32[]{:S(2)}, u32[]{:S(2)}) collective-permute-start(bf16[256,640]{1,0:T(8,128)(2,1)S(1)} %constant_dynamic-update-slice_fusion.slot_out), channel_id=1, source_target_pairs={{0,32},{32,0},{64,96},{96,64},{128,160},{160,128},{192,224},{224,1... | collective-permute-start | bytes 983048 | tf_op jit(solution)/shard_map/ppermute | solution.py:332

commit v5 on v4

--- a/solution.py
+++ b/solution.py
@@ -15,7 +15,8 @@
 
 
 def _core():
-    return lax.rem(lax.axis_index("seq"), 2)
+    seq = lax.axis_index("seq")
+    return lax.rem(seq + lax.div(seq, 2) + _y(), 2)
 
 
 def _y():
@@ -31,11 +32,15 @@
 
 
 def _x_perm(k):
-    return [(s, ((s // 2 + k) % 4) * 2 + s % 2) for s in range(8)]
+    return [(s, ((s // 2 + k) % 4) * 2 + (s + k) % 2) for s in range(8)]
 
 
 def _y_perm(k):
-    return [(e, ((e // 4 + k) % 4) * 4 + e % 4) for e in range(16)]
+    return [
+        (s * 16 + e, (s ^ (k & 1)) * 16 + ((e // 4 + k) % 4) * 4 + e % 4)
+        for s in range(8)
+        for e in range(16)
+    ]
 
 
 def _z_perm(k):
@@ -306,7 +311,7 @@
     own = own_sums(tok, dispatch, stat)
 
     own, stat, *send = core_merge(own, stat, got)
-    got = [lax.ppermute(v, "exp", _y_perm(k + 1)) for k, v in enumerate(send)]
+    got = [lax.ppermute(v, ("seq", "exp"), _y_perm(k + 1)) for k, v in enumerate(send)]
     combine, w_in, w_out = combine_weights(own, logits, w_in[0], w_out[0])
     own, *send = y_merge(combine, own, stat, *got)
     got = [lax.ppermute(v, "exp", _z_perm(k + 1)) for k, v in enumerate(send)]
@@ -319,16 +324,16 @@
     whole = part + sum(lax.ppermute(part, "seq", _x_perm(k)) for k in range(1, 4))
     out = whole.astype(BF16)
 
-    def gather(block, index, perm):
+    def gather(block, index, axes, perm):
         n = block.shape[0]
         res = jnp.zeros((4 * n, block.shape[1]), block.dtype)
-        blocks = [block] + [lax.ppermute(block, "exp", perm(k)) for k in range(1, 4)]
+        blocks = [block] + [lax.ppermute(block, axes, perm(k)) for k in range(1, 4)]
         for k, g in enumerate(blocks):
             res = lax.dynamic_update_slice_in_dim(res, g, ((index - k) % 4) * n, 0)
         return res
 
-    out = gather(out, z, _z_perm)
-    out = gather(out, y, _y_perm)
+    out = gather(out, z, "exp", _z_perm)
+    out = gather(out, y, ("seq", "exp"), _y_perm)
     other = lax.ppermute(out, "seq", _core_perm())
     mixed = mix(combine, out)
     return mix(combine, other, mixed)

time: 67.5 us -> 66.7 us (0.988)
  starting transfers between devices: 32.2 us -> 28.1 us
  waiting for transfers between devices: 21.7 us -> 25.2 us
    ppermute x1, starting transfers between devices: 4.83 us -> 0.33 us  [body(): other = lax.ppermute(out, 'seq', _core_perm())]
    ppermute x1, starting transfers between devices: 3.55 us -> 0.66 us  [body(): got = lax.ppermute(slot_half, 'seq', _core_perm())]
    ppermute x9, starting transfers between devices: 9.65 us -> 11.8 us  [the longest x6 7.9 us: gather(): blocks = [block] + [lax.ppermute(block, axes, perm(k)) for k in range(1, 4)]]
    ppermute x9, waiting for transfers between devices: 8.96 us -> 10.9 us  [the longest x6 7.98 us: gather(): blocks = [block] + [lax.ppermute(block, axes, perm(k)) for k in range(1, 4)]]
    ppermute x3, starting transfers between devices: 3.67 us -> 5.04 us  [body(): got = [lax.ppermute(own, 'seq', _x_perm(k)) for k in range(1, 4)]]
    ppermute x3, waiting for transfers between devices: 3.6 us -> 4.55 us  [body(): lax.ppermute(part, 'seq', _x_perm(k))]
    ppermute x3, waiting for transfers between devices: 3.85 us -> 4.69 us  [body(): got = [lax.ppermute(own, 'seq', _x_perm(k)) for k in range(1, 4)]]
  transfers between devices with their start and end apart: 22 -> 22, of which waited for: 18 -> 17; matrix products, arithmetic and copies ran while one was open for 0% -> 0% of each run, Pallas kernels for 7% -> 7%
where the time goes in v5:
time: 66.7 us
  starting transfers between devices  28.1 us (42%)
  waiting for transfers between devices  25.2 us (38%)
  Pallas kernels  12.8 us (19%)
    ppermute x6, waiting for transfers between devices, gather(): blocks = [block] + [lax.ppermute(block, axes, perm(k)) for k in range(1, 4)]  7.98 us
    ppermute x6, starting transfers between devices, gather(): blocks = [block] + [lax.ppermute(block, axes, perm(k)) for k in range(1, 4)]  7.9 us
    ppermute x3, starting transfers between devices, body(): got = [lax.ppermute(own, 'seq', _x_perm(k)) for k in range(1, 4)]  5.04 us
    pallas_call x1, Pallas kernels, first(): _call(functools.partial(first_kernel, CHUNKS), 'logits_and_sums', [pltpu....  4.76 us
    ppermute x3, waiting for transfers between devices, body(): got = [lax.ppermute(own, 'seq', _x_perm(k)) for k in range(1, 4)]  4.69 us
    ppermute x3, waiting for transfers between devices, body(): lax.ppermute(part, 'seq', _x_perm(k))  4.55 us
    ppermute x3, starting transfers between devices, body(): got = [lax.ppermute(v, 'exp', _z_perm(k + 1)) for k, v in enumerate(send)]  4.3 us
    ppermute x3, starting transfers between devices, body(): lax.ppermute(v, ('seq', 'exp'), _y_perm(k + 1))  3.9 us
  transfers between devices with their start and end apart: 22, of which 17 were waited for; matrix products, arithmetic and copies ran while one was open for 0% of the time, Pallas kernels for 7%

profile of v5, /device:TPU:1, one launch (start us, length us, event | category | flops | bytes accessed | tf_op | source)
XLA Modules:
  0.0 66.7 jit_solution(11795191818881203283)
XLA Ops:
  0.0 4.8 %logits_and_sums.1 = (bf16[2048,1280]{1,0:T(8,128)(2,1)S(1)}, f32[256,2048]{1,0:T(8,128)S(1)}, bf16[256,2048]{1,0:T(8,128)(2,1)S(1)}, bf16[256,768]{1,0:T(8,128)(2,1)S(1)}, f32[256,768]{1,0:T(8,128)S(1)}) custom-call(bf16[2048,1280]{1,0:T(8,128)(2,1)} %tok_hbm.1, bf16[1280,256]{1,0:T(8,128)(2,1)} %keys_hbm.1), custom_call_target="tpu_custom_call" | custom-call | flops 2013265920 | bytes 5242880 | tf_op jit(solution)/shard_map/logits_and_sums/pallas_call | solution.py:349
  4.8 3.4 %collective-permute-start = (bf16[256,768]{1,0:T(8,128)(2,1)S(1)}, bf16[256,768]{1,0:T(8,128)(2,1)S(1)}, u32[]{:S(2)}, u32[]{:S(2)}) collective-permute-start(bf16[256,768]{1,0:T(8,128)(2,1)S(1)} %get-tuple-element.27), channel_id=1, source_target_pairs={{0,32},{32,0},{64,96},{96,64},{128,160},{160,128},{192,224},{224,1... | collective-permute-start | bytes 1179656 | tf_op jit(solution)/shard_map/ppermute | solution.py:310
  8.1 1.0 %own_sums.1.own = f32[256,640]{1,0:T(8,128)S(1)} custom-call(bf16[2048,1280]{1,0:T(8,128)(2,1)S(1)} %get-tuple-element.24.tok, bf16[256,2048]{1,0:T(8,128)(2,1)S(1)} %get-tuple-element.25.dispatch, f32[256,768]{1,0:T(8,128)S(1)} %get-tuple-element.26.stat), custom_call_target="tpu_custom_call" | custom-call | flops 671088640 | tf_op jit(solution)/shard_map/own_sums/pallas_call | solution.py:372
  9.2 0.3 collective-permute-done.got
  9.5 0.3 core_merge.1
  9.8 0.1 collective-permute-start.1
  9.9 2.4 %collective-permute-start.2 = (bf16[64,768]{1,0:T(8,128)(2,1)S(1)}, bf16[64,768]{1,0:T(8,128)(2,1)S(1)}, u32[]{:S(2)}, u32[]{:S(2)}) collective-permute-start(bf16[64,768]{1,0:T(8,128)(2,1)S(1)} %get-tuple-element.33), channel_id=1, source_target_pairs={{0,16},{2,18},{4,20},{6,22},{8,24},{10,26},{12,28},{14,30},{16,0},... | collective-permute-start | bytes 294920 | tf_op jit(solution)/shard_map/ppermute | solution.py:314
  12.3 1.4 %collective-permute-start.3 = (bf16[64,768]{1,0:T(8,128)(2,1)S(1)}, bf16[64,768]{1,0:T(8,128)(2,1)S(1)}, u32[]{:S(2)}, u32[]{:S(2)}) collective-permute-start(bf16[64,768]{1,0:T(8,128)(2,1)S(1)} %get-tuple-element.34), channel_id=1, source_target_pairs={{0,56},{2,58},{4,60},{6,62},{8,32},{10,34},{12,36},{14,38},{16,40}... | collective-permute-start | bytes 294920 | tf_op jit(solution)/shard_map/ppermute | solution.py:314
  13.7 1.9 %combine.1 = (bf16[2048,256]{1,0:T(8,128)(2,1)S(1)}, bf16[1280,640]{1,0:T(8,128)(2,1)S(1)}, bf16[640,1280]{1,0:T(8,128)(2,1)S(1)}) custom-call(f32[64,640]{1,0:T(8,128)S(1)} %get-tuple-element.28.after.own, f32[256,2048]{1,0:T(8,128)S(1)} %get-tuple-element.29.logits, bf16[1280,640]{1,0:T(8,128)(2,1)} %bitcast.2, bf16[640,1280]{1,0:T(8,128)(2,1)} %bitcast.3), custom_call_target="tpu_custom_call" | custom-call | flops 5242880 | bytes 3276800 | tf_op jit(solution)/shard_map/combine/pallas_call | solution.py:384
  15.7 2.3 %collective-permute-done.1.got1 = bf16[64,768]{1,0:T(8,128)(2,1)S(1)} collective-permute-done((bf16[64,768]{1,0:T(8,128)(2,1)S(1)}, bf16[64,768]{1,0:T(8,128)(2,1)S(1)}, u32[]{:S(2)}, u32[]{:S(2)}) %collective-permute-start.1) | collective-permute-done | bytes 98336 | tf_op jit(solution)/shard_map/ppermute | solution.py:314
  18.0 0.6 collective-permute-done.3.got3
  18.6 0.2 y_merge.1
  18.8 0.6 collective-permute-start.4
  19.4 3.0 %collective-permute-start.5 = (f32[16,768]{1,0:T(8,128)S(1)}, f32[16,768]{1,0:T(8,128)S(1)}, u32[]{:S(2)}, u32[]{:S(2)}) collective-permute-start(f32[16,768]{1,0:T(8,128)S(1)} %get-tuple-element.37), channel_id=1, source_target_pairs={{0,4},{2,6},{4,0},{6,2},{8,12},{10,14},{12,8},{14,10},{16,20},{18,... | collective-permute-start | bytes 147464 | tf_op jit(solution)/shard_map/ppermute | solution.py:317
  22.4 0.7 %collective-permute-start.6 = (f32[16,768]{1,0:T(8,128)S(1)}, f32[16,768]{1,0:T(8,128)S(1)}, u32[]{:S(2)}, u32[]{:S(2)}) collective-permute-start(f32[16,768]{1,0:T(8,128)S(1)} %get-tuple-element.38), channel_id=1, source_target_pairs={{0,6},{2,0},{4,2},{6,4},{8,14},{10,8},{12,10},{14,12},{16,22},{18,... | collective-permute-start | bytes 147464 | tf_op jit(solution)/shard_map/ppermute | solution.py:317
  23.1 0.5 collective-permute-done.4.got1
  23.6 2.1 %collective-permute-done.5.got2 = f32[16,768]{1,0:T(8,128)S(1)} collective-permute-done((f32[16,768]{1,0:T(8,128)S(1)}, f32[16,768]{1,0:T(8,128)S(1)}, u32[]{:S(2)}, u32[]{:S(2)}) %collective-permute-start.5) | collective-permute-done | bytes 49184 | tf_op jit(solution)/shard_map/ppermute | solution.py:317
  25.7 0.5 collective-permute-done.6.got3
  26.2 0.1 z_merge.1.own
  26.3 4.1 %collective-permute-start.9 = (f32[16,768]{1,0:T(8,128)S(1)}, f32[16,768]{1,0:T(8,128)S(1)}, u32[]{:S(2)}, u32[]{:S(2)}) collective-permute-start(f32[16,768]{1,0:T(8,128)S(1)} %z_merge.1.own), channel_id=1, source_target_pairs={{0,224},{32,192},{64,32},{96,0},{128,96},{160,64},{192,160},{224,1... | collective-permute-start | bytes 147464 | tf_op jit(solution)/shard_map/ppermute | solution.py:319
  30.4 0.5 collective-permute-start.8
  30.9 0.4 collective-permute-start.7
  31.3 0.2 collective-permute-done.9.got3
  31.5 3.7 %collective-permute-done.8.got2 = f32[16,768]{1,0:T(8,128)S(1)} collective-permute-done((f32[16,768]{1,0:T(8,128)S(1)}, f32[16,768]{1,0:T(8,128)S(1)}, u32[]{:S(2)}, u32[]{:S(2)}) %collective-permute-start.8) | collective-permute-done | bytes 49184 | tf_op jit(solution)/shard_map/ppermute | solution.py:319
  35.2 0.8 %collective-permute-done.7.got1 = f32[16,768]{1,0:T(8,128)S(1)} collective-permute-done((f32[16,768]{1,0:T(8,128)S(1)}, f32[16,768]{1,0:T(8,128)S(1)}, u32[]{:S(2)}, u32[]{:S(2)}) %collective-permute-start.7) | collective-permute-done | bytes 49184 | tf_op jit(solution)/shard_map/ppermute | solution.py:319
  36.0 0.1 x_merge.1.slot_own
  36.1 0.7 collective-permute-start.10
  36.8 0.8 %collective-permute-done.10.slot_other = bf16[16,640]{1,0:T(8,128)(2,1)S(1)} collective-permute-done((bf16[16,640]{1,0:T(8,128)(2,1)S(1)}, bf16[16,640]{1,0:T(8,128)(2,1)S(1)}, u32[]{:S(2)}, u32[]{:S(2)}) %collective-permute-start.10) | collective-permute-done | bytes 20512 | tf_op jit(solution)/shard_map/ppermute | solution.py:321
  37.6 0.6 expert.1
  38.3 0.4 collective-permute-start.11
  38.7 0.9 %collective-permute-done.11 = f32[16,640]{1,0:T(8,128)S(1)} collective-permute-done((f32[16,640]{1,0:T(8,128)S(1)}, f32[16,640]{1,0:T(8,128)S(1)}, u32[]{:S(2)}, u32[]{:S(2)}) %collective-permute-start.11) | collective-permute-done | bytes 40992 | tf_op jit(solution)/shard_map/ppermute | solution.py:323
  39.6 0.7 collective-permute-start.14
  40.2 0.7 %collective-permute-start.13 = (f32[16,640]{1,0:T(8,128)S(1)}, f32[16,640]{1,0:T(8,128)S(1)}, u32[]{:S(2)}, u32[]{:S(2)}) collective-permute-start(f32[16,640]{1,0:T(8,128)S(1)} %add.67), channel_id=1, source_target_pairs={{0,128},{32,160},{64,192},{96,224},{128,0},{160,32},{192,64},{224,... | collective-permute-start | bytes 122888 | tf_op jit(solution)/shard_map/ppermute | solution.py:324
  41.0 0.8 %collective-permute-start.12 = (f32[16,640]{1,0:T(8,128)S(1)}, f32[16,640]{1,0:T(8,128)S(1)}, u32[]{:S(2)}, u32[]{:S(2)}) collective-permute-start(f32[16,640]{1,0:T(8,128)S(1)} %add.67), channel_id=1, source_target_pairs={{0,96},{32,64},{64,160},{96,128},{128,224},{160,192},{192,32},{224... | collective-permute-start | bytes 122888 | tf_op jit(solution)/shard_map/ppermute | solution.py:324
  41.8 1.6 %collective-permute-done.14 = f32[16,640]{1,0:T(8,128)S(1)} collective-permute-done((f32[16,640]{1,0:T(8,128)S(1)}, f32[16,640]{1,0:T(8,128)S(1)}, u32[]{:S(2)}, u32[]{:S(2)}) %collective-permute-start.14) | collective-permute-done | bytes 40992 | tf_op jit(solution)/shard_map/ppermute | solution.py:324
  43.4 1.2 %collective-permute-done.13 = f32[16,640]{1,0:T(8,128)S(1)} collective-permute-done((f32[16,640]{1,0:T(8,128)S(1)}, f32[16,640]{1,0:T(8,128)S(1)}, u32[]{:S(2)}, u32[]{:S(2)}) %collective-permute-start.13) | collective-permute-done | bytes 40992 | tf_op jit(solution)/shard_map/ppermute | solution.py:324
  44.6 1.8 %collective-permute-done.12 = f32[16,640]{1,0:T(8,128)S(1)} collective-permute-done((f32[16,640]{1,0:T(8,128)S(1)}, f32[16,640]{1,0:T(8,128)S(1)}, u32[]{:S(2)}, u32[]{:S(2)}) %collective-permute-start.12) | collective-permute-done | bytes 40992 | tf_op jit(solution)/shard_map/ppermute | solution.py:324
  46.4 0.6 collective-permute-start.15
  47.0 2.2 %collective-permute-start.16 = (bf16[16,640]{1,0:T(8,128)(2,1)S(1)}, bf16[16,640]{1,0:T(8,128)(2,1)S(1)}, u32[]{:S(2)}, u32[]{:S(2)}) collective-permute-start(bf16[16,640]{1,0:T(8,128)(2,1)S(1)} %get-tuple-element.44), channel_id=1, source_target_pairs={{0,4},{2,6},{4,0},{6,2},{8,12},{10,14},{12,8},{14,10},{16,20},{18,... | collective-permute-start | bytes 61448 | tf_op jit(solution)/shard_map/ppermute | solution.py:330
  49.2 0.5 collective-permute-start.17
  49.7 1.2 %collective-permute-done.15 = bf16[16,640]{1,0:T(8,128)(2,1)S(1)} collective-permute-done((bf16[16,640]{1,0:T(8,128)(2,1)S(1)}, bf16[16,640]{1,0:T(8,128)(2,1)S(1)}, u32[]{:S(2)}, u32[]{:S(2)}) %collective-permute-start.15) | collective-permute-done | bytes 20512 | tf_op jit(solution)/shard_map/ppermute | solution.py:330
  50.9 1.3 %collective-permute-done.17 = bf16[16,640]{1,0:T(8,128)(2,1)S(1)} collective-permute-done((bf16[16,640]{1,0:T(8,128)(2,1)S(1)}, bf16[16,640]{1,0:T(8,128)(2,1)S(1)}, u32[]{:S(2)}, u32[]{:S(2)}) %collective-permute-start.17) | collective-permute-done | bytes 20512 | tf_op jit(solution)/shard_map/ppermute | solution.py:330
  52.2 3.3 %collective-permute-start.20 = (bf16[64,640]{1,0:T(8,128)(2,1)S(1)}, bf16[64,640]{1,0:T(8,128)(2,1)S(1)}, u32[]{:S(2)}, u32[]{:S(2)}) collective-permute-start(bf16[64,640]{1,0:T(8,128)(2,1)S(1)} %constant_dynamic-update-slice_fusion.4), channel_id=1, source_target_pairs={{0,56},{2,58},{4,60},{6,62},{8,32},{10,34},{12,36},{14,38},{16,40}... | collective-permute-start | bytes 245768 | tf_op jit(solution)/shard_map/ppermute | solution.py:330
  55.5 1.3 %collective-permute-start.19 = (bf16[64,640]{1,0:T(8,128)(2,1)S(1)}, bf16[64,640]{1,0:T(8,128)(2,1)S(1)}, u32[]{:S(2)}, u32[]{:S(2)}) collective-permute-start(bf16[64,640]{1,0:T(8,128)(2,1)S(1)} %constant_dynamic-update-slice_fusion.4), channel_id=1, source_target_pairs={{0,16},{2,18},{4,20},{6,22},{8,24},{10,26},{12,28},{14,30},{16,0},... | collective-permute-start | bytes 245768 | tf_op jit(solution)/shard_map/ppermute | solution.py:330
  56.8 5.5 %collective-permute-done.18 = bf16[64,640]{1,0:T(8,128)(2,1)S(1)} collective-permute-done((bf16[64,640]{1,0:T(8,128)(2,1)S(1)}, bf16[64,640]{1,0:T(8,128)(2,1)S(1)}, u32[]{:S(2)}, u32[]{:S(2)}) %collective-permute-start.18) | collective-permute-done | bytes 81952 | tf_op jit(solution)/shard_map/ppermute | solution.py:330
  62.4 0.3 collective-permute-start.21
  62.8 1.8 %mix.2.refs_0_ = bf16[2048,1280]{1,0:T(8,128)(2,1)} custom-call(bf16[2048,256]{1,0:T(8,128)(2,1)S(1)} %get-tuple-element.30.after.combine, bf16[256,640]{1,0:T(8,128)(2,1)S(1)} %constant_dynamic-update-slice_fusion.slot_out), custom_call_target="tpu_custom_call" | custom-call | flops 671088640 | bytes 2621440 | tf_op jit(solution)/shard_map/mix/pallas_call | solution.py:444
  64.6 1.9 %mix.3 = bf16[2048,1280]{1,0:T(8,128)(2,1)} custom-call(bf16[2048,256]{1,0:T(8,128)(2,1)S(1)} %get-tuple-element.30.after.combine, bf16[256,640]{1,0:T(8,128)(2,1)S(1)} %collective-permute-done.21.slot_out, bf16[2048,1280]{1,0:T(8,128)(2,1)} %mix.2.refs_0_), custom_call_target="tpu_custom_call", output_to_operand_aliasing={{}: (2, {})} | custom-call | flops 671088640 | bytes 2621440 | tf_op jit(solution)/shard_map/mix/pallas_call | solution.py:444
  (17 shorter events, 0.2 us)
Async XLA Ops:
  4.8 4.7 %collective-permute-start = (bf16[256,768]{1,0:T(8,128)(2,1)S(1)}, bf16[256,768]{1,0:T(8,128)(2,1)S(1)}, u32[]{:S(2)}, u32[]{:S(2)}) collective-permute-start(bf16[256,768]{1,0:T(8,128)(2,1)S(1)} %get-tuple-element.27), channel_id=1, source_target_pairs={{0,32},{32,0},{64,96},{96,64},{128,160},{160,128},{192,224},{224,1... | collective-permute-start | bytes 1179656 | tf_op jit(solution)/shard_map/ppermute | solution.py:310
  9.8 8.2 %collective-permute-start.1 = (bf16[64,768]{1,0:T(8,128)(2,1)S(1)}, bf16[64,768]{1,0:T(8,128)(2,1)S(1)}, u32[]{:S(2)}, u32[]{:S(2)}) collective-permute-start(bf16[64,768]{1,0:T(8,128)(2,1)S(1)} %get-tuple-element.32), channel_id=1, source_target_pairs={{0,40},{2,42},{4,44},{6,46},{8,48},{10,50},{12,52},{14,54},{16,56}... | collective-permute-start | bytes 294920 | tf_op jit(solution)/shard_map/ppermute | solution.py:314
  9.9 8.1 %collective-permute-start.2 = (bf16[64,768]{1,0:T(8,128)(2,1)S(1)}, bf16[64,768]{1,0:T(8,128)(2,1)S(1)}, u32[]{:S(2)}, u32[]{:S(2)}) collective-permute-start(bf16[64,768]{1,0:T(8,128)(2,1)S(1)} %get-tuple-element.33), channel_id=1, source_target_pairs={{0,16},{2,18},{4,20},{6,22},{8,24},{10,26},{12,28},{14,30},{16,0},... | collective-permute-start | bytes 294920 | tf_op jit(solution)/shard_map/ppermute | solution.py:314
  12.3 6.3 %collective-permute-start.3 = (bf16[64,768]{1,0:T(8,128)(2,1)S(1)}, bf16[64,768]{1,0:T(8,128)(2,1)S(1)}, u32[]{:S(2)}, u32[]{:S(2)}) collective-permute-start(bf16[64,768]{1,0:T(8,128)(2,1)S(1)} %get-tuple-element.34), channel_id=1, source_target_pairs={{0,56},{2,58},{4,60},{6,62},{8,32},{10,34},{12,36},{14,38},{16,40}... | collective-permute-start | bytes 294920 | tf_op jit(solution)/shard_map/ppermute | solution.py:314
  18.8 4.8 %collective-permute-start.4 = (f32[16,768]{1,0:T(8,128)S(1)}, f32[16,768]{1,0:T(8,128)S(1)}, u32[]{:S(2)}, u32[]{:S(2)}) collective-permute-start(f32[16,768]{1,0:T(8,128)S(1)} %get-tuple-element.36), channel_id=1, source_target_pairs={{0,2},{2,4},{4,6},{6,0},{8,10},{10,12},{12,14},{14,8},{16,18},{18,... | collective-permute-start | bytes 147464 | tf_op jit(solution)/shard_map/ppermute | solution.py:317
  19.4 6.3 %collective-permute-start.5 = (f32[16,768]{1,0:T(8,128)S(1)}, f32[16,768]{1,0:T(8,128)S(1)}, u32[]{:S(2)}, u32[]{:S(2)}) collective-permute-start(f32[16,768]{1,0:T(8,128)S(1)} %get-tuple-element.37), channel_id=1, source_target_pairs={{0,4},{2,6},{4,0},{6,2},{8,12},{10,14},{12,8},{14,10},{16,20},{18,... | collective-permute-start | bytes 147464 | tf_op jit(solution)/shard_map/ppermute | solution.py:317
  22.4 3.8 %collective-permute-start.6 = (f32[16,768]{1,0:T(8,128)S(1)}, f32[16,768]{1,0:T(8,128)S(1)}, u32[]{:S(2)}, u32[]{:S(2)}) collective-permute-start(f32[16,768]{1,0:T(8,128)S(1)} %get-tuple-element.38), channel_id=1, source_target_pairs={{0,6},{2,0},{4,2},{6,4},{8,14},{10,8},{12,10},{14,12},{16,22},{18,... | collective-permute-start | bytes 147464 | tf_op jit(solution)/shard_map/ppermute | solution.py:317
  26.3 5.3 %collective-permute-start.9 = (f32[16,768]{1,0:T(8,128)S(1)}, f32[16,768]{1,0:T(8,128)S(1)}, u32[]{:S(2)}, u32[]{:S(2)}) collective-permute-start(f32[16,768]{1,0:T(8,128)S(1)} %z_merge.1.own), channel_id=1, source_target_pairs={{0,224},{32,192},{64,32},{96,0},{128,96},{160,64},{192,160},{224,1... | collective-permute-start | bytes 147464 | tf_op jit(solution)/shard_map/ppermute | solution.py:319
  30.4 4.9 %collective-permute-start.8 = (f32[16,768]{1,0:T(8,128)S(1)}, f32[16,768]{1,0:T(8,128)S(1)}, u32[]{:S(2)}, u32[]{:S(2)}) collective-permute-start(f32[16,768]{1,0:T(8,128)S(1)} %z_merge.1.own), channel_id=1, source_target_pairs={{0,128},{32,160},{64,192},{96,224},{128,0},{160,32},{192,64},{224,... | collective-permute-start | bytes 147464 | tf_op jit(solution)/shard_map/ppermute | solution.py:319
  30.9 5.1 %collective-permute-start.7 = (f32[16,768]{1,0:T(8,128)S(1)}, f32[16,768]{1,0:T(8,128)S(1)}, u32[]{:S(2)}, u32[]{:S(2)}) collective-permute-start(f32[16,768]{1,0:T(8,128)S(1)} %z_merge.1.own), channel_id=1, source_target_pairs={{0,96},{32,64},{64,160},{96,128},{128,224},{160,192},{192,32},{224... | collective-permute-start | bytes 147464 | tf_op jit(solution)/shard_map/ppermute | solution.py:319
  36.1 1.5 %collective-permute-start.10 = (bf16[16,640]{1,0:T(8,128)(2,1)S(1)}, bf16[16,640]{1,0:T(8,128)(2,1)S(1)}, u32[]{:S(2)}, u32[]{:S(2)}) collective-permute-start(bf16[16,640]{1,0:T(8,128)(2,1)S(1)} %x_merge.1.slot_own), channel_id=1, source_target_pairs={{0,32},{32,0},{64,96},{96,64},{128,160},{160,128},{192,224},{224,1... | collective-permute-start | bytes 61448 | tf_op jit(solution)/shard_map/ppermute | solution.py:321
  38.3 1.3 %collective-permute-start.11 = (f32[16,640]{1,0:T(8,128)S(1)}, f32[16,640]{1,0:T(8,128)S(1)}, u32[]{:S(2)}, u32[]{:S(2)}) collective-permute-start(f32[16,640]{1,0:T(8,128)S(1)} %get-tuple-element.42), channel_id=1, source_target_pairs={{0,32},{32,0},{64,96},{96,64},{128,160},{160,128},{192,224},{224,1... | collective-permute-start | bytes 122888 | tf_op jit(solution)/shard_map/ppermute | solution.py:323
  39.6 3.9 %collective-permute-start.14 = (f32[16,640]{1,0:T(8,128)S(1)}, f32[16,640]{1,0:T(8,128)S(1)}, u32[]{:S(2)}, u32[]{:S(2)}) collective-permute-start(f32[16,640]{1,0:T(8,128)S(1)} %add.67), channel_id=1, source_target_pairs={{0,224},{32,192},{64,32},{96,0},{128,96},{160,64},{192,160},{224,1... | collective-permute-start | bytes 122888 | tf_op jit(solution)/shard_map/ppermute | solution.py:324
  40.2 4.4 %collective-permute-start.13 = (f32[16,640]{1,0:T(8,128)S(1)}, f32[16,640]{1,0:T(8,128)S(1)}, u32[]{:S(2)}, u32[]{:S(2)}) collective-permute-start(f32[16,640]{1,0:T(8,128)S(1)} %add.67), channel_id=1, source_target_pairs={{0,128},{32,160},{64,192},{96,224},{128,0},{160,32},{192,64},{224,... | collective-permute-start | bytes 122888 | tf_op jit(solution)/shard_map/ppermute | solution.py:324
  41.0 5.4 %collective-permute-start.12 = (f32[16,640]{1,0:T(8,128)S(1)}, f32[16,640]{1,0:T(8,128)S(1)}, u32[]{:S(2)}, u32[]{:S(2)}) collective-permute-start(f32[16,640]{1,0:T(8,128)S(1)} %add.67), channel_id=1, source_target_pairs={{0,96},{32,64},{64,160},{96,128},{128,224},{160,192},{192,32},{224... | collective-permute-start | bytes 122888 | tf_op jit(solution)/shard_map/ppermute | solution.py:324
  46.4 4.5 %collective-permute-start.15 = (bf16[16,640]{1,0:T(8,128)(2,1)S(1)}, bf16[16,640]{1,0:T(8,128)(2,1)S(1)}, u32[]{:S(2)}, u32[]{:S(2)}) collective-permute-start(bf16[16,640]{1,0:T(8,128)(2,1)S(1)} %get-tuple-element.44), channel_id=1, source_target_pairs={{0,2},{2,4},{4,6},{6,0},{8,10},{10,12},{12,14},{14,8},{16,18},{18,... | collective-permute-start | bytes 61448 | tf_op jit(solution)/shard_map/ppermute | solution.py:330
  47.0 3.9 %collective-permute-start.16 = (bf16[16,640]{1,0:T(8,128)(2,1)S(1)}, bf16[16,640]{1,0:T(8,128)(2,1)S(1)}, u32[]{:S(2)}, u32[]{:S(2)}) collective-permute-start(bf16[16,640]{1,0:T(8,128)(2,1)S(1)} %get-tuple-element.44), channel_id=1, source_target_pairs={{0,4},{2,6},{4,0},{6,2},{8,12},{10,14},{12,8},{14,10},{16,20},{18,... | collective-permute-start | bytes 61448 | tf_op jit(solution)/shard_map/ppermute | solution.py:330
  49.2 3.0 %collective-permute-start.17 = (bf16[16,640]{1,0:T(8,128)(2,1)S(1)}, bf16[16,640]{1,0:T(8,128)(2,1)S(1)}, u32[]{:S(2)}, u32[]{:S(2)}) collective-permute-start(bf16[16,640]{1,0:T(8,128)(2,1)S(1)} %get-tuple-element.44), channel_id=1, source_target_pairs={{0,6},{2,0},{4,2},{6,4},{8,14},{10,8},{12,10},{14,12},{16,22},{18,... | collective-permute-start | bytes 61448 | tf_op jit(solution)/shard_map/ppermute | solution.py:330
  52.2 10.2 %collective-permute-start.20 = (bf16[64,640]{1,0:T(8,128)(2,1)S(1)}, bf16[64,640]{1,0:T(8,128)(2,1)S(1)}, u32[]{:S(2)}, u32[]{:S(2)}) collective-permute-start(bf16[64,640]{1,0:T(8,128)(2,1)S(1)} %constant_dynamic-update-slice_fusion.4), channel_id=1, source_target_pairs={{0,56},{2,58},{4,60},{6,62},{8,32},{10,34},{12,36},{14,38},{16,40}... | collective-permute-start | bytes 245768 | tf_op jit(solution)/shard_map/ppermute | solution.py:330
  55.5 6.9 %collective-permute-start.19 = (bf16[64,640]{1,0:T(8,128)(2,1)S(1)}, bf16[64,640]{1,0:T(8,128)(2,1)S(1)}, u32[]{:S(2)}, u32[]{:S(2)}) collective-permute-start(bf16[64,640]{1,0:T(8,128)(2,1)S(1)} %constant_dynamic-update-slice_fusion.4), channel_id=1, source_target_pairs={{0,16},{2,18},{4,20},{6,22},{8,24},{10,26},{12,28},{14,30},{16,0},... | collective-permute-start | bytes 245768 | tf_op jit(solution)/shard_map/ppermute | solution.py:330
  56.8 5.6 %collective-permute-start.18 = (bf16[64,640]{1,0:T(8,128)(2,1)S(1)}, bf16[64,640]{1,0:T(8,128)(2,1)S(1)}, u32[]{:S(2)}, u32[]{:S(2)}) collective-permute-start(bf16[64,640]{1,0:T(8,128)(2,1)S(1)} %constant_dynamic-update-slice_fusion.4), channel_id=1, source_target_pairs={{0,40},{2,42},{4,44},{6,46},{8,48},{10,50},{12,52},{14,54},{16,56}... | collective-permute-start | bytes 245768 | tf_op jit(solution)/shard_map/ppermute | solution.py:330
  62.4 2.2 %collective-permute-start.21 = (bf16[256,640]{1,0:T(8,128)(2,1)S(1)}, bf16[256,640]{1,0:T(8,128)(2,1)S(1)}, u32[]{:S(2)}, u32[]{:S(2)}) collective-permute-start(bf16[256,640]{1,0:T(8,128)(2,1)S(1)} %constant_dynamic-update-slice_fusion.slot_out), channel_id=1, source_target_pairs={{0,32},{32,0},{64,96},{96,64},{128,160},{160,128},{192,224},{224,1... | collective-permute-start | bytes 983048 | tf_op jit(solution)/shard_map/ppermute | solution.py:337

commit v6 on v5

--- a/solution.py
+++ b/solution.py
@@ -16,7 +16,7 @@
 
 def _core():
     seq = lax.axis_index("seq")
-    return lax.rem(seq + lax.div(seq, 2) + _y(), 2)
+    return lax.rem(seq + lax.div(seq, 2) + _y() + _z(), 2)
 
 
 def _y():
@@ -44,7 +44,11 @@
 
 
 def _z_perm(k):
-    return [(e, (e // 4) * 4 + (e % 4 + k) % 4) for e in range(16)]
+    return [
+        (s * 16 + e, (s ^ (k & 1)) * 16 + (e // 4) * 4 + (e % 4 + k) % 4)
+        for s in range(8)
+        for e in range(16)
+    ]
 
 
 def _call(kernel, name, out_shape, in_specs, scratch=(), out_specs=None, vmem=6, flops=0, bytes_accessed=0, **kw):
@@ -314,7 +318,7 @@
     got = [lax.ppermute(v, ("seq", "exp"), _y_perm(k + 1)) for k, v in enumerate(send)]
     combine, w_in, w_out = combine_weights(own, logits, w_in[0], w_out[0])
     own, *send = y_merge(combine, own, stat, *got)
-    got = [lax.ppermute(v, "exp", _z_perm(k + 1)) for k, v in enumerate(send)]
+    got = [lax.ppermute(v, ("seq", "exp"), _z_perm(k + 1)) for k, v in enumerate(send)]
     own = z_merge(own, *got)
     got = [lax.ppermute(own, "seq", _x_perm(k)) for k in range(1, 4)]
     slot_half = x_merge(own, *got)
@@ -324,16 +328,16 @@
     whole = part + sum(lax.ppermute(part, "seq", _x_perm(k)) for k in range(1, 4))
     out = whole.astype(BF16)
 
-    def gather(block, index, axes, perm):
+    def gather(block, index, perm):
         n = block.shape[0]
         res = jnp.zeros((4 * n, block.shape[1]), block.dtype)
-        blocks = [block] + [lax.ppermute(block, axes, perm(k)) for k in range(1, 4)]
+        blocks = [block] + [lax.ppermute(block, ("seq", "exp"), perm(k)) for k in range(1, 4)]
         for k, g in enumerate(blocks):
             res = lax.dynamic_update_slice_in_dim(res, g, ((index - k) % 4) * n, 0)
         return res
 
-    out = gather(out, z, "exp", _z_perm)
-    out = gather(out, y, ("seq", "exp"), _y_perm)
+    out = gather(out, z, _z_perm)
+    out = gather(out, y, _y_perm)
     other = lax.ppermute(out, "seq", _core_perm())
     mixed = mix(combine, out)
     return mix(combine, other, mixed)

time: 66.7 us -> 66.7 us (level)
    ppermute x9, waiting for transfers between devices: 11 us -> 11.9 us  [the longest x6 8.29 us: gather(): lax.ppermute(block, ('seq', 'exp'), perm(k))]
    ppermute x3, starting transfers between devices: 5.04 us -> 4.25 us  [body(): got = [lax.ppermute(own, 'seq', _x_perm(k)) for k in range(1, 4)]]
where the time goes in v6:
time: 66.7 us
  starting transfers between devices  27.8 us (42%)
  waiting for transfers between devices  25.5 us (38%)
  Pallas kernels  12.8 us (19%)
    ppermute x6, waiting for transfers between devices, gather(): lax.ppermute(block, ('seq', 'exp'), perm(k))  8.29 us
    ppermute x6, starting transfers between devices, gather(): lax.ppermute(block, ('seq', 'exp'), perm(k))  7.8 us
    ppermute x3, starting transfers between devices, body(): lax.ppermute(v, ('seq', 'exp'), _z_perm(k + 1))  4.86 us
    pallas_call x1, Pallas kernels, first(): _call(functools.partial(first_kernel, CHUNKS), 'logits_and_sums', [pltpu....  4.76 us
    ppermute x3, waiting for transfers between devices, body(): got = [lax.ppermute(own, 'seq', _x_perm(k)) for k in range(1, 4)]  4.56 us
    ppermute x3, starting transfers between devices, body(): got = [lax.ppermute(own, 'seq', _x_perm(k)) for k in range(1, 4)]  4.25 us
    ppermute x3, waiting for transfers between devices, body(): lax.ppermute(part, 'seq', _x_perm(k))  4.09 us
    ppermute x3, starting transfers between devices, body(): lax.ppermute(v, ('seq', 'exp'), _y_perm(k + 1))  3.9 us
  transfers between devices with their start and end apart: 22, of which 17 were waited for; matrix products, arithmetic and copies ran while one was open for 0% of the time, Pallas kernels for 7%

profile of v6, /device:TPU:1, one launch (start us, length us, event | category | flops | bytes accessed | tf_op | source)
XLA Modules:
  0.0 66.7 jit_solution(17571586156425675320)
XLA Ops:
  0.0 4.8 %logits_and_sums.1 = (bf16[2048,1280]{1,0:T(8,128)(2,1)S(1)}, f32[256,2048]{1,0:T(8,128)S(1)}, bf16[256,2048]{1,0:T(8,128)(2,1)S(1)}, bf16[256,768]{1,0:T(8,128)(2,1)S(1)}, f32[256,768]{1,0:T(8,128)S(1)}) custom-call(bf16[2048,1280]{1,0:T(8,128)(2,1)} %tok_hbm.1, bf16[1280,256]{1,0:T(8,128)(2,1)} %keys_hbm.1), custom_call_target="tpu_custom_call" | custom-call | flops 2013265920 | bytes 5242880 | tf_op jit(solution)/shard_map/logits_and_sums/pallas_call | solution.py:353
  4.8 3.4 %collective-permute-start = (bf16[256,768]{1,0:T(8,128)(2,1)S(1)}, bf16[256,768]{1,0:T(8,128)(2,1)S(1)}, u32[]{:S(2)}, u32[]{:S(2)}) collective-permute-start(bf16[256,768]{1,0:T(8,128)(2,1)S(1)} %get-tuple-element.27), channel_id=1, source_target_pairs={{0,32},{32,0},{64,96},{96,64},{128,160},{160,128},{192,224},{224,1... | collective-permute-start | bytes 1179656 | tf_op jit(solution)/shard_map/ppermute | solution.py:314
  8.1 1.0 %own_sums.1.own = f32[256,640]{1,0:T(8,128)S(1)} custom-call(bf16[2048,1280]{1,0:T(8,128)(2,1)S(1)} %get-tuple-element.24.tok, bf16[256,2048]{1,0:T(8,128)(2,1)S(1)} %get-tuple-element.25.dispatch, f32[256,768]{1,0:T(8,128)S(1)} %get-tuple-element.26.stat), custom_call_target="tpu_custom_call" | custom-call | flops 671088640 | tf_op jit(solution)/shard_map/own_sums/pallas_call | solution.py:376
  9.2 0.3 collective-permute-done.got
  9.5 0.3 core_merge.1
  9.9 2.4 %collective-permute-start.2 = (bf16[64,768]{1,0:T(8,128)(2,1)S(1)}, bf16[64,768]{1,0:T(8,128)(2,1)S(1)}, u32[]{:S(2)}, u32[]{:S(2)}) collective-permute-start(bf16[64,768]{1,0:T(8,128)(2,1)S(1)} %get-tuple-element.33), channel_id=1, source_target_pairs={{0,16},{2,18},{4,20},{6,22},{8,24},{10,26},{12,28},{14,30},{16,0},... | collective-permute-start | bytes 294920 | tf_op jit(solution)/shard_map/ppermute | solution.py:318
  12.3 1.4 %collective-permute-start.3 = (bf16[64,768]{1,0:T(8,128)(2,1)S(1)}, bf16[64,768]{1,0:T(8,128)(2,1)S(1)}, u32[]{:S(2)}, u32[]{:S(2)}) collective-permute-start(bf16[64,768]{1,0:T(8,128)(2,1)S(1)} %get-tuple-element.34), channel_id=1, source_target_pairs={{0,56},{2,58},{4,60},{6,62},{8,32},{10,34},{12,36},{14,38},{16,40}... | collective-permute-start | bytes 294920 | tf_op jit(solution)/shard_map/ppermute | solution.py:318
  13.7 1.9 %combine.1 = (bf16[2048,256]{1,0:T(8,128)(2,1)S(1)}, bf16[1280,640]{1,0:T(8,128)(2,1)S(1)}, bf16[640,1280]{1,0:T(8,128)(2,1)S(1)}) custom-call(f32[64,640]{1,0:T(8,128)S(1)} %get-tuple-element.28.after.own, f32[256,2048]{1,0:T(8,128)S(1)} %get-tuple-element.29.logits, bf16[1280,640]{1,0:T(8,128)(2,1)} %bitcast.2, bf16[640,1280]{1,0:T(8,128)(2,1)} %bitcast.3), custom_call_target="tpu_custom_call" | custom-call | flops 5242880 | bytes 3276800 | tf_op jit(solution)/shard_map/combine/pallas_call | solution.py:388
  15.7 2.3 %collective-permute-done.1.got1 = bf16[64,768]{1,0:T(8,128)(2,1)S(1)} collective-permute-done((bf16[64,768]{1,0:T(8,128)(2,1)S(1)}, bf16[64,768]{1,0:T(8,128)(2,1)S(1)}, u32[]{:S(2)}, u32[]{:S(2)}) %collective-permute-start.1) | collective-permute-done | bytes 98336 | tf_op jit(solution)/shard_map/ppermute | solution.py:318
  18.0 0.6 collective-permute-done.3.got3
  18.6 0.2 y_merge.1
  18.8 1.2 %collective-permute-start.4 = (f32[16,768]{1,0:T(8,128)S(1)}, f32[16,768]{1,0:T(8,128)S(1)}, u32[]{:S(2)}, u32[]{:S(2)}) collective-permute-start(f32[16,768]{1,0:T(8,128)S(1)} %get-tuple-element.36), channel_id=1, source_target_pairs={{0,34},{2,36},{4,38},{6,32},{8,42},{10,44},{12,46},{14,40},{16,50}... | collective-permute-start | bytes 147464 | tf_op jit(solution)/shard_map/ppermute | solution.py:321
  20.0 3.0 %collective-permute-start.5 = (f32[16,768]{1,0:T(8,128)S(1)}, f32[16,768]{1,0:T(8,128)S(1)}, u32[]{:S(2)}, u32[]{:S(2)}) collective-permute-start(f32[16,768]{1,0:T(8,128)S(1)} %get-tuple-element.37), channel_id=1, source_target_pairs={{0,4},{2,6},{4,0},{6,2},{8,12},{10,14},{12,8},{14,10},{16,20},{18,... | collective-permute-start | bytes 147464 | tf_op jit(solution)/shard_map/ppermute | solution.py:321
  23.0 0.6 collective-permute-start.6
  23.7 0.9 %collective-permute-done.4.got1 = f32[16,768]{1,0:T(8,128)S(1)} collective-permute-done((f32[16,768]{1,0:T(8,128)S(1)}, f32[16,768]{1,0:T(8,128)S(1)}, u32[]{:S(2)}, u32[]{:S(2)}) %collective-permute-start.4) | collective-permute-done | bytes 49184 | tf_op jit(solution)/shard_map/ppermute | solution.py:321
  24.6 2.2 %collective-permute-done.5.got2 = f32[16,768]{1,0:T(8,128)S(1)} collective-permute-done((f32[16,768]{1,0:T(8,128)S(1)}, f32[16,768]{1,0:T(8,128)S(1)}, u32[]{:S(2)}, u32[]{:S(2)}) %collective-permute-start.5) | collective-permute-done | bytes 49184 | tf_op jit(solution)/shard_map/ppermute | solution.py:321
  26.8 0.5 collective-permute-done.6.got3
  27.3 0.1 z_merge.1.own
  27.4 2.7 %collective-permute-start.9 = (f32[16,768]{1,0:T(8,128)S(1)}, f32[16,768]{1,0:T(8,128)S(1)}, u32[]{:S(2)}, u32[]{:S(2)}) collective-permute-start(f32[16,768]{1,0:T(8,128)S(1)} %z_merge.1.own), channel_id=1, source_target_pairs={{0,224},{32,192},{64,32},{96,0},{128,96},{160,64},{192,160},{224,1... | collective-permute-start | bytes 147464 | tf_op jit(solution)/shard_map/ppermute | solution.py:323
  30.1 0.5 collective-permute-start.8
  30.6 1.1 %collective-permute-start.7 = (f32[16,768]{1,0:T(8,128)S(1)}, f32[16,768]{1,0:T(8,128)S(1)}, u32[]{:S(2)}, u32[]{:S(2)}) collective-permute-start(f32[16,768]{1,0:T(8,128)S(1)} %z_merge.1.own), channel_id=1, source_target_pairs={{0,96},{32,64},{64,160},{96,128},{128,224},{160,192},{192,32},{224... | collective-permute-start | bytes 147464 | tf_op jit(solution)/shard_map/ppermute | solution.py:323
  31.7 2.9 %collective-permute-done.8.got2 = f32[16,768]{1,0:T(8,128)S(1)} collective-permute-done((f32[16,768]{1,0:T(8,128)S(1)}, f32[16,768]{1,0:T(8,128)S(1)}, u32[]{:S(2)}, u32[]{:S(2)}) %collective-permute-start.8) | collective-permute-done | bytes 49184 | tf_op jit(solution)/shard_map/ppermute | solution.py:323
  34.5 1.7 %collective-permute-done.7.got1 = f32[16,768]{1,0:T(8,128)S(1)} collective-permute-done((f32[16,768]{1,0:T(8,128)S(1)}, f32[16,768]{1,0:T(8,128)S(1)}, u32[]{:S(2)}, u32[]{:S(2)}) %collective-permute-start.7) | collective-permute-done | bytes 49184 | tf_op jit(solution)/shard_map/ppermute | solution.py:323
  36.2 0.1 x_merge.1.slot_own
  36.3 0.7 collective-permute-start.10
  37.0 0.8 %collective-permute-done.10.slot_other = bf16[16,640]{1,0:T(8,128)(2,1)S(1)} collective-permute-done((bf16[16,640]{1,0:T(8,128)(2,1)S(1)}, bf16[16,640]{1,0:T(8,128)(2,1)S(1)}, u32[]{:S(2)}, u32[]{:S(2)}) %collective-permute-start.10) | collective-permute-done | bytes 20512 | tf_op jit(solution)/shard_map/ppermute | solution.py:325
  37.8 0.6 expert.1
  38.5 0.4 collective-permute-start.11
  38.9 0.9 %collective-permute-done.11 = f32[16,640]{1,0:T(8,128)S(1)} collective-permute-done((f32[16,640]{1,0:T(8,128)S(1)}, f32[16,640]{1,0:T(8,128)S(1)}, u32[]{:S(2)}, u32[]{:S(2)}) %collective-permute-start.11) | collective-permute-done | bytes 40992 | tf_op jit(solution)/shard_map/ppermute | solution.py:327
  39.8 0.2 collective-permute-start.14
  40.0 0.9 %collective-permute-start.13 = (f32[16,640]{1,0:T(8,128)S(1)}, f32[16,640]{1,0:T(8,128)S(1)}, u32[]{:S(2)}, u32[]{:S(2)}) collective-permute-start(f32[16,640]{1,0:T(8,128)S(1)} %add.67), channel_id=1, source_target_pairs={{0,128},{32,160},{64,192},{96,224},{128,0},{160,32},{192,64},{224,... | collective-permute-start | bytes 122888 | tf_op jit(solution)/shard_map/ppermute | solution.py:328
  40.9 1.0 %collective-permute-start.12 = (f32[16,640]{1,0:T(8,128)S(1)}, f32[16,640]{1,0:T(8,128)S(1)}, u32[]{:S(2)}, u32[]{:S(2)}) collective-permute-start(f32[16,640]{1,0:T(8,128)S(1)} %add.67), channel_id=1, source_target_pairs={{0,96},{32,64},{64,160},{96,128},{128,224},{160,192},{192,32},{224... | collective-permute-start | bytes 122888 | tf_op jit(solution)/shard_map/ppermute | solution.py:328
  41.9 1.7 %collective-permute-done.14 = f32[16,640]{1,0:T(8,128)S(1)} collective-permute-done((f32[16,640]{1,0:T(8,128)S(1)}, f32[16,640]{1,0:T(8,128)S(1)}, u32[]{:S(2)}, u32[]{:S(2)}) %collective-permute-start.14) | collective-permute-done | bytes 40992 | tf_op jit(solution)/shard_map/ppermute | solution.py:328
  43.6 0.7 %collective-permute-done.13 = f32[16,640]{1,0:T(8,128)S(1)} collective-permute-done((f32[16,640]{1,0:T(8,128)S(1)}, f32[16,640]{1,0:T(8,128)S(1)}, u32[]{:S(2)}, u32[]{:S(2)}) %collective-permute-start.13) | collective-permute-done | bytes 40992 | tf_op jit(solution)/shard_map/ppermute | solution.py:328
  44.3 1.7 %collective-permute-done.12 = f32[16,640]{1,0:T(8,128)S(1)} collective-permute-done((f32[16,640]{1,0:T(8,128)S(1)}, f32[16,640]{1,0:T(8,128)S(1)}, u32[]{:S(2)}, u32[]{:S(2)}) %collective-permute-start.12) | collective-permute-done | bytes 40992 | tf_op jit(solution)/shard_map/ppermute | solution.py:328
  46.0 1.3 %collective-permute-start.15 = (bf16[16,640]{1,0:T(8,128)(2,1)S(1)}, bf16[16,640]{1,0:T(8,128)(2,1)S(1)}, u32[]{:S(2)}, u32[]{:S(2)}) collective-permute-start(bf16[16,640]{1,0:T(8,128)(2,1)S(1)} %get-tuple-element.44), channel_id=1, source_target_pairs={{0,34},{2,36},{4,38},{6,32},{8,42},{10,44},{12,46},{14,40},{16,50}... | collective-permute-start | bytes 61448 | tf_op jit(solution)/shard_map/ppermute | solution.py:334
  47.4 1.4 %collective-permute-start.16 = (bf16[16,640]{1,0:T(8,128)(2,1)S(1)}, bf16[16,640]{1,0:T(8,128)(2,1)S(1)}, u32[]{:S(2)}, u32[]{:S(2)}) collective-permute-start(bf16[16,640]{1,0:T(8,128)(2,1)S(1)} %get-tuple-element.44), channel_id=1, source_target_pairs={{0,4},{2,6},{4,0},{6,2},{8,12},{10,14},{12,8},{14,10},{16,20},{18,... | collective-permute-start | bytes 61448 | tf_op jit(solution)/shard_map/ppermute | solution.py:334
  48.8 1.4 %collective-permute-start.17 = (bf16[16,640]{1,0:T(8,128)(2,1)S(1)}, bf16[16,640]{1,0:T(8,128)(2,1)S(1)}, u32[]{:S(2)}, u32[]{:S(2)}) collective-permute-start(bf16[16,640]{1,0:T(8,128)(2,1)S(1)} %get-tuple-element.44), channel_id=1, source_target_pairs={{0,38},{2,32},{4,34},{6,36},{8,46},{10,40},{12,42},{14,44},{16,54}... | collective-permute-start | bytes 61448 | tf_op jit(solution)/shard_map/ppermute | solution.py:334
  50.2 1.1 %collective-permute-done.15 = bf16[16,640]{1,0:T(8,128)(2,1)S(1)} collective-permute-done((bf16[16,640]{1,0:T(8,128)(2,1)S(1)}, bf16[16,640]{1,0:T(8,128)(2,1)S(1)}, u32[]{:S(2)}, u32[]{:S(2)}) %collective-permute-start.15) | collective-permute-done | bytes 20512 | tf_op jit(solution)/shard_map/ppermute | solution.py:334
  51.3 0.7 %collective-permute-done.16 = bf16[16,640]{1,0:T(8,128)(2,1)S(1)} collective-permute-done((bf16[16,640]{1,0:T(8,128)(2,1)S(1)}, bf16[16,640]{1,0:T(8,128)(2,1)S(1)}, u32[]{:S(2)}, u32[]{:S(2)}) %collective-permute-start.16) | collective-permute-done | bytes 20512 | tf_op jit(solution)/shard_map/ppermute | solution.py:334
  52.1 0.1 collective-permute-done.17
  52.2 2.3 %collective-permute-start.20 = (bf16[64,640]{1,0:T(8,128)(2,1)S(1)}, bf16[64,640]{1,0:T(8,128)(2,1)S(1)}, u32[]{:S(2)}, u32[]{:S(2)}) collective-permute-start(bf16[64,640]{1,0:T(8,128)(2,1)S(1)} %constant_dynamic-update-slice_fusion.4), channel_id=1, source_target_pairs={{0,56},{2,58},{4,60},{6,62},{8,32},{10,34},{12,36},{14,38},{16,40}... | collective-permute-start | bytes 245768 | tf_op jit(solution)/shard_map/ppermute | solution.py:334
  54.5 1.1 %collective-permute-start.19 = (bf16[64,640]{1,0:T(8,128)(2,1)S(1)}, bf16[64,640]{1,0:T(8,128)(2,1)S(1)}, u32[]{:S(2)}, u32[]{:S(2)}) collective-permute-start(bf16[64,640]{1,0:T(8,128)(2,1)S(1)} %constant_dynamic-update-slice_fusion.4), channel_id=1, source_target_pairs={{0,16},{2,18},{4,20},{6,22},{8,24},{10,26},{12,28},{14,30},{16,0},... | collective-permute-start | bytes 245768 | tf_op jit(solution)/shard_map/ppermute | solution.py:334
  55.6 0.3 collective-permute-start.18
  55.9 6.3 %collective-permute-done.18 = bf16[64,640]{1,0:T(8,128)(2,1)S(1)} collective-permute-done((bf16[64,640]{1,0:T(8,128)(2,1)S(1)}, bf16[64,640]{1,0:T(8,128)(2,1)S(1)}, u32[]{:S(2)}, u32[]{:S(2)}) %collective-permute-start.18) | collective-permute-done | bytes 81952 | tf_op jit(solution)/shard_map/ppermute | solution.py:334
  62.3 0.5 collective-permute-start.21
  62.8 1.8 %mix.2.refs_0_ = bf16[2048,1280]{1,0:T(8,128)(2,1)} custom-call(bf16[2048,256]{1,0:T(8,128)(2,1)S(1)} %get-tuple-element.30.after.combine, bf16[256,640]{1,0:T(8,128)(2,1)S(1)} %constant_dynamic-update-slice_fusion.slot_out), custom_call_target="tpu_custom_call" | custom-call | flops 671088640 | bytes 2621440 | tf_op jit(solution)/shard_map/mix/pallas_call | solution.py:448
  64.6 1.9 %mix.3 = bf16[2048,1280]{1,0:T(8,128)(2,1)} custom-call(bf16[2048,256]{1,0:T(8,128)(2,1)S(1)} %get-tuple-element.30.after.combine, bf16[256,640]{1,0:T(8,128)(2,1)S(1)} %collective-permute-done.21.slot_out, bf16[2048,1280]{1,0:T(8,128)(2,1)} %mix.2.refs_0_), custom_call_target="tpu_custom_call", output_to_operand_aliasing={{}: (2, {})} | custom-call | flops 671088640 | bytes 2621440 | tf_op jit(solution)/shard_map/mix/pallas_call | solution.py:448
  (17 shorter events, 0.3 us)
Async XLA Ops:
  4.8 4.7 %collective-permute-start = (bf16[256,768]{1,0:T(8,128)(2,1)S(1)}, bf16[256,768]{1,0:T(8,128)(2,1)S(1)}, u32[]{:S(2)}, u32[]{:S(2)}) collective-permute-start(bf16[256,768]{1,0:T(8,128)(2,1)S(1)} %get-tuple-element.27), channel_id=1, source_target_pairs={{0,32},{32,0},{64,96},{96,64},{128,160},{160,128},{192,224},{224,1... | collective-permute-start | bytes 1179656 | tf_op jit(solution)/shard_map/ppermute | solution.py:314
  9.8 8.2 %collective-permute-start.1 = (bf16[64,768]{1,0:T(8,128)(2,1)S(1)}, bf16[64,768]{1,0:T(8,128)(2,1)S(1)}, u32[]{:S(2)}, u32[]{:S(2)}) collective-permute-start(bf16[64,768]{1,0:T(8,128)(2,1)S(1)} %get-tuple-element.32), channel_id=1, source_target_pairs={{0,40},{2,42},{4,44},{6,46},{8,48},{10,50},{12,52},{14,54},{16,56}... | collective-permute-start | bytes 294920 | tf_op jit(solution)/shard_map/ppermute | solution.py:318
  9.9 8.1 %collective-permute-start.2 = (bf16[64,768]{1,0:T(8,128)(2,1)S(1)}, bf16[64,768]{1,0:T(8,128)(2,1)S(1)}, u32[]{:S(2)}, u32[]{:S(2)}) collective-permute-start(bf16[64,768]{1,0:T(8,128)(2,1)S(1)} %get-tuple-element.33), channel_id=1, source_target_pairs={{0,16},{2,18},{4,20},{6,22},{8,24},{10,26},{12,28},{14,30},{16,0},... | collective-permute-start | bytes 294920 | tf_op jit(solution)/shard_map/ppermute | solution.py:318
  12.3 6.3 %collective-permute-start.3 = (bf16[64,768]{1,0:T(8,128)(2,1)S(1)}, bf16[64,768]{1,0:T(8,128)(2,1)S(1)}, u32[]{:S(2)}, u32[]{:S(2)}) collective-permute-start(bf16[64,768]{1,0:T(8,128)(2,1)S(1)} %get-tuple-element.34), channel_id=1, source_target_pairs={{0,56},{2,58},{4,60},{6,62},{8,32},{10,34},{12,36},{14,38},{16,40}... | collective-permute-start | bytes 294920 | tf_op jit(solution)/shard_map/ppermute | solution.py:318
  18.8 5.8 %collective-permute-start.4 = (f32[16,768]{1,0:T(8,128)S(1)}, f32[16,768]{1,0:T(8,128)S(1)}, u32[]{:S(2)}, u32[]{:S(2)}) collective-permute-start(f32[16,768]{1,0:T(8,128)S(1)} %get-tuple-element.36), channel_id=1, source_target_pairs={{0,34},{2,36},{4,38},{6,32},{8,42},{10,44},{12,46},{14,40},{16,50}... | collective-permute-start | bytes 147464 | tf_op jit(solution)/shard_map/ppermute | solution.py:321
  20.0 6.8 %collective-permute-start.5 = (f32[16,768]{1,0:T(8,128)S(1)}, f32[16,768]{1,0:T(8,128)S(1)}, u32[]{:S(2)}, u32[]{:S(2)}) collective-permute-start(f32[16,768]{1,0:T(8,128)S(1)} %get-tuple-element.37), channel_id=1, source_target_pairs={{0,4},{2,6},{4,0},{6,2},{8,12},{10,14},{12,8},{14,10},{16,20},{18,... | collective-permute-start | bytes 147464 | tf_op jit(solution)/shard_map/ppermute | solution.py:321
  23.0 4.3 %collective-permute-start.6 = (f32[16,768]{1,0:T(8,128)S(1)}, f32[16,768]{1,0:T(8,128)S(1)}, u32[]{:S(2)}, u32[]{:S(2)}) collective-permute-start(f32[16,768]{1,0:T(8,128)S(1)} %get-tuple-element.38), channel_id=1, source_target_pairs={{0,38},{2,32},{4,34},{6,36},{8,46},{10,40},{12,42},{14,44},{16,54}... | collective-permute-start | bytes 147464 | tf_op jit(solution)/shard_map/ppermute | solution.py:321
  27.4 4.3 %collective-permute-start.9 = (f32[16,768]{1,0:T(8,128)S(1)}, f32[16,768]{1,0:T(8,128)S(1)}, u32[]{:S(2)}, u32[]{:S(2)}) collective-permute-start(f32[16,768]{1,0:T(8,128)S(1)} %z_merge.1.own), channel_id=1, source_target_pairs={{0,224},{32,192},{64,32},{96,0},{128,96},{160,64},{192,160},{224,1... | collective-permute-start | bytes 147464 | tf_op jit(solution)/shard_map/ppermute | solution.py:323
  30.1 4.4 %collective-permute-start.8 = (f32[16,768]{1,0:T(8,128)S(1)}, f32[16,768]{1,0:T(8,128)S(1)}, u32[]{:S(2)}, u32[]{:S(2)}) collective-permute-start(f32[16,768]{1,0:T(8,128)S(1)} %z_merge.1.own), channel_id=1, source_target_pairs={{0,128},{32,160},{64,192},{96,224},{128,0},{160,32},{192,64},{224,... | collective-permute-start | bytes 147464 | tf_op jit(solution)/shard_map/ppermute | solution.py:323
  30.6 5.6 %collective-permute-start.7 = (f32[16,768]{1,0:T(8,128)S(1)}, f32[16,768]{1,0:T(8,128)S(1)}, u32[]{:S(2)}, u32[]{:S(2)}) collective-permute-start(f32[16,768]{1,0:T(8,128)S(1)} %z_merge.1.own), channel_id=1, source_target_pairs={{0,96},{32,64},{64,160},{96,128},{128,224},{160,192},{192,32},{224... | collective-permute-start | bytes 147464 | tf_op jit(solution)/shard_map/ppermute | solution.py:323
  36.3 1.5 %collective-permute-start.10 = (bf16[16,640]{1,0:T(8,128)(2,1)S(1)}, bf16[16,640]{1,0:T(8,128)(2,1)S(1)}, u32[]{:S(2)}, u32[]{:S(2)}) collective-permute-start(bf16[16,640]{1,0:T(8,128)(2,1)S(1)} %x_merge.1.slot_own), channel_id=1, source_target_pairs={{0,32},{32,0},{64,96},{96,64},{128,160},{160,128},{192,224},{224,1... | collective-permute-start | bytes 61448 | tf_op jit(solution)/shard_map/ppermute | solution.py:325
  38.5 1.3 %collective-permute-start.11 = (f32[16,640]{1,0:T(8,128)S(1)}, f32[16,640]{1,0:T(8,128)S(1)}, u32[]{:S(2)}, u32[]{:S(2)}) collective-permute-start(f32[16,640]{1,0:T(8,128)S(1)} %get-tuple-element.42), channel_id=1, source_target_pairs={{0,32},{32,0},{64,96},{96,64},{128,160},{160,128},{192,224},{224,1... | collective-permute-start | bytes 122888 | tf_op jit(solution)/shard_map/ppermute | solution.py:327
  39.8 3.9 %collective-permute-start.14 = (f32[16,640]{1,0:T(8,128)S(1)}, f32[16,640]{1,0:T(8,128)S(1)}, u32[]{:S(2)}, u32[]{:S(2)}) collective-permute-start(f32[16,640]{1,0:T(8,128)S(1)} %add.67), channel_id=1, source_target_pairs={{0,224},{32,192},{64,32},{96,0},{128,96},{160,64},{192,160},{224,1... | collective-permute-start | bytes 122888 | tf_op jit(solution)/shard_map/ppermute | solution.py:328
  40.0 4.4 %collective-permute-start.13 = (f32[16,640]{1,0:T(8,128)S(1)}, f32[16,640]{1,0:T(8,128)S(1)}, u32[]{:S(2)}, u32[]{:S(2)}) collective-permute-start(f32[16,640]{1,0:T(8,128)S(1)} %add.67), channel_id=1, source_target_pairs={{0,128},{32,160},{64,192},{96,224},{128,0},{160,32},{192,64},{224,... | collective-permute-start | bytes 122888 | tf_op jit(solution)/shard_map/ppermute | solution.py:328
  40.9 5.1 %collective-permute-start.12 = (f32[16,640]{1,0:T(8,128)S(1)}, f32[16,640]{1,0:T(8,128)S(1)}, u32[]{:S(2)}, u32[]{:S(2)}) collective-permute-start(f32[16,640]{1,0:T(8,128)S(1)} %add.67), channel_id=1, source_target_pairs={{0,96},{32,64},{64,160},{96,128},{128,224},{160,192},{192,32},{224... | collective-permute-start | bytes 122888 | tf_op jit(solution)/shard_map/ppermute | solution.py:328
  46.0 5.3 %collective-permute-start.15 = (bf16[16,640]{1,0:T(8,128)(2,1)S(1)}, bf16[16,640]{1,0:T(8,128)(2,1)S(1)}, u32[]{:S(2)}, u32[]{:S(2)}) collective-permute-start(bf16[16,640]{1,0:T(8,128)(2,1)S(1)} %get-tuple-element.44), channel_id=1, source_target_pairs={{0,34},{2,36},{4,38},{6,32},{8,42},{10,44},{12,46},{14,40},{16,50}... | collective-permute-start | bytes 61448 | tf_op jit(solution)/shard_map/ppermute | solution.py:334
  47.4 4.7 %collective-permute-start.16 = (bf16[16,640]{1,0:T(8,128)(2,1)S(1)}, bf16[16,640]{1,0:T(8,128)(2,1)S(1)}, u32[]{:S(2)}, u32[]{:S(2)}) collective-permute-start(bf16[16,640]{1,0:T(8,128)(2,1)S(1)} %get-tuple-element.44), channel_id=1, source_target_pairs={{0,4},{2,6},{4,0},{6,2},{8,12},{10,14},{12,8},{14,10},{16,20},{18,... | collective-permute-start | bytes 61448 | tf_op jit(solution)/shard_map/ppermute | solution.py:334
  48.8 3.4 %collective-permute-start.17 = (bf16[16,640]{1,0:T(8,128)(2,1)S(1)}, bf16[16,640]{1,0:T(8,128)(2,1)S(1)}, u32[]{:S(2)}, u32[]{:S(2)}) collective-permute-start(bf16[16,640]{1,0:T(8,128)(2,1)S(1)} %get-tuple-element.44), channel_id=1, source_target_pairs={{0,38},{2,32},{4,34},{6,36},{8,46},{10,40},{12,42},{14,44},{16,54}... | collective-permute-start | bytes 61448 | tf_op jit(solution)/shard_map/ppermute | solution.py:334
  52.2 10.1 %collective-permute-start.20 = (bf16[64,640]{1,0:T(8,128)(2,1)S(1)}, bf16[64,640]{1,0:T(8,128)(2,1)S(1)}, u32[]{:S(2)}, u32[]{:S(2)}) collective-permute-start(bf16[64,640]{1,0:T(8,128)(2,1)S(1)} %constant_dynamic-update-slice_fusion.4), channel_id=1, source_target_pairs={{0,56},{2,58},{4,60},{6,62},{8,32},{10,34},{12,36},{14,38},{16,40}... | collective-permute-start | bytes 245768 | tf_op jit(solution)/shard_map/ppermute | solution.py:334
  54.5 7.7 %collective-permute-start.19 = (bf16[64,640]{1,0:T(8,128)(2,1)S(1)}, bf16[64,640]{1,0:T(8,128)(2,1)S(1)}, u32[]{:S(2)}, u32[]{:S(2)}) collective-permute-start(bf16[64,640]{1,0:T(8,128)(2,1)S(1)} %constant_dynamic-update-slice_fusion.4), channel_id=1, source_target_pairs={{0,16},{2,18},{4,20},{6,22},{8,24},{10,26},{12,28},{14,30},{16,0},... | collective-permute-start | bytes 245768 | tf_op jit(solution)/shard_map/ppermute | solution.py:334
  55.6 6.6 %collective-permute-start.18 = (bf16[64,640]{1,0:T(8,128)(2,1)S(1)}, bf16[64,640]{1,0:T(8,128)(2,1)S(1)}, u32[]{:S(2)}, u32[]{:S(2)}) collective-permute-start(bf16[64,640]{1,0:T(8,128)(2,1)S(1)} %constant_dynamic-update-slice_fusion.4), channel_id=1, source_target_pairs={{0,40},{2,42},{4,44},{6,46},{8,48},{10,50},{12,52},{14,54},{16,56}... | collective-permute-start | bytes 245768 | tf_op jit(solution)/shard_map/ppermute | solution.py:334
  62.3 2.3 %collective-permute-start.21 = (bf16[256,640]{1,0:T(8,128)(2,1)S(1)}, bf16[256,640]{1,0:T(8,128)(2,1)S(1)}, u32[]{:S(2)}, u32[]{:S(2)}) collective-permute-start(bf16[256,640]{1,0:T(8,128)(2,1)S(1)} %constant_dynamic-update-slice_fusion.slot_out), channel_id=1, source_target_pairs={{0,32},{32,0},{64,96},{96,64},{128,160},{160,128},{192,224},{224,1... | collective-permute-start | bytes 983048 | tf_op jit(solution)/shard_map/ppermute | solution.py:341
